TPU v7x, 256 devices: a whole 4x4x8 slice. The times are simulated.
256 devices in a mesh: ctx: 32 (over z, x_hi, core), tp: 8 (over x_lo, y).
Axes of the slice: x: 4 (x_hi: 2, x_lo: 2; x = x_hi * 2 + x_lo), y: 4, z: 8, core: 2. Of those that a mesh axis runs over, the one named last changes fastest.
Arguments:
- tokens: bfloat16 [32768, 4096], P('ctx', 'tp'), may hold values from -6 to 6
- proj_weight: bfloat16 [4096, 3, 2048], P('ctx', None, 'tp'), may hold values from -0.09375 to 0.09375
- short_taps: float32 [3, 3, 2048], P(None, None, 'tp'), may hold values from -3 to 3
- long_filter: float32 [2048, 32768], P(('tp', 'ctx')), as said below
- skip_gain: float32 [2048], P(('tp', 'ctx')), may hold values from 0.5 to 1.5
Outputs:
- block_output: bfloat16 [32768, 2048], P('ctx', 'tp')
Inputs may be any that keep to these rules, and one draw needn't show every extreme that they name: `long_filter`: each channel's taps are scaled so that their squares sum to at most about one.
All inputs are finite; a program needn't handle non-finite values.
Results may differ from a plain program's by a relative error of at most 0.012.
Values may be sent and summed in bfloat16 or wider, within the bound.
No kernel may reach another device: no remote copies, remote signals or barrier semaphores. Data moves between devices by JAX's collectives and lax.ppermute only.
A program may use at most 64 MiB of HBM per device.

v0:
```python
import math

import jax
import jax.numpy as jnp
from jax import lax
from jax.sharding import PartitionSpec as P


def from_behind(x, axis, by):
    size = lax.axis_size(axis)
    pairs = [(i, i + by) for i in range(size) if 0 <= i + by < size]
    return lax.ppermute(x, axis, pairs)


def angle_table(row_count, col_count, modulus):
    products = (
        jnp.arange(row_count, dtype=jnp.int32)[:, None]
        * jnp.arange(col_count, dtype=jnp.int32)[None, :]
        % modulus
    )
    return 2.0 * math.pi / modulus * products.astype(jnp.float32)


def split_length(seq_len):
    padded_len = 2 * seq_len
    inner = 1
    for factor in range(1, math.isqrt(padded_len) + 1):
        if seq_len % factor == 0:
            inner = factor
    return (padded_len // inner, inner)


def forward_transform(signal, outer, inner):
    padded_len = outer * inner
    outer_angle = angle_table(outer, outer // 2, outer)
    real_part = jnp.einsum(
        "kn,cnb->ckb", jnp.cos(outer_angle), signal, precision=lax.Precision.HIGH
    )
    imag_part = -jnp.einsum(
        "kn,cnb->ckb", jnp.sin(outer_angle), signal, precision=lax.Precision.HIGH
    )
    twiddle = angle_table(outer, inner, padded_len)
    tw_cos = jnp.cos(twiddle)
    tw_sin = jnp.sin(twiddle)
    turned_real = real_part * tw_cos + imag_part * tw_sin
    turned_imag = imag_part * tw_cos - real_part * tw_sin
    inner_angle = angle_table(inner, inner, inner)
    stacked = jnp.stack([turned_real, turned_imag])
    with_cos = jnp.einsum(
        "xckn,nm->xckm", stacked, jnp.cos(inner_angle), precision=lax.Precision.HIGH
    )
    with_sin = jnp.einsum(
        "xckn,nm->xckm", stacked, jnp.sin(inner_angle), precision=lax.Precision.HIGH
    )
    return (with_cos[0] + with_sin[1], with_cos[1] - with_sin[0])


def inverse_transform(real_in, imag_in, outer, inner):
    padded_len = outer * inner
    inner_angle = angle_table(inner, inner, inner)
    stacked = jnp.stack([real_in, imag_in])
    with_cos = jnp.einsum(
        "xckm,mn->xckn", stacked, jnp.cos(inner_angle), precision=lax.Precision.HIGH
    )
    with_sin = jnp.einsum(
        "xckm,mn->xckn", stacked, jnp.sin(inner_angle), precision=lax.Precision.HIGH
    )
    back_real = with_cos[0] - with_sin[1]
    back_imag = with_cos[1] + with_sin[0]
    twiddle = angle_table(outer, inner, padded_len)
    tw_cos = jnp.cos(twiddle)
    tw_sin = jnp.sin(twiddle)
    turned_real = back_real * tw_cos - back_imag * tw_sin
    turned_imag = back_imag * tw_cos + back_real * tw_sin
    outer_angle = angle_table(outer, outer // 2, outer)
    result = jnp.einsum(
        "kn,ckb->cnb", jnp.cos(outer_angle), turned_real, precision=lax.Precision.HIGH
    )
    result = result - jnp.einsum(
        "kn,ckb->cnb", jnp.sin(outer_angle), turned_imag, precision=lax.Precision.HIGH
    )
    return result / padded_len


def body(tokens, proj_weight, short_taps, long_filter, skip_gain):
    tok_rows = tokens.shape[0]
    branch_count = proj_weight.shape[1]
    local_channels = proj_weight.shape[2]
    features = lax.all_gather(tokens, "tp", axis=1, tiled=True)
    portion = lax.all_gather(proj_weight, "ctx", axis=0, tiled=True)
    projected = jnp.dot(
        features, portion.reshape(portion.shape[0], -1), preferred_element_type=jnp.float32
    )
    projected = projected.astype(jnp.bfloat16).reshape(tok_rows, branch_count, local_channels)
    lag_count = short_taps.shape[0]
    rim_block = from_behind(projected[tok_rows - (lag_count - 1) :], "ctx", 1)
    padded = jnp.concatenate([rim_block, projected], 0).astype(jnp.float32)
    mixed = jnp.zeros((tok_rows, branch_count, local_channels), jnp.float32)
    for lag_index in range(lag_count):
        first_row = lag_count - 1 - lag_index
        mixed = mixed + short_taps[lag_index] * padded[first_row : first_row + tok_rows]
    gate_query = mixed[:, 0].T.astype(jnp.bfloat16)
    gated_input = (mixed[:, 1] * mixed[:, 2]).T.astype(jnp.bfloat16)
    owned = lax.all_to_all(gated_input, "ctx", split_axis=0, concat_axis=1, tiled=True)
    owned_channels = owned.shape[0]
    seq_len = owned.shape[1]
    outer, inner = split_length(seq_len)
    signal = owned.astype(jnp.float32)
    signal_real, signal_imag = forward_transform(
        signal.reshape(owned_channels, outer // 2, inner), outer, inner
    )
    filter_real, filter_imag = forward_transform(
        long_filter.reshape(owned_channels, outer // 2, inner), outer, inner
    )
    spectrum_real = signal_real * filter_real - signal_imag * filter_imag
    spectrum_imag = signal_real * filter_imag + signal_imag * filter_real
    convolved = inverse_transform(spectrum_real, spectrum_imag, outer, inner).reshape(
        owned_channels, seq_len
    )
    convolved = (convolved + skip_gain[:, None] * signal).astype(jnp.bfloat16)
    returned = lax.all_to_all(convolved, "ctx", split_axis=1, concat_axis=0, tiled=True)
    product = gate_query.astype(jnp.float32) * returned.astype(jnp.float32)
    return product.T.astype(jnp.bfloat16)


def solution(mesh):
    placed = (
        P("ctx", "tp"),
        P("ctx", None, "tp"),
        P(None, None, "tp"),
        P(("tp", "ctx"), None),
        P(("tp", "ctx")),
    )
    return jax.shard_map(
        body, mesh=mesh, in_specs=placed, out_specs=P("ctx", "tp"), check_vma=False
    )
```

profile of v0, /device:TPU:1, one launch (start us, length us, event | category | flops | bytes accessed | tf_op | source)
XLA Modules:
  0.0 315.4 jit_solution(15167963860470727017)
XLA Ops:
  6.5 1.8 copy.18
  9.1 0.7 slice_bitcast_fusion.2
  9.9 101.9 %all-gather.5.cloned.1.call-done = bf16[4096,3,256]{0,2,1:T(8,128)(2,1)} async-done(((bf16[128,3,256]{0,2,1:T(8,128)(2,1)}), bf16[4096,3,256]{0,2,1:T(8,128)(2,1)}) %all-gather.5.cloned.1.call-update) | async-done | bytes 6291472 | tf_op jit(solution)/shard_map/all_gather | solution.py:90
  111.8 92.4 %all-gather.3.cloned.1.call-done = bf16[1024,4096]{1,0:T(8,128)(2,1)} async-done(((bf16[1024,512]{1,0:T(8,128)(2,1)}), bf16[1024,4096]{1,0:T(8,128)(2,1)}) %all-gather.3.cloned.1.call-update) | async-done | bytes 8388624 | tf_op jit(solution)/shard_map/all_gather | solution.py:89
  204.2 11.9 %convolution_convert_fusion = bf16[1024,768]{1,0:T(8,128)(2,1)} fusion(bf16[1024,4096]{1,0:T(8,128)(2,1)} %all-gather.3.cloned.1.call-done, bf16[4096,768]{0,1:T(8,128)(2,1)} %bitcast.130), kind=kOutput, calls=%fused_computation.43 | convolution fusion | flops 6443237376 | bytes 16252928 | tf_op jit(solution)/shard_map/dot_general | solution.py:91
  216.1 0.7 slice.93
  216.8 4.9 %collective-permute-start = (bf16[2,3,256]{2,1,0:T(4,128)(2,1)S(1)}, bf16[2,3,256]{2,1,0:T(4,128)(2,1)S(1)}, u32[]{:S(2)}, u32[]{:S(2)}) collective-permute-start(bf16[2,3,256]{2,1,0:T(4,128)(2,1)S(1)} %slice.72), channel_id=1, source_target_pairs={{0,8},{8,16},{16,24},{24,32},{32,40},{40,48},{48,56},{56,64},{64,7... | collective-permute-start | bytes 9224 | tf_op jit(solution)/shard_map/ppermute | solution.py:12
  221.7 1.0 fusion.85
  223.5 1.7 copy.19
  225.3 0.8 copy.20
  226.1 1.7 maximum_convert_fusion
  227.8 2.5 fusion.6
  230.3 1.7 copy-done.4
  232.0 0.9 fusion.48
  233.0 8.5 %all-to-all-start = ((bf16[32,8,1024]{2,1,0:T(8,128)(2,1)}), bf16[32,8,1024]{2,1,0:T(8,128)(2,1)S(1)}, u32[]{:S(2)}, u32[]{:S(2)}) async-start(bf16[32,8,1024]{2,1,0:T(8,128)(2,1)} %fusion.48), calls=%async_computation | async-start | bytes 1048576 | tf_op jit(solution)/shard_map/all_to_all | solution.py:104
  241.5 1.5 fusion.38
  243.0 2.0 add_bitcast_fusion
  245.0 4.7 %fusion.2 = f32[2,8,256,256]{3,2,1,0:T(8,128)} fusion(f32[1,8,256,256]{3,2,1,0:T(8,128)S(1)} %get-tuple-element.8, f32[1,8,256,256]{3,2,1,0:T(8,128)S(1)} %get-tuple-element.7), kind=kOutput, calls=%fused_computation.5 | convolution fusion | flops 1612578816 | bytes 8388608 | tf_op jit(solution)/shard_map/xckn,nm->xckm/dot_general | solution.py:52
  249.7 4.8 %fusion.3 = f32[2,8,256,256]{3,2,1,0:T(8,128)} fusion(f32[1,8,256,256]{3,2,1,0:T(8,128)S(1)} %get-tuple-element.8, f32[1,8,256,256]{3,2,1,0:T(8,128)S(1)} %get-tuple-element.7), kind=kOutput, calls=%fused_computation.6 | convolution fusion | flops 1612578816 | bytes 8388608 | tf_op jit(solution)/shard_map/xckn,nm->xckm/dot_general | solution.py:49
  254.5 3.5 %all-to-all-done = bf16[32,8,1024]{2,1,0:T(8,128)(2,1)S(1)} async-done(((bf16[32,8,1024]{2,1,0:T(8,128)(2,1)}), bf16[32,8,1024]{2,1,0:T(8,128)(2,1)S(1)}, u32[]{:S(2)}, u32[]{:S(2)}) %all-to-all-start) | async-done | bytes 524320 | tf_op jit(solution)/shard_map/all_to_all | solution.py:104
  258.6 1.2 fusion.71
  259.9 1.7 fusion.11
  261.5 4.4 %fusion.4 = f32[2,8,256,256]{3,2,1,0:T(8,128)S(1)} fusion(f32[1,8,256,256]{2,3,1,0:T(8,128)S(1)} %get-tuple-element.10, f32[1,8,256,256]{2,3,1,0:T(8,128)S(1)} %get-tuple-element.9), kind=kOutput, calls=%fused_computation.7 | convolution fusion | flops 1612578816 | bytes 8388608 | tf_op jit(solution)/shard_map/xckn,nm->xckm/dot_general | solution.py:52
  266.0 4.4 %fusion.5 = f32[2,8,256,256]{3,2,1,0:T(8,128)S(1)} fusion(f32[1,8,256,256]{2,3,1,0:T(8,128)S(1)} %get-tuple-element.10, f32[1,8,256,256]{2,3,1,0:T(8,128)S(1)} %get-tuple-element.9), kind=kOutput, calls=%fused_computation.8 | convolution fusion | flops 1612578816 | bytes 8388608 | tf_op jit(solution)/shard_map/xckn,nm->xckm/dot_general | solution.py:49
  270.4 1.3 multiply_subtract_fusion
  271.8 3.0 fusion
  274.8 3.0 fusion.1
  277.7 1.9 fusion.14
  279.6 1.9 fusion.28
  282.9 23.1 %all_to_all.26 = bf16[8,32,1024]{2,0,1:T(8,128)(2,1)S(1)} all-to-all(bf16[8,32,1024]{2,0,1:T(8,128)(2,1)S(1)} %fusion.33), channel_id=1, replica_groups=mesh['ctx'=32,'tp'=8] {'ctx'}, dimensions={1} | all-to-all | bytes 1048576 | tf_op jit(solution)/shard_map/all_to_all | solution.py:121
  305.9 1.4 fusion.46
  307.3 1.0 copy.36
  (28 shorter events, 3.5 us)
Async XLA Ops:
  6.5 235.0 %copy-start = (f32[8,32768]{1,0:T(8,128)S(1)}, f32[8,32768]{1,0:T(8,128)}, u32[]{:S(2)}) copy-start(f32[8,32768]{1,0:T(8,128)} %param.8) | copy-start | bytes 3145732
  6.5 105.3 %all-gather.5.cloned.1.call-start = ((), (), s32[]{:S(2)}) async-start(), calls=%async_computation.3 | async-start | bytes 6488064 | tf_op jit(solution)/shard_map/all_gather | solution.py:90
  8.4 195.8 %all-gather.3.cloned.1.call-start = ((), (), s32[]{:S(2)}) async-start(), calls=%async_computation.2 | async-start | bytes 9437184 | tf_op jit(solution)/shard_map/all_gather | solution.py:89
  216.8 8.5 %collective-permute-start = (bf16[2,3,256]{2,1,0:T(4,128)(2,1)S(1)}, bf16[2,3,256]{2,1,0:T(4,128)(2,1)S(1)}, u32[]{:S(2)}, u32[]{:S(2)}) collective-permute-start(bf16[2,3,256]{2,1,0:T(4,128)(2,1)S(1)} %slice.72), channel_id=1, source_target_pairs={{0,8},{8,16},{16,24},{24,32},{32,40},{40,48},{48,56},{56,64},{64,7... | collective-permute-start | bytes 9224 | tf_op jit(solution)/shard_map/ppermute | solution.py:12
  222.7 0.7 copy-start.5
  230.3 1.7 copy-start.4
  233.0 10.1 %copy-start.6 = (f32[256,256]{1,0:T(8,128)S(1)}, f32[256,256]{1,0:T(8,128)}, u32[]{:S(2)}) copy-start(f32[256,256]{1,0:T(8,128)} %copy-done.5) | copy-start | bytes 786436
  233.0 25.1 %all-to-all-start = ((bf16[32,8,1024]{2,1,0:T(8,128)(2,1)}), bf16[32,8,1024]{2,1,0:T(8,128)(2,1)S(1)}, u32[]{:S(2)}, u32[]{:S(2)}) async-start(bf16[32,8,1024]{2,1,0:T(8,128)(2,1)} %fusion.48), calls=%async_computation | async-start | bytes 1048576 | tf_op jit(solution)/shard_map/all_to_all | solution.py:104
  266.0 4.4 %copy-start.2 = (f32[2,8,256,256]{3,2,1,0:T(8,128)S(1)}, f32[2,8,256,256]{3,2,1,0:T(8,128)}, u32[]{:S(2)}) copy-start(f32[2,8,256,256]{3,2,1,0:T(8,128)} %fusion.2) | copy-start | bytes 12582916
  266.0 4.4 %copy-start.3 = (f32[2,8,256,256]{3,2,1,0:T(8,128)S(1)}, f32[2,8,256,256]{3,2,1,0:T(8,128)}, u32[]{:S(2)}) copy-start(f32[2,8,256,256]{3,2,1,0:T(8,128)} %fusion.3) | copy-start | bytes 12582916
  281.6 0.7 copy-start.7
  282.2 26.1 %copy-start.1 = (f32[8,32768]{1,0:T(8,128)S(1)}, f32[8,32768]{1,0:T(8,128)}, u32[]{:S(2)}) copy-start(f32[8,32768]{1,0:T(8,128)} %param.8) | copy-start | bytes 3145732
Sparse Core Ops, SparseCore 0:
  9.9 101.8 all-gather.4
  113.6 90.5 all-gather.2
where the time goes:
time: 321 us; the launch traced here: 315 us
  waiting for transfers between devices  199 us (62%)
  matrix products  46.3 us (14%)
  blocking collectives  23.1 us (7%)
  between operations  13.9 us (4%)
  starting transfers between devices  13.4 us (4%)
  local copies, waits for them, and re-layouts  10.6 us (3%)
  other arithmetic  9.52 us (3%)
    all_gather x1, waiting for transfers between devices, body(): portion = lax.all_gather(proj_weight, 'ctx', axis=0, tiled=True)  102 us
    all_gather x1, waiting for transfers between devices, body(): features = lax.all_gather(tokens, 'tp', axis=1, tiled=True)  92.4 us
    all_to_all x1, blocking collectives, body(): lax.all_to_all(convolved, 'ctx', split_axis=1, concat_axis=0, tiled=True)  23.1 us
    dot_general x1, matrix products, body(): jnp.dot(features, portion.reshape(portion.shape[0], -1), preferred_elemen...  11.9 us
    dot_general x2, matrix products, forward_transform(): jnp.einsum('xckn,nm->xckm', stacked, jnp.cos(inner_angle), precision=lax....  9.18 us
    dot_general x2, matrix products, forward_transform(): jnp.einsum('xckn,nm->xckm', stacked, jnp.sin(inner_angle), precision=lax....  9.14 us
    all_to_all x1, starting transfers between devices, body(): lax.all_to_all(gated_input, 'ctx', split_axis=0, concat_axis=1, tiled=True)  8.51 us
  transfers between devices with their start and end apart: 4, of which 3 were waited for; matrix products, arithmetic and copies ran while one was open for 5% of the time, Pallas kernels for 0%

commit v1 on v0

v1 whole, which is shorter than its diff:
```python
import math

import jax
import jax.numpy as jnp
import numpy as np
from jax import lax
from jax.experimental import pallas as pl
from jax.experimental.pallas import tpu as pltpu
from jax.sharding import PartitionSpec as P

F32 = jnp.float32
BF16 = jnp.bfloat16
MIB = 1 << 20
VMEM = 56 * MIB

Z_GROUPS = [[z * 4 + r for z in range(8)] for r in range(4)]
OTHER_CORE = [(i, i ^ 1) for i in range(32)]
OTHER_XLO = [(i, i ^ 4) for i in range(8)]
FROM_UP = [(i, (i & 4) | ((i - 1) & 3)) for i in range(8)]
FROM_DOWN = [(i, (i & 4) | ((i + 1) & 3)) for i in range(8)]
ACROSS = [(i, (i & 4) | ((i + 2) & 3)) for i in range(8)]
ROWS = 1024
HALF = 512
OWN = 384
FOUR_GROUPS = [[z * 4 + r for r in range(4)] for z in range(8)]
HALO = 16
OUTER = 128
INNER = 256


def other_xlo(x):
    return lax.ppermute(x, "tp", OTHER_XLO)


def from_up(x):
    return lax.ppermute(x, "tp", FROM_UP)


def from_down(x):
    return lax.ppermute(x, "tp", FROM_DOWN)


def tied(*xs):
    return lax.optimization_barrier(xs)


def dot(a, b):
    return jnp.dot(a, b, preferred_element_type=F32)


def vmem_specs(count):
    return [pl.BlockSpec(memory_space=pltpu.VMEM)] * count


def whole(shape):
    return pl.BlockSpec(shape, lambda r: (0,) * len(shape))


def tile(rows, cols):
    return pl.BlockSpec((rows, cols), lambda r: (r, 0))


def halves(cols):
    return [
        pl.BlockSpec((256, cols), lambda r: (jnp.minimum(r, 1), 0)),
        pl.BlockSpec((256, cols), lambda r: (jnp.maximum(r - 2, 0), 0)),
    ]


def for_each_half(step):
    r = pl.program_id(0)
    pl.when(r < 2)(lambda: step(0))
    pl.when(r >= 2)(lambda: step(1))


def partial_kernel(places, *refs):
    units, (last_ref, w_ref, out_ref, rim_ref) = refs[:14], refs[14:]

    def step(half):
        total = dot(units[half][...], w_ref[places[0]])
        for u in range(1, 7):
            total += dot(units[2 * u + half][...], w_ref[places[u]])
        out_ref[...] = total

    for_each_half(step)

    @pl.when(pl.program_id(0) == 3)
    def _():
        rim = out_ref[256 - HALO :, :256] + dot(last_ref[...], w_ref[places[7], :, :256])
        rim_ref[...] = rim.astype(BF16)


def partial_products(places, units, last_rows, w):
    return pl.pallas_call(
        partial_kernel,
        grid=(4,),
        out_shape=(
            jax.ShapeDtypeStruct((ROWS, OWN), F32),
            jax.ShapeDtypeStruct((HALO, 256), BF16),
        ),
        in_specs=[pl.BlockSpec(memory_space=pltpu.SMEM)]
        + halves(512) * 7
        + [whole((HALO, 512)), whole((8, 512, OWN))],
        out_specs=(tile(256, OWN), whole((HALO, 256))),
        compiler_params=pltpu.CompilerParams(vmem_limit_bytes=VMEM),
        cost_estimate=pl.CostEstimate(
            flops=2 * 7 * 1024 * 512 * OWN, bytes_accessed=11 * MIB, transcendentals=0
        ),
    )(places, *units, last_rows, w)


def rim_kernel(places, *refs):
    units, (w_ref, out_ref) = refs[:8], refs[8:]
    total = dot(units[0][...], w_ref[places[0], :, :256])
    for u in range(1, 8):
        total += dot(units[u][...], w_ref[places[u], :, :256])
    out_ref[...] = total.astype(BF16)


def rim_rows(places, units, last_rows, w):
    last = HALF // HALO - 1
    return pl.pallas_call(
        rim_kernel,
        grid=(1,),
        out_shape=jax.ShapeDtypeStruct((HALO, 256), BF16),
        in_specs=[pl.BlockSpec(memory_space=pltpu.SMEM)]
        + [pl.BlockSpec((HALO, 512), lambda r: (last, 0))] * 7
        + [whole((HALO, 512)), whole((8, 512, OWN))],
        out_specs=whole((HALO, 256)),
        compiler_params=pltpu.CompilerParams(vmem_limit_bytes=VMEM),
        cost_estimate=pl.CostEstimate(
            flops=2 * 8 * 256 * 512 * 256, bytes_accessed=4 * MIB, transcendentals=0
        ),
    )(places, *units[1::2], last_rows, w)


def filtered(scratch, branch, taps, start, size):
    total = taps[0:1, :] * scratch[branch, pl.ds(HALO + start, size), :]
    for lag in (1, 2):
        total = total + taps[lag : lag + 1, :] * scratch[branch, pl.ds(HALO + start - lag, size), :]
    return total


def gated_kernel(places, *refs):
    units, (acc_ref, own_ref, sib_ref, rim_ref, taps_ref, out_ref, scratch) = refs[:16], refs[16:]
    r = pl.program_id(0)

    @pl.when(r == 0)
    def _():
        scratch[0, 0:HALO, :] = rim_ref[:, :256].astype(F32)
        scratch[1, 0:HALO, :] = rim_ref[:, 256:].astype(F32)

    @pl.when(r > 0)
    def _():
        scratch[:, 0:HALO, :] = scratch[:, 256 : 256 + HALO, :]

    def step(half):
        own = acc_ref[:, :256] + dot(units[14 + half][...], own_ref[0, :, :256])
        scratch[0, HALO:, :] = own.astype(BF16).astype(F32)
        sib = dot(units[half][...], sib_ref[places[0], :, :256])
        for u in range(1, 8):
            sib += dot(units[2 * u + half][...], sib_ref[places[u], :, :256])
        scratch[1, HALO:, :] = sib.astype(BF16).astype(F32)

    for_each_half(step)
    a = filtered(scratch, 0, taps_ref[0], 0, 256)
    b = filtered(scratch, 1, taps_ref[1], 0, 256)
    out_ref[...] = (a * b).T.reshape(32, 8, 256).astype(BF16)


def gated_input(places, units, acc, own, sib, rim, taps):
    specs = (
        [pl.BlockSpec((256, 512), lambda r, p: (jnp.minimum(r, 1), 0)),
         pl.BlockSpec((256, 512), lambda r, p: (jnp.maximum(r - 2, 0), 0))] * 8
        + [
            pl.BlockSpec((256, OWN), lambda r, p: (r, 0)),
            pl.BlockSpec((1, 512, OWN), lambda r, p: (p[7], 0, 0)),
            pl.BlockSpec((8, 512, OWN), lambda r, p: (0, 0, 0)),
            pl.BlockSpec((HALO, 512), lambda r, p: (0, 0)),
            pl.BlockSpec((2, 3, 256), lambda r, p: (0, 0, 0)),
        ]
    )
    return pl.pallas_call(
        gated_kernel,
        out_shape=jax.ShapeDtypeStruct((32, 8, ROWS), BF16),
        grid_spec=pltpu.PrefetchScalarGridSpec(
            num_scalar_prefetch=1,
            grid=(4,),
            in_specs=specs,
            out_specs=pl.BlockSpec((32, 8, 256), lambda r, p: (0, 0, r)),
            scratch_shapes=[pltpu.VMEM((2, HALO + 256, 256), F32)],
        ),
        compiler_params=pltpu.CompilerParams(vmem_limit_bytes=VMEM),
        cost_estimate=pl.CostEstimate(
            flops=2 * 9 * 1024 * 512 * 256, bytes_accessed=13 * MIB, transcendentals=0
        ),
    )(places, *units, acc, own, sib, rim, taps)


def query_kernel(places, even, *refs):
    units, (acc_ref, own_ref, sib_ref, out_ref) = refs[:16], refs[16:]

    def step(half):
        own = acc_ref[:, 256:] + dot(units[14 + half][...], own_ref[0, :, 256:])
        sib = dot(units[half][...], sib_ref[places[0]])
        for u in range(1, 8):
            sib += dot(units[2 * u + half][...], sib_ref[places[u]])
        first_core = even[0] == 1
        left = jnp.where(first_core, own, sib)
        right = jnp.where(first_core, sib, own)
        out_ref[...] = jnp.concatenate([left, right], 1).astype(BF16)

    for_each_half(step)


def query_rows(places, even, units, acc, own, sib):
    specs = (
        [pl.BlockSpec((256, 512), lambda r, p, e: (jnp.minimum(r, 1), 0)),
         pl.BlockSpec((256, 512), lambda r, p, e: (jnp.maximum(r - 2, 0), 0))] * 8
        + [
            pl.BlockSpec((256, OWN), lambda r, p, e: (r, 0)),
            pl.BlockSpec((1, 512, OWN), lambda r, p, e: (p[7], 0, 0)),
            pl.BlockSpec((8, 512, 128), lambda r, p, e: (0, 0, 2)),
        ]
    )
    return pl.pallas_call(
        query_kernel,
        out_shape=jax.ShapeDtypeStruct((ROWS, 256), BF16),
        grid_spec=pltpu.PrefetchScalarGridSpec(
            num_scalar_prefetch=2,
            grid=(4,),
            in_specs=specs,
            out_specs=pl.BlockSpec((256, 256), lambda r, p, e: (r, 0)),
        ),
        compiler_params=pltpu.CompilerParams(vmem_limit_bytes=VMEM),
        cost_estimate=pl.CostEstimate(
            flops=2 * 9 * 1024 * 512 * 128, bytes_accessed=16 * MIB, transcendentals=0
        ),
    )(places, even, *units, acc, own, sib)


def gate_kernel(query_ref, rim_ref, taps_ref, out_ref, scratch):
    scratch[0, 0:HALO, :] = rim_ref[...].astype(F32)
    scratch[0, HALO:, :] = query_ref[...].astype(F32)
    for r in range(ROWS // 256):
        out_ref[r * 256 : r * 256 + 256, :] = filtered(scratch, 0, taps_ref[...], r * 256, 256).astype(BF16)


def query_gate(query, rim, taps):
    return pl.pallas_call(
        gate_kernel,
        out_shape=jax.ShapeDtypeStruct((ROWS, 256), BF16),
        in_specs=vmem_specs(3),
        out_specs=pl.BlockSpec(memory_space=pltpu.VMEM),
        scratch_shapes=[pltpu.VMEM((1, HALO + ROWS, 256), F32)],
        compiler_params=pltpu.CompilerParams(vmem_limit_bytes=VMEM),
        cost_estimate=pl.CostEstimate(flops=1024 * 256 * 6, bytes_accessed=MIB, transcendentals=0),
    )(query, rim, taps)


def two_parts(table):
    high = table.astype(BF16)
    return np.stack([high, (table - high.astype(np.float64)).astype(BF16)])


def tables():
    a = np.arange(OUTER, dtype=np.float64)
    b = np.arange(INNER, dtype=np.float64)
    outer = 2 * np.pi / OUTER * np.outer(a + 0.25, a)
    first = np.concatenate([np.cos(outer), -np.sin(outer)], 0)
    order = (4 * np.arange(32)[None, :] + np.arange(4)[:, None]).reshape(-1)
    inner = 2 * np.pi / INNER * (np.outer(b, b) % INNER)
    turn = np.concatenate([np.cos(inner), np.sin(inner)], 1)
    twist = 2 * np.pi / (OUTER * INNER) * np.outer(a + 0.25, b)
    twiddle = np.stack([np.cos(twist), np.sin(twist)]).astype(np.float32)
    shuffled = first[:, order].astype(BF16)
    packed = np.concatenate([turn.astype(BF16), shuffled, np.concatenate([shuffled[:, :].T, np.zeros((128, 256), BF16)], 0)], 1)
    return two_parts(first), two_parts(turn), packed, twiddle


def split_value(x):
    high = x.astype(BF16)
    return high, (x - high.astype(F32)).astype(BF16)


def turned_forward(wave, c, s):
    real, imag = wave[:OUTER], wave[OUTER:]
    return jnp.concatenate([real * c + imag * s, imag * c - real * s], 0)


def joined_forward(r):
    return r[:OUTER, :INNER] + r[OUTER:, INNER:], r[OUTER:, :INNER] - r[:OUTER, INNER:]


def filter_kernel(h_ref, first_ref, turn_ref, twiddle_ref, out_ref):
    c, s = twiddle_ref[0], twiddle_ref[1]

    def step(ch, carry):
        high, low = split_value(h_ref[ch])
        wave = dot(first_ref[0], high) + (dot(first_ref[1], high) + dot(first_ref[0], low))
        high, low = split_value(turned_forward(wave, c, s))
        wave = dot(high, turn_ref[0]) + (dot(high, turn_ref[1]) + dot(low, turn_ref[0]))
        out_ref[ch] = jnp.concatenate(joined_forward(wave), 0) * (1.0 / (OUTER * INNER))
        return carry

    lax.fori_loop(0, 8, step, 0)


def filter_spectrum(h, first, turn, twiddle):
    return pl.pallas_call(
        filter_kernel,
        out_shape=jax.ShapeDtypeStruct((8, 2 * OUTER, INNER), F32),
        in_specs=vmem_specs(4),
        out_specs=pl.BlockSpec(memory_space=pltpu.VMEM),
        compiler_params=pltpu.CompilerParams(vmem_limit_bytes=VMEM),
        cost_estimate=pl.CostEstimate(
            flops=2 * 3 * 8 * (128 * 256 * 256 + 256 * 256 * 512), bytes_accessed=5 * MIB, transcendentals=0
        ),
    )(h, first, turn, twiddle)


def convolve_kernel(x_ref, h_ref, gain_ref, table_ref, twiddle_ref, out_ref, wide, result):
    c, s = twiddle_ref[0], twiddle_ref[1]
    turn, first, last = table_ref[:, :512], table_ref[:, 512:640], table_ref[:128, 640:]
    wide[...] = x_ref[...].astype(F32)
    for ch in range(8):
        row = wide[:, ch, :]
        x = jnp.concatenate([row[:, q * 256 : q * 256 + 256] for q in range(4)], 0).astype(BF16)
        turned = turned_forward(dot(first, x), c, s).astype(BF16)
        xr, xi = joined_forward(dot(turned, turn))
        hr, hi = h_ref[ch, :OUTER], h_ref[ch, OUTER:]
        product = jnp.concatenate([xr * hr - xi * hi, xr * hi + xi * hr], 0).astype(BF16)
        r = dot(product, turn)
        br = r[:OUTER, :INNER] - r[OUTER:, INNER:]
        bi = r[:OUTER, INNER:] + r[OUTER:, :INNER]
        back = jnp.concatenate([br * c - bi * s, bi * c + br * s], 0).astype(BF16)
        y = dot(last, back)
        result[:, ch, :] = jnp.concatenate([y[q * 32 : q * 32 + 32] for q in range(4)], 1)
    out_ref[...] = (result[...] + gain_ref[...][None] * wide[...]).astype(BF16)


def convolve(x, h, gain, table, twiddle):
    return pl.pallas_call(
        convolve_kernel,
        out_shape=jax.ShapeDtypeStruct((32, 8, ROWS), BF16),
        in_specs=vmem_specs(5),
        out_specs=pl.BlockSpec(memory_space=pltpu.VMEM),
        scratch_shapes=[pltpu.VMEM((32, 8, ROWS), F32)] * 2,
        compiler_params=pltpu.CompilerParams(vmem_limit_bytes=VMEM),
        cost_estimate=pl.CostEstimate(
            flops=2 * 8 * 2 * (128 * 256 * 256 + 256 * 256 * 512), bytes_accessed=5 * MIB, transcendentals=0
        ),
    )(x, h, gain, table, twiddle)


def finish_kernel(conv_ref, gate_ref, out_ref):
    for r in range(ROWS // 256):
        cols = slice(r * 256, r * 256 + 256)
        conv = conv_ref[:, :, cols].astype(F32).reshape(256, 256).T
        out_ref[cols, :] = (conv * gate_ref[cols, :].astype(F32)).astype(BF16)


def finish(conv, gate):
    return pl.pallas_call(
        finish_kernel,
        out_shape=jax.ShapeDtypeStruct((ROWS, 256), BF16),
        in_specs=vmem_specs(2),
        out_specs=pl.BlockSpec(memory_space=pltpu.VMEM),
        compiler_params=pltpu.CompilerParams(vmem_limit_bytes=VMEM),
        cost_estimate=pl.CostEstimate(flops=1024 * 256, bytes_accessed=2 * MIB, transcendentals=0),
    )(conv, gate)


def next_shard(x):
    return lax.ppermute(x, "ctx", [(i, i + 1) for i in range(31)])


def body(tokens, proj_weight, short_taps, long_filter, skip_gain):
    ctx, tp = lax.axis_index("ctx"), lax.axis_index("tp")
    even = ctx % 2 == 0
    first, turn, packed, twiddle = (jnp.asarray(t) for t in tables())

    near = lax.all_gather(proj_weight.transpose(1, 0, 2), "ctx", axis_index_groups=FOUR_GROUPS)
    q, k, v = (near[:, g].reshape(512, 256) for g in range(3))
    block = jnp.concatenate([jnp.where(even, k, v), jnp.where(even, q[:, :128], q[:, 128:])], 1)
    own = lax.all_gather(block, "ctx", axis_index_groups=Z_GROUPS)

    spectrum = filter_spectrum(long_filter.reshape(8, OUTER, INNER), first, turn, twiddle)
    a0 = (tokens[:HALF], tokens[HALF:])
    ap, am, b0 = zip(*(tied(from_up(t), from_down(t), other_xlo(t)) for t in a0))
    bp, bm, a2 = zip(*(tied(other_xlo(p), from_down(b), from_up(p)) for p, b in zip(ap, b0)))
    rim_b2 = lax.ppermute(b0[1][HALF - HALO :], "tp", ACROSS)
    b2 = (from_up(bp[0]), from_down(bm[1]))
    own, spectrum, a2, bp, bm = tied(own, spectrum, a2, bp, bm)

    xlo, y = tp // 4, tp % 4
    mine, others = xlo * 4, (1 - xlo) * 4
    shift = lambda n: (y + n) % 4
    places = jnp.stack(
        [
            mine + y,
            mine + shift(1),
            mine + shift(3),
            others + y,
            others + shift(1),
            others + shift(3),
            mine + shift(2),
            others + shift(2),
        ]
    ).astype(jnp.int32)
    sib = lax.ppermute(own, "ctx", OTHER_CORE)
    units = (*a0, *ap, *am, *b0, *bp, *bm, *a2)
    acc, rim_own = partial_products(places, units, rim_b2, own)
    rim = next_shard(jnp.concatenate([rim_rows(places, units, rim_b2, sib), rim_own], 1))
    taps = short_taps.transpose(1, 0, 2)
    taps_kv = jnp.where(even, taps[1:3], taps[2:0:-1])
    gated = gated_input(places, units + b2, acc, own, sib, rim, taps_kv)

    owned = lax.all_to_all(gated, "ctx", 0, 0)
    convolved = convolve(owned, spectrum, skip_gain[:, None], packed, twiddle)
    returned = lax.all_to_all(convolved, "ctx", 0, 0)

    flag = even.astype(jnp.int32).reshape(1)
    query = query_rows(places, flag, units + b2, acc, own, sib)
    gate = query_gate(query, next_shard(query[ROWS - HALO :]), taps[0])
    return finish(returned, gate)


def solution(mesh):
    placed = (
        P("ctx", "tp"),
        P("ctx", None, "tp"),
        P(None, None, "tp"),
        P(("tp", "ctx"), None),
        P(("tp", "ctx")),
    )
    return jax.shard_map(
        body, mesh=mesh, in_specs=placed, out_specs=P("ctx", "tp"), check_vma=False
    )
```

time: 321 us -> 183 us (0.57); the launches traced: 315 us -> 182 us
  waiting for transfers between devices: 199 us -> 42.1 us
  Pallas kernels: 0 us -> 52.6 us
  matrix products: 46.3 us -> 0 us
  starting transfers between devices: 13.4 us -> 46.5 us
  blocking collectives: 23.1 us -> 12.1 us
  other arithmetic: 9.52 us -> 2.19 us
    all_gather x2 -> x1, waiting for transfers between devices: 194 us -> 0.01 us  [body(): own = lax.all_gather(block, 'ctx', axis_index_groups=Z_GROUPS)]
    pallas_call x0 -> x8, Pallas kernels: none -> 52.6 us  [the longest x1 9.84 us: gated_input(): pl.pallas_call(gated_kernel, out_shape=jax.ShapeDtypeStruct((32, 8, ROWS)...]
    dot_general x13 -> x0, matrix products: 46.3 us -> none  [the longest x1 11.9 us: body(): jnp.dot(features, portion.reshape(portion.shape[0], -1), preferred_elemen...]
    ppermute x1 -> x18, waiting for transfers between devices: 0.01 us -> 25.7 us  [the longest x4 15.5 us: other_xlo(): return lax.ppermute(x, 'tp', OTHER_XLO)]
    ppermute x1 -> x18, starting transfers between devices: 4.85 us -> 28.7 us  [the longest x2 10.4 us: next_shard(): return lax.ppermute(x, 'ctx', [(i, i + 1) for i in range(31)])]
    all_to_all x1 -> x0, blocking collectives: 23.1 us -> none  [body(): lax.all_to_all(convolved, 'ctx', split_axis=1, concat_axis=0, tiled=True)]
    all_to_all x1 -> x2, waiting for transfers between devices: 3.52 us -> 16.3 us  [the longest x1 16.3 us: body(): owned = lax.all_to_all(gated, 'ctx', 0, 0)]
    all_gather x0 -> x1, blocking collectives: none -> 12.1 us  [body(): lax.all_gather(proj_weight.transpose(1, 0, 2), 'ctx', axis_index_groups=F...]
  transfers between devices with their start and end apart: 4 -> 21, of which waited for: 3 -> 10; matrix products, arithmetic and copies ran while one was open for 5% -> 3% of each run, Pallas kernels for 0% -> 17%
where the time goes in v1:
time: 183 us; the launch traced here: 182 us
  Pallas kernels  52.6 us (29%)
  starting transfers between devices  46.5 us (25%)
  waiting for transfers between devices  42.1 us (23%)
  between operations  13.6 us (7%)
  local copies, waits for them, and re-layouts  12.6 us (7%)
  blocking collectives  12.1 us (7%)
  other arithmetic  2.19 us (1%)
    all_to_all x1, waiting for transfers between devices, body(): owned = lax.all_to_all(gated, 'ctx', 0, 0)  16.3 us
    ppermute x4, waiting for transfers between devices, other_xlo(): return lax.ppermute(x, 'tp', OTHER_XLO)  15.5 us
    all_gather x1, blocking collectives, body(): lax.all_gather(proj_weight.transpose(1, 0, 2), 'ctx', axis_index_groups=F...  12.1 us
    all_to_all x1, starting transfers between devices, body(): owned = lax.all_to_all(gated, 'ctx', 0, 0)  12.1 us
    ppermute x2, starting transfers between devices, next_shard(): return lax.ppermute(x, 'ctx', [(i, i + 1) for i in range(31)])  10.4 us
    ppermute x5, starting transfers between devices, from_up(): return lax.ppermute(x, 'tp', FROM_UP)  10.3 us
    pallas_call x1, Pallas kernels, gated_input(): pl.pallas_call(gated_kernel, out_shape=jax.ShapeDtypeStruct((32, 8, ROWS)...  9.84 us
    ppermute x5, waiting for transfers between devices, from_down(): return lax.ppermute(x, 'tp', FROM_DOWN)  9.3 us
  transfers between devices with their start and end apart: 21, of which 10 were waited for; matrix products, arithmetic and copies ran while one was open for 3% of the time, Pallas kernels for 17%

profile of v1, /device:TPU:1, one launch (start us, length us, event | category | flops | bytes accessed | tf_op | source)
XLA Modules:
  0.0 181.7 jit_solution(8687832114685859280)
XLA Ops:
  6.5 12.1 %all-gather = bf16[12,128,256]{2,1,0:T(8,128)(2,1)S(1)} all-gather(bf16[3,128,256]{2,1,0:T(8,128)(2,1)} %bitcast.33), channel_id=2, replica_groups={{0,8,16,24},{32,40,48,56},{64,72,80,88},{96,104,112,120},{128,136,144,1..., dimensions={0}, use_global_device_ids=true | all-gather | bytes 983040 | tf_op jit(solution)/shard_map/all_gather | solution.py:383
  18.8 0.8 pad_maximum_fusion
  20.3 1.3 collective-permute-start.1
  21.6 1.4 collective-permute-start
  23.0 1.0 collective-permute-start.5
  24.0 9.2 %collective-permute-done.2.refs_6_ = bf16[512,512]{1,0:T(8,128)(2,1)S(1)} collective-permute-done((bf16[512,512]{1,0:T(8,128)(2,1)S(1)}, bf16[512,512]{1,0:T(8,128)(2,1)S(1)}, u32[]{:S(2)}, u32[]{:S(2)}) %collective-permute-start.2) | collective-permute-done | bytes 524320 | tf_op jit(solution)/shard_map/ppermute | solution.py:32
  33.2 2.4 %collective-permute-start.3 = (bf16[512,512]{1,0:T(8,128)(2,1)S(1)}, bf16[512,512]{1,0:T(8,128)(2,1)S(1)}, u32[]{:S(2)}, u32[]{:S(2)}) collective-permute-start(bf16[512,512]{1,0:T(8,128)(2,1)S(1)} %get-tuple-element.49.refs_1_.refs_0_), channel_id=1, source_target_pairs={{0,3},{1,0},{2,1},{3,2},{4,7},{5,4},{6,5},{7,6},{8,11},{9,8},{10,9... | collective-permute-start | bytes 1572872 | tf_op jit(solution)/shard_map/ppermute | solution.py:36
  35.7 2.7 %collective-permute-start.8 = (bf16[512,512]{1,0:T(8,128)(2,1)S(1)}, bf16[512,512]{1,0:T(8,128)(2,1)S(1)}, u32[]{:S(2)}, u32[]{:S(2)}) collective-permute-start(bf16[512,512]{1,0:T(8,128)(2,1)S(1)} %collective-permute-done.refs_2_), channel_id=1, source_target_pairs={{0,3},{1,0},{2,1},{3,2},{4,7},{5,4},{6,5},{7,6},{8,11},{9,8},{10,9... | collective-permute-start | bytes 1572872 | tf_op jit(solution)/shard_map/ppermute | solution.py:36
  38.4 6.2 %collective-permute-done.5.refs_7_.refs_3_ = bf16[512,512]{1,0:T(8,128)(2,1)S(1)} collective-permute-done((bf16[512,512]{1,0:T(8,128)(2,1)S(1)}, bf16[512,512]{1,0:T(8,128)(2,1)S(1)}, u32[]{:S(2)}, u32[]{:S(2)}) %collective-permute-start.5) | collective-permute-done | bytes 524320 | tf_op jit(solution)/shard_map/ppermute | solution.py:32
  45.0 1.0 collective-permute-done.4.refs_5_.refs_2_
  46.0 2.8 %collective-permute-start.11 = (bf16[512,512]{1,0:T(8,128)(2,1)S(1)}, bf16[512,512]{1,0:T(8,128)(2,1)S(1)}, u32[]{:S(2)}, u32[]{:S(2)}) collective-permute-start(bf16[512,512]{1,0:T(8,128)(2,1)S(1)} %collective-permute-done.3.refs_3_.refs_1_), channel_id=1, source_target_pairs={{0,3},{1,0},{2,1},{3,2},{4,7},{5,4},{6,5},{7,6},{8,11},{9,8},{10,9... | collective-permute-start | bytes 1572872 | tf_op jit(solution)/shard_map/ppermute | solution.py:36
  49.6 7.7 %collective-permute-done.7.refs_10_ = bf16[512,512]{1,0:T(8,128)(2,1)S(1)} collective-permute-done((bf16[512,512]{1,0:T(8,128)(2,1)S(1)}, bf16[512,512]{1,0:T(8,128)(2,1)S(1)}, u32[]{:S(2)}, u32[]{:S(2)}) %collective-permute-start.7) | collective-permute-done | bytes 524320 | tf_op jit(solution)/shard_map/ppermute | solution.py:40
  58.1 1.3 copy.17
  59.4 8.9 %shard_map.91.h_ref = f32[8,256,256]{2,1,0:T(8,128)} custom-call(f32[8,128,256]{2,1,0:T(8,128)} %bitcast.32, bf16[2,256,128]{2,1,0:T(8,128)(2,1)} %constant.72.clone.first_ref, bf16[2,256,512]{2,1,0:T(8,128)(2,1)} %constant.73.clone.turn_ref, f32[2,128,256]{2,1,0:T(8,128)} %constant.75.clone.twiddle_ref), custom_call_target="tpu_custom_call" | custom-call | flops 2013265920 | bytes 5242880 | tf_op jit(solution)/shard_map/pallas_call | solution.py:310
  70.9 2.0 %collective-permute-start.15 = (bf16[8,512,384]{2,1,0:T(8,128)(2,1)}, bf16[8,512,384]{2,1,0:T(8,128)(2,1)S(1)}, u32[]{:S(2)}, u32[]{:S(2)}) collective-permute-start(bf16[8,512,384]{2,1,0:T(8,128)(2,1)} %bitcast.24), channel_id=1, source_target_pairs={{0,8},{8,0},{16,24},{24,16},{32,40},{40,32},{48,56},{56,48},{64,72... | collective-permute-start | bytes 9437192 | tf_op jit(solution)/shard_map/ppermute | solution.py:411
  73.6 1.3 collective-permute-start.14
  75.6 1.0 collective-permute-start.12
  78.3 9.1 %shard_map.92 = (f32[1024,384]{1,0:T(8,128)}, bf16[16,256]{1,0:T(8,128)(2,1)}) custom-call(s32[8]{0:T(128)} %stack.35.places, bf16[512,512]{1,0:T(8,128)(2,1)} %copy-done.3, bf16[512,512]{1,0:T(8,128)(2,1)} %copy-done.1, bf16[512,512]{1,0:T(8,128)(2,1)} %copy-done.10, bf16[512,512]{1,0:T(8,128)(2,1)} %copy-done.5, bf16[512,512]{1,0:T(8,128)(2,1)} %copy-done.9, ...), custom_call_target="tpu_custom_call" | custom-call | flops 2818572288 | bytes 11534336 | tf_op jit(solution)/shard_map/pallas_call | solution.py:94
  87.5 1.7 copy-done
  89.1 3.0 %shard_map.93 = bf16[16,256]{1,0:T(8,128)(2,1)} custom-call(s32[8]{0:T(128)} %stack.35.places, bf16[512,512]{1,0:T(8,128)(2,1)} %copy-done.1, bf16[512,512]{1,0:T(8,128)(2,1)} %copy-done.5, bf16[512,512]{1,0:T(8,128)(2,1)} %copy-done.4, bf16[512,512]{1,0:T(8,128)(2,1)} %copy-done.2, bf16[512,512]{1,0:T(8,128)(2,1)} %copy-done.7, ...), custom_call_target="tpu_custom_call" | custom-call | flops 536870912 | bytes 4194304 | tf_op jit(solution)/shard_map/pallas_call | solution.py:122
  92.8 5.4 %collective-permute-start.16 = (bf16[16,512]{1,0:T(8,128)(2,1)S(1)}, bf16[16,512]{1,0:T(8,128)(2,1)S(1)}, u32[]{:S(2)}, u32[]{:S(2)}) collective-permute-start(bf16[16,512]{1,0:T(8,128)(2,1)S(1)} %pad_maximum_fusion.1), channel_id=1, source_target_pairs={{0,8},{8,16},{16,24},{24,32},{32,40},{40,48},{48,56},{56,64},{64,7... | collective-permute-start | bytes 49160 | tf_op jit(solution)/shard_map/ppermute | solution.py:375
  99.8 9.8 %shard_map.94 = bf16[32,8,1024]{2,1,0:T(8,128)(2,1)} custom-call(s32[8]{0:T(128)} %stack.35.places, bf16[512,512]{1,0:T(8,128)(2,1)} %copy-done.3, bf16[512,512]{1,0:T(8,128)(2,1)} %copy-done.1, bf16[512,512]{1,0:T(8,128)(2,1)} %copy-done.10, bf16[512,512]{1,0:T(8,128)(2,1)} %copy-done.5, bf16[512,512]{1,0:T(8,128)(2,1)} %copy-done.9, ...), custom_call_target="tpu_custom_call" | custom-call | flops 2415919104 | bytes 13631488 | tf_op jit(solution)/shard_map/pallas_call | solution.py:183
  109.7 12.1 %all-to-all-start = ((bf16[32,8,1024]{2,1,0:T(8,128)(2,1)}), bf16[32,8,1024]{2,1,0:T(8,128)(2,1)S(1)}, u32[]{:S(2)}, u32[]{:S(2)}) async-start(bf16[32,8,1024]{2,1,0:T(8,128)(2,1)} %shard_map.94), calls=%async_computation | async-start | bytes 1048576 | tf_op jit(solution)/shard_map/all_to_all | solution.py:419
  122.5 16.3 %all-to-all-done.x_ref = bf16[32,8,1024]{2,1,0:T(8,128)(2,1)S(1)} async-done(((bf16[32,8,1024]{2,1,0:T(8,128)(2,1)}), bf16[32,8,1024]{2,1,0:T(8,128)(2,1)S(1)}, u32[]{:S(2)}, u32[]{:S(2)}) %all-to-all-start) | async-done | bytes 524320 | tf_op jit(solution)/shard_map/all_to_all | solution.py:419
  138.8 0.8 copy-done.19
  139.6 8.8 %shard_map.95 = bf16[32,8,1024]{2,1,0:T(8,128)(2,1)} custom-call(bf16[32,8,1024]{2,1,0:T(8,128)(2,1)} %copy-done.19, f32[8,256,256]{2,1,0:T(8,128)} %shard_map.91.h_ref, f32[8,1]{1,0:T(8,128)} %copy.13.gain_ref, bf16[256,896]{1,0:T(8,128)(2,1)} %constant.74.clone.table_ref, f32[2,128,256]{2,1,0:T(8,128)} %constant.75.clone.twiddle_ref), custom_call_target="tpu_custom_call" | custom-call | flops 1342177280 | bytes 5242880 | tf_op jit(solution)/shard_map/pallas_call | solution.py:343
  148.4 5.7 %all-to-all-start.1 = ((bf16[32,8,1024]{2,1,0:T(8,128)(2,1)}), bf16[32,8,1024]{2,1,0:T(8,128)(2,1)S(1)}, u32[]{:S(2)}, u32[]{:S(2)}) async-start(bf16[32,8,1024]{2,1,0:T(8,128)(2,1)} %shard_map.95), calls=%async_computation.1 | async-start | bytes 1048576 | tf_op jit(solution)/shard_map/all_to_all | solution.py:421
  154.1 8.3 %shard_map.96.query_ref = bf16[1024,256]{1,0:T(8,128)(2,1)} custom-call(s32[8]{0:T(128)} %stack.35.places, s32[1]{0:T(128)} %bitcast.15.even, bf16[512,512]{1,0:T(8,128)(2,1)} %copy-done.3, bf16[512,512]{1,0:T(8,128)(2,1)} %copy-done.1, bf16[512,512]{1,0:T(8,128)(2,1)} %copy-done.10, bf16[512,512]{1,0:T(8,128)(2,1)} %copy-done.5, ...), custom_call_target="tpu_custom_call" | custom-call | flops 1207959552 | bytes 16777216 | tf_op jit(solution)/shard_map/pallas_call | solution.py:226
  163.1 5.0 %collective-permute-start.17 = (bf16[16,256]{1,0:T(8,128)(2,1)S(1)}, bf16[16,256]{1,0:T(8,128)(2,1)S(1)}, u32[]{:S(2)}, u32[]{:S(2)}) collective-permute-start(bf16[16,256]{1,0:T(8,128)(2,1)S(1)} %slice.51), channel_id=1, source_target_pairs={{0,8},{8,16},{16,24},{24,32},{32,40},{40,48},{48,56},{56,64},{64,7... | collective-permute-start | bytes 24584 | tf_op jit(solution)/shard_map/ppermute | solution.py:375
  169.5 2.4 %shard_map.97.gate_ref = bf16[1024,256]{1,0:T(8,128)(2,1)} custom-call(bf16[1024,256]{1,0:T(8,128)(2,1)} %shard_map.96.query_ref, bf16[16,256]{1,0:T(8,128)(2,1)} %copy-done.23, f32[3,256]{1,0:T(4,128)} %slice_bitcast_fusion.taps_ref), custom_call_target="tpu_custom_call" | custom-call | flops 1572864 | bytes 1048576 | tf_op jit(solution)/shard_map/pallas_call | solution.py:250
  171.9 0.8 copy-done.14
  172.7 2.2 %shard_map.98 = bf16[1024,256]{1,0:T(8,128)(2,1)} custom-call(bf16[32,8,1024]{2,1,0:T(8,128)(2,1)} %copy-done.14, bf16[1024,256]{1,0:T(8,128)(2,1)} %shard_map.97.gate_ref), custom_call_target="tpu_custom_call" | custom-call | flops 262144 | bytes 2097152 | tf_op jit(solution)/shard_map/pallas_call | solution.py:364
  (86 shorter events, 13.5 us)
Async XLA Ops:
  6.5 13.1 %copy-start.17 = (bf16[1024,512]{1,0:T(8,128)(2,1)S(1)}, bf16[1024,512]{1,0:T(8,128)(2,1)}, u32[]{:S(2)}) copy-start(bf16[1024,512]{1,0:T(8,128)(2,1)} %param.9) | copy-start | bytes 3145732
  6.5 51.5 %copy-start.18 = (f32[8,32768]{1,0:T(8,128)S(1)}, f32[8,32768]{1,0:T(8,128)}, u32[]{:S(2)}) copy-start(f32[8,32768]{1,0:T(8,128)} %param.12) | copy-start | bytes 3145732
  6.5 64.3 %all-gather.4.cloned.1.call-start = ((), (), s32[]{:S(2)}) async-start(), calls=%async_computation.2 | async-start | bytes 3538944 | tf_op jit(solution)/shard_map/all_gather | solution.py:386
  19.7 13.5 %copy-start.1 = (bf16[512,512]{1,0:T(8,128)(2,1)}, bf16[512,512]{1,0:T(8,128)(2,1)S(1)}, u32[]{:S(2)}) copy-start(bf16[512,512]{1,0:T(8,128)(2,1)S(1)} %get-tuple-element.49.refs_1_.refs_0_) | copy-start | bytes 1572868
  19.7 29.9 %copy-start.3 = (bf16[512,512]{1,0:T(8,128)(2,1)}, bf16[512,512]{1,0:T(8,128)(2,1)S(1)}, u32[]{:S(2)}) copy-start(bf16[512,512]{1,0:T(8,128)(2,1)S(1)} %get-tuple-element.50.refs_0_) | copy-start | bytes 1572868
  19.7 13.5 %collective-permute-start.2 = (bf16[512,512]{1,0:T(8,128)(2,1)S(1)}, bf16[512,512]{1,0:T(8,128)(2,1)S(1)}, u32[]{:S(2)}, u32[]{:S(2)}) collective-permute-start(bf16[512,512]{1,0:T(8,128)(2,1)S(1)} %get-tuple-element.50.refs_0_), channel_id=1, source_target_pairs={{0,4},{1,5},{2,6},{3,7},{4,0},{5,1},{6,2},{7,3},{8,12},{9,13},{10,... | collective-permute-start | bytes 1572872 | tf_op jit(solution)/shard_map/ppermute | solution.py:32
  20.3 15.3 %collective-permute-start.1 = (bf16[512,512]{1,0:T(8,128)(2,1)S(1)}, bf16[512,512]{1,0:T(8,128)(2,1)S(1)}, u32[]{:S(2)}, u32[]{:S(2)}) collective-permute-start(bf16[512,512]{1,0:T(8,128)(2,1)S(1)} %get-tuple-element.50.refs_0_), channel_id=1, source_target_pairs={{0,1},{1,2},{2,3},{3,0},{4,5},{5,6},{6,7},{7,4},{8,9},{9,10},{10,1... | collective-permute-start | bytes 1572872 | tf_op jit(solution)/shard_map/ppermute | solution.py:40
  21.6 14.0 %collective-permute-start = (bf16[512,512]{1,0:T(8,128)(2,1)S(1)}, bf16[512,512]{1,0:T(8,128)(2,1)S(1)}, u32[]{:S(2)}, u32[]{:S(2)}) collective-permute-start(bf16[512,512]{1,0:T(8,128)(2,1)S(1)} %get-tuple-element.50.refs_0_), channel_id=1, source_target_pairs={{0,3},{1,0},{2,1},{3,2},{4,7},{5,4},{6,5},{7,6},{8,11},{9,8},{10,9... | collective-permute-start | bytes 1572872 | tf_op jit(solution)/shard_map/ppermute | solution.py:36
  23.0 21.5 %collective-permute-start.5 = (bf16[512,512]{1,0:T(8,128)(2,1)S(1)}, bf16[512,512]{1,0:T(8,128)(2,1)S(1)}, u32[]{:S(2)}, u32[]{:S(2)}) collective-permute-start(bf16[512,512]{1,0:T(8,128)(2,1)S(1)} %get-tuple-element.49.refs_1_.refs_0_), channel_id=1, source_target_pairs={{0,4},{1,5},{2,6},{3,7},{4,0},{5,1},{6,2},{7,3},{8,12},{9,13},{10,... | collective-permute-start | bytes 1572872 | tf_op jit(solution)/shard_map/ppermute | solution.py:32
  24.0 22.0 %collective-permute-start.4 = (bf16[512,512]{1,0:T(8,128)(2,1)S(1)}, bf16[512,512]{1,0:T(8,128)(2,1)S(1)}, u32[]{:S(2)}, u32[]{:S(2)}) collective-permute-start(bf16[512,512]{1,0:T(8,128)(2,1)S(1)} %get-tuple-element.49.refs_1_.refs_0_), channel_id=1, source_target_pairs={{0,1},{1,2},{2,3},{3,0},{4,5},{5,6},{6,7},{7,4},{8,9},{9,10},{10,1... | collective-permute-start | bytes 1572872 | tf_op jit(solution)/shard_map/ppermute | solution.py:40
  33.2 24.1 %copy-start.8 = (bf16[512,512]{1,0:T(8,128)(2,1)}, bf16[512,512]{1,0:T(8,128)(2,1)S(1)}, u32[]{:S(2)}) copy-start(bf16[512,512]{1,0:T(8,128)(2,1)S(1)} %collective-permute-done.2.refs_6_) | copy-start | bytes 1572868
  33.2 12.8 %collective-permute-start.3 = (bf16[512,512]{1,0:T(8,128)(2,1)S(1)}, bf16[512,512]{1,0:T(8,128)(2,1)S(1)}, u32[]{:S(2)}, u32[]{:S(2)}) collective-permute-start(bf16[512,512]{1,0:T(8,128)(2,1)S(1)} %get-tuple-element.49.refs_1_.refs_0_), channel_id=1, source_target_pairs={{0,3},{1,0},{2,1},{3,2},{4,7},{5,4},{6,5},{7,6},{8,11},{9,8},{10,9... | collective-permute-start | bytes 1572872 | tf_op jit(solution)/shard_map/ppermute | solution.py:36
  35.6 21.7 %copy-start.9 = (bf16[512,512]{1,0:T(8,128)(2,1)}, bf16[512,512]{1,0:T(8,128)(2,1)S(1)}, u32[]{:S(2)}) copy-start(bf16[512,512]{1,0:T(8,128)(2,1)S(1)} %collective-permute-done.1.refs_4_) | copy-start | bytes 1572868
  35.6 32.9 %copy-start.10 = (bf16[512,512]{1,0:T(8,128)(2,1)}, bf16[512,512]{1,0:T(8,128)(2,1)S(1)}, u32[]{:S(2)}) copy-start(bf16[512,512]{1,0:T(8,128)(2,1)S(1)} %collective-permute-done.refs_2_) | copy-start | bytes 1572868
  35.6 21.6 %collective-permute-start.7 = (bf16[512,512]{1,0:T(8,128)(2,1)S(1)}, bf16[512,512]{1,0:T(8,128)(2,1)S(1)}, u32[]{:S(2)}, u32[]{:S(2)}) collective-permute-start(bf16[512,512]{1,0:T(8,128)(2,1)S(1)} %collective-permute-done.2.refs_6_), channel_id=1, source_target_pairs={{0,1},{1,2},{2,3},{3,0},{4,5},{5,6},{6,7},{7,4},{8,9},{9,10},{10,1... | collective-permute-start | bytes 1572872 | tf_op jit(solution)/shard_map/ppermute | solution.py:40
  35.7 32.6 %collective-permute-start.8 = (bf16[512,512]{1,0:T(8,128)(2,1)S(1)}, bf16[512,512]{1,0:T(8,128)(2,1)S(1)}, u32[]{:S(2)}, u32[]{:S(2)}) collective-permute-start(bf16[512,512]{1,0:T(8,128)(2,1)S(1)} %collective-permute-done.refs_2_), channel_id=1, source_target_pairs={{0,3},{1,0},{2,1},{3,2},{4,7},{5,4},{6,5},{7,6},{8,11},{9,8},{10,9... | collective-permute-start | bytes 1572872 | tf_op jit(solution)/shard_map/ppermute | solution.py:36
  44.5 23.8 %copy-start.2 = (bf16[512,512]{1,0:T(8,128)(2,1)}, bf16[512,512]{1,0:T(8,128)(2,1)S(1)}, u32[]{:S(2)}) copy-start(bf16[512,512]{1,0:T(8,128)(2,1)S(1)} %collective-permute-done.5.refs_7_.refs_3_) | copy-start | bytes 1572868
  44.5 23.8 %collective-permute-start.6 = (bf16[512,512]{1,0:T(8,128)(2,1)S(1)}, bf16[512,512]{1,0:T(8,128)(2,1)S(1)}, u32[]{:S(2)}, u32[]{:S(2)}) collective-permute-start(bf16[512,512]{1,0:T(8,128)(2,1)S(1)} %collective-permute-done.refs_2_), channel_id=1, source_target_pairs={{0,4},{1,5},{2,6},{3,7},{4,0},{5,1},{6,2},{7,3},{8,12},{9,13},{10,... | collective-permute-start | bytes 1572872 | tf_op jit(solution)/shard_map/ppermute | solution.py:32
  46.0 22.3 %copy-start.5 = (bf16[512,512]{1,0:T(8,128)(2,1)}, bf16[512,512]{1,0:T(8,128)(2,1)S(1)}, u32[]{:S(2)}) copy-start(bf16[512,512]{1,0:T(8,128)(2,1)S(1)} %collective-permute-done.3.refs_3_.refs_1_) | copy-start | bytes 1572868
  46.0 22.3 %collective-permute-start.11 = (bf16[512,512]{1,0:T(8,128)(2,1)S(1)}, bf16[512,512]{1,0:T(8,128)(2,1)S(1)}, u32[]{:S(2)}, u32[]{:S(2)}) collective-permute-start(bf16[512,512]{1,0:T(8,128)(2,1)S(1)} %collective-permute-done.3.refs_3_.refs_1_), channel_id=1, source_target_pairs={{0,3},{1,0},{2,1},{3,2},{4,7},{5,4},{6,5},{7,6},{8,11},{9,8},{10,9... | collective-permute-start | bytes 1572872 | tf_op jit(solution)/shard_map/ppermute | solution.py:36
  48.8 19.7 %collective-permute-start.9 = (bf16[512,512]{1,0:T(8,128)(2,1)S(1)}, bf16[512,512]{1,0:T(8,128)(2,1)S(1)}, u32[]{:S(2)}, u32[]{:S(2)}) collective-permute-start(bf16[512,512]{1,0:T(8,128)(2,1)S(1)} %collective-permute-done.3.refs_3_.refs_1_), channel_id=1, source_target_pairs={{0,4},{1,5},{2,6},{3,7},{4,0},{5,1},{6,2},{7,3},{8,12},{9,13},{10,... | collective-permute-start | bytes 1572872 | tf_op jit(solution)/shard_map/ppermute | solution.py:32
  57.2 13.6 %collective-permute-start.10 = (bf16[512,512]{1,0:T(8,128)(2,1)S(1)}, bf16[512,512]{1,0:T(8,128)(2,1)}, u32[]{:S(2)}, u32[]{:S(2)}) collective-permute-start(bf16[512,512]{1,0:T(8,128)(2,1)S(1)} %collective-permute-done.5.refs_7_.refs_3_), channel_id=1, source_target_pairs={{0,1},{1,2},{2,3},{3,0},{4,5},{5,6},{6,7},{7,4},{8,9},{9,10},{10,1... | collective-permute-start | bytes 1572872 | tf_op jit(solution)/shard_map/ppermute | solution.py:40
  59.4 15.5 %copy-start.22 = (f32[3,3,256]{2,1,0:T(4,128)S(1)}, f32[3,3,256]{2,1,0:T(4,128)}, u32[]{:S(2)}) copy-start(f32[3,3,256]{2,1,0:T(4,128)} %param.11) | copy-start | bytes 27652
  70.9 16.6 %collective-permute-start.15 = (bf16[8,512,384]{2,1,0:T(8,128)(2,1)}, bf16[8,512,384]{2,1,0:T(8,128)(2,1)S(1)}, u32[]{:S(2)}, u32[]{:S(2)}) collective-permute-start(bf16[8,512,384]{2,1,0:T(8,128)(2,1)} %bitcast.24), channel_id=1, source_target_pairs={{0,8},{8,0},{16,24},{24,16},{32,40},{40,32},{48,56},{56,48},{64,72... | collective-permute-start | bytes 9437192 | tf_op jit(solution)/shard_map/ppermute | solution.py:411
  73.6 4.1 %collective-permute-start.14 = (bf16[16,512]{1,0:T(8,128)(2,1)S(1)}, bf16[16,512]{1,0:T(8,128)(2,1)S(1)}, u32[]{:S(2)}, u32[]{:S(2)}) collective-permute-start(bf16[16,512]{1,0:T(8,128)(2,1)S(1)} %slice.41), channel_id=1, source_target_pairs={{0,2},{1,3},{2,0},{3,1},{4,6},{5,7},{6,4},{7,5},{8,10},{9,11},{10,... | collective-permute-start | bytes 49160 | tf_op jit(solution)/shard_map/ppermute | solution.py:392
  75.6 23.2 %collective-permute-start.12 = (bf16[512,512]{1,0:T(8,128)(2,1)}, bf16[512,512]{1,0:T(8,128)(2,1)S(1)}, u32[]{:S(2)}, u32[]{:S(2)}) collective-permute-start(bf16[512,512]{1,0:T(8,128)(2,1)} %copy-done.13), channel_id=1, source_target_pairs={{0,3},{1,0},{2,1},{3,2},{4,7},{5,4},{6,5},{7,6},{8,11},{9,8},{10,9... | collective-permute-start | bytes 1572872 | tf_op jit(solution)/shard_map/ppermute | solution.py:36
  76.6 22.2 %collective-permute-start.13 = (bf16[512,512]{1,0:T(8,128)(2,1)}, bf16[512,512]{1,0:T(8,128)(2,1)S(1)}, u32[]{:S(2)}, u32[]{:S(2)}) collective-permute-start(bf16[512,512]{1,0:T(8,128)(2,1)} %collective-permute-done.10.refs_11_.refs_5_), channel_id=1, source_target_pairs={{0,1},{1,2},{2,3},{3,0},{4,5},{5,6},{6,7},{7,4},{8,9},{9,10},{10,1... | collective-permute-start | bytes 1572872 | tf_op jit(solution)/shard_map/ppermute | solution.py:40
  92.8 6.2 %collective-permute-start.16 = (bf16[16,512]{1,0:T(8,128)(2,1)S(1)}, bf16[16,512]{1,0:T(8,128)(2,1)S(1)}, u32[]{:S(2)}, u32[]{:S(2)}) collective-permute-start(bf16[16,512]{1,0:T(8,128)(2,1)S(1)} %pad_maximum_fusion.1), channel_id=1, source_target_pairs={{0,8},{8,16},{16,24},{24,32},{32,40},{40,48},{48,56},{56,64},{64,7... | collective-permute-start | bytes 49160 | tf_op jit(solution)/shard_map/ppermute | solution.py:375
  99.8 22.0 %copy-start.25 = (f32[8]{0:T(128)S(1)}, f32[8]{0:T(128)}, u32[]{:S(2)}) copy-start(f32[8]{0:T(128)} %param.13) | copy-start | bytes 100
  109.7 29.1 %all-to-all-start = ((bf16[32,8,1024]{2,1,0:T(8,128)(2,1)}), bf16[32,8,1024]{2,1,0:T(8,128)(2,1)S(1)}, u32[]{:S(2)}, u32[]{:S(2)}) async-start(bf16[32,8,1024]{2,1,0:T(8,128)(2,1)} %shard_map.94), calls=%async_computation | async-start | bytes 1048576 | tf_op jit(solution)/shard_map/all_to_all | solution.py:419
  148.4 23.4 %all-to-all-start.1 = ((bf16[32,8,1024]{2,1,0:T(8,128)(2,1)}), bf16[32,8,1024]{2,1,0:T(8,128)(2,1)S(1)}, u32[]{:S(2)}, u32[]{:S(2)}) async-start(bf16[32,8,1024]{2,1,0:T(8,128)(2,1)} %shard_map.95), calls=%async_computation.1 | async-start | bytes 1048576 | tf_op jit(solution)/shard_map/all_to_all | solution.py:421
  163.1 5.8 %collective-permute-start.17 = (bf16[16,256]{1,0:T(8,128)(2,1)S(1)}, bf16[16,256]{1,0:T(8,128)(2,1)S(1)}, u32[]{:S(2)}, u32[]{:S(2)}) collective-permute-start(bf16[16,256]{1,0:T(8,128)(2,1)S(1)} %slice.51), channel_id=1, source_target_pairs={{0,8},{8,16},{16,24},{24,32},{32,40},{40,48},{48,56},{56,64},{64,7... | collective-permute-start | bytes 24584 | tf_op jit(solution)/shard_map/ppermute | solution.py:375
  (15 other events, 27.4 us)
Sparse Core Ops, SparseCore 0:
  19.7 46.4 all-gather.3

commit v2 on v1

v2 whole, which is shorter than its diff:
```python
import functools

import jax
import jax.numpy as jnp
import numpy as np
from jax import lax
from jax.experimental import pallas as pl
from jax.experimental.pallas import tpu as pltpu
from jax.sharding import PartitionSpec as P

F32 = jnp.float32
BF16 = jnp.bfloat16
MIB = 1 << 20
VMEM = 56 * MIB

FROM_ABOVE = [(i, (i - 4) % 32) for i in range(32)]
FROM_BELOW = [(i, (i + 4) % 32) for i in range(32)]
OTHER_CORE = [(i, i ^ 1) for i in range(32)]
OTHER_XHI = [(i, i ^ 2) for i in range(32)]
OTHER_XLO = [(i, i ^ 4) for i in range(8)]
FROM_UP = [(i, (i & 4) | ((i - 1) & 3)) for i in range(8)]
FROM_DOWN = [(i, (i & 4) | ((i + 1) & 3)) for i in range(8)]
ROWS = 1024
HALF = 512
FOUR_GROUPS = [[z * 4 + r for r in range(4)] for z in range(8)]
HALO = 16
AHEAD = 8
KV = pl.ds(0, 256)
QUERY = pl.ds(256, 128)
OUTER = 128
INNER = 256


def other_xlo(x):
    return lax.ppermute(x, "tp", OTHER_XLO)


def from_up(x):
    return lax.ppermute(x, "tp", FROM_UP)


def from_down(x):
    return lax.ppermute(x, "tp", FROM_DOWN)


def from_above(x):
    return lax.ppermute(x, "ctx", FROM_ABOVE)


def from_below(x):
    return lax.ppermute(x, "ctx", FROM_BELOW)


def tied(*xs):
    return lax.optimization_barrier(xs)


def dot(a, b):
    return jnp.dot(a, b, preferred_element_type=F32)


def vmem_specs(count):
    return [pl.BlockSpec(memory_space=pltpu.VMEM)] * count


def unit_copies(places, u, units, weights, a_buf, b_buf, w_bufs, sems):
    unit = units[u]
    if len(unit) == 1:
        a, b = unit[0].at[pl.ds(0, HALF)], unit[0].at[pl.ds(HALF, HALF + HALO)]
    else:
        a, b = unit
    pairs = [(a, a_buf.at[u]), (b, b_buf.at[u])]
    pairs += [(w.at[places[u], :, cols], buf.at[u]) for (w, cols), buf in zip(weights, w_bufs)]
    return [pltpu.make_async_copy(*pair, sems.at[u, n]) for n, pair in enumerate(pairs)]


def grouped(refs, sizes):
    refs = list(refs)
    return [[refs.pop(0) for _ in range(size)] for size in sizes], refs


def flat(units):
    return [array for unit in units for array in unit]


def add_products(total, first, a, b, w):
    low = dot(a, w)
    high = dot(b, w)
    for rows, value in (
        (slice(HALO, HALO + HALF), low),
        (slice(HALO + HALF, HALO + ROWS), high[:HALF]),
        (slice(0, HALO), high[HALF:]),
    ):
        total[rows, :] = value if first else total[rows, :] + value


def sum_units(places, count, units, weights, joined, total, a_buf, b_buf, w_bufs, sems, others=()):
    copies = [
        unit_copies(places, u, units, weights, a_buf, b_buf, w_bufs, sems) for u in range(count)
    ]
    for u in range(min(AHEAD, count)):
        for copy in copies[u]:
            copy.start()
    for copy in others:
        copy.start()
    for u in range(count):
        if u + AHEAD < count:
            for copy in copies[u + AHEAD]:
                copy.start()
        for copy in copies[u]:
            copy.wait()
        add_products(total, u == 0, a_buf[u], b_buf[u], joined([buf[u] for buf in w_bufs]))


def unit_scratch(count, widths):
    return [
        pltpu.VMEM((count, HALF, 512), BF16),
        pltpu.VMEM((count, HALF + HALO, 512), BF16),
        *[pltpu.VMEM((count, 512, width), BF16) for width in widths],
        pltpu.SemaphoreType.DMA((count, 2 + len(widths))),
    ]


ANY = pl.BlockSpec(memory_space=pl.ANY)
SMEM = pl.BlockSpec(memory_space=pltpu.SMEM)


def partial_kernel(sizes, places, *refs):
    units, (w_ref, out_ref, a_buf, b_buf, w_buf, sems) = grouped(refs, sizes)
    sum_units(places, 7, units, [(w_ref, KV)], lambda w: w[0], out_ref, a_buf, b_buf, [w_buf], sems)


def partial_products(places, units, w):
    return pl.pallas_call(
        functools.partial(partial_kernel, [len(unit) for unit in units]),
        out_shape=jax.ShapeDtypeStruct((HALO + ROWS, 256), F32),
        in_specs=[SMEM] + [ANY] * (len(flat(units)) + 1),
        out_specs=pl.BlockSpec(memory_space=pltpu.VMEM),
        scratch_shapes=unit_scratch(7, [256]),
        compiler_params=pltpu.CompilerParams(vmem_limit_bytes=VMEM),
        cost_estimate=pl.CostEstimate(
            flops=2 * 7 * 1024 * 512 * 256, bytes_accessed=11 * MIB, transcendentals=0
        ),
    )(places, *flat(units), w)


def filtered(branch, taps, start, size):
    total = taps[0:1, :] * branch[pl.ds(HALO + start, size), :]
    for lag in (1, 2):
        total = total + taps[lag : lag + 1, :] * branch[pl.ds(HALO + start - lag, size), :]
    return total


def rounded(branch):
    branch[...] = branch[...].astype(BF16).astype(F32)


def gated_kernel(sizes, places, *refs):
    units, refs = grouped(refs, sizes)
    acc_ref, own_ref, sib_ref, taps_ref, out_ref, a_buf, b_buf, w_buf, sems = refs[:9]
    own_buf, own_sems, mine, theirs = refs[9:]
    copies = [
        pltpu.make_async_copy(acc_ref, mine, own_sems.at[0]),
        pltpu.make_async_copy(own_ref.at[places[7], :, KV], own_buf, own_sems.at[1]),
    ]
    sum_units(places, 8, units, [(sib_ref, KV)], lambda w: w[0], theirs, a_buf, b_buf, [w_buf], sems, copies)
    for copy in copies:
        copy.wait()
    add_products(mine, False, a_buf[7], b_buf[7], own_buf[...])
    rounded(mine)
    rounded(theirs)
    for r in range(ROWS // 256):
        a = filtered(mine, taps_ref[0], r * 256, 256)
        b = filtered(theirs, taps_ref[1], r * 256, 256)
        out_ref[:, :, r * 256 : r * 256 + 256] = (a * b).T.reshape(32, 8, 256).astype(BF16)


def gated_input(places, units, acc, own, sib, taps):
    return pl.pallas_call(
        functools.partial(gated_kernel, [len(unit) for unit in units]),
        out_shape=jax.ShapeDtypeStruct((32, 8, ROWS), BF16),
        in_specs=[SMEM] + [ANY] * (len(flat(units)) + 3) + vmem_specs(1),
        out_specs=pl.BlockSpec(memory_space=pltpu.VMEM),
        scratch_shapes=unit_scratch(8, [256])
        + [
            pltpu.VMEM((512, 256), BF16),
            pltpu.SemaphoreType.DMA((2,)),
            pltpu.VMEM((HALO + ROWS, 256), F32),
            pltpu.VMEM((HALO + ROWS, 256), F32),
        ],
        compiler_params=pltpu.CompilerParams(vmem_limit_bytes=VMEM),
        cost_estimate=pl.CostEstimate(
            flops=2 * 9 * 1024 * 512 * 256, bytes_accessed=13 * MIB, transcendentals=0
        ),
    )(places, *flat(units), acc, own, sib, taps)


def query_kernel(sizes, places, even, *refs):
    units, refs = grouped(refs, sizes)
    own_ref, sib_ref, taps_ref, out_ref, a_buf, b_buf, own_buf, sib_buf, sems, total = refs
    first_core = even[0] == 1

    def joined(w):
        own, sib = w
        return jnp.concatenate([jnp.where(first_core, own, sib), jnp.where(first_core, sib, own)], 1)

    sum_units(places, 8, units, [(own_ref, QUERY), (sib_ref, QUERY)], joined, total, a_buf, b_buf, [own_buf, sib_buf], sems)
    rounded(total)
    for r in range(ROWS // 256):
        out_ref[r * 256 : r * 256 + 256, :] = filtered(total, taps_ref[...], r * 256, 256).astype(BF16)


def query_gate(places, even, units, own, sib, taps):
    return pl.pallas_call(
        functools.partial(query_kernel, [len(unit) for unit in units]),
        out_shape=jax.ShapeDtypeStruct((ROWS, 256), BF16),
        in_specs=[SMEM] * 2 + [ANY] * (len(flat(units)) + 2) + vmem_specs(1),
        out_specs=pl.BlockSpec(memory_space=pltpu.VMEM),
        scratch_shapes=unit_scratch(8, [128, 128]) + [pltpu.VMEM((HALO + ROWS, 256), F32)],
        compiler_params=pltpu.CompilerParams(vmem_limit_bytes=VMEM),
        cost_estimate=pl.CostEstimate(
            flops=2 * 8 * 1024 * 512 * 256, bytes_accessed=12 * MIB, transcendentals=0
        ),
    )(places, even, *flat(units), own, sib, taps)


def two_parts(table):
    high = table.astype(BF16)
    return np.stack([high, (table - high.astype(np.float64)).astype(BF16)])


def tables():
    a = np.arange(OUTER, dtype=np.float64)
    b = np.arange(INNER, dtype=np.float64)
    outer = 2 * np.pi / OUTER * np.outer(a + 0.25, a)
    first = np.concatenate([np.cos(outer), -np.sin(outer)], 0)
    order = (4 * np.arange(32)[None, :] + np.arange(4)[:, None]).reshape(-1)
    inner = 2 * np.pi / INNER * (np.outer(b, b) % INNER)
    turn = np.concatenate([np.cos(inner), np.sin(inner)], 1)
    twist = 2 * np.pi / (OUTER * INNER) * np.outer(a + 0.25, b)
    twiddle = np.stack([np.cos(twist), np.sin(twist)]).astype(np.float32)
    shuffled = first[:, order].astype(BF16)
    packed = np.concatenate([turn.astype(BF16), shuffled, np.concatenate([shuffled[:, :].T, np.zeros((128, 256), BF16)], 0)], 1)
    return two_parts(first), two_parts(turn), packed, twiddle


def split_value(x):
    high = x.astype(BF16)
    return high, (x - high.astype(F32)).astype(BF16)


def turned_forward(wave, c, s):
    real, imag = wave[:OUTER], wave[OUTER:]
    return jnp.concatenate([real * c + imag * s, imag * c - real * s], 0)


def joined_forward(r):
    return r[:OUTER, :INNER] + r[OUTER:, INNER:], r[OUTER:, :INNER] - r[:OUTER, INNER:]


def filter_kernel(h_ref, first_ref, turn_ref, twiddle_ref, out_ref, work):
    c, s = twiddle_ref[0], twiddle_ref[1]
    for ch in range(8):
        high, low = split_value(h_ref[ch])
        wave = dot(first_ref[0], high) + (dot(first_ref[1], high) + dot(first_ref[0], low))
        work[0, ch], work[1, ch] = split_value(turned_forward(wave, c, s))
    for ch in range(8):
        high, low = work[0, ch], work[1, ch]
        wave = dot(high, turn_ref[0]) + (dot(high, turn_ref[1]) + dot(low, turn_ref[0]))
        real, imag = joined_forward(wave)
        out_ref[ch, :OUTER] = real * (1.0 / (OUTER * INNER))
        out_ref[ch, OUTER:] = imag * (1.0 / (OUTER * INNER))


def filter_spectrum(h, first, turn, twiddle):
    return pl.pallas_call(
        filter_kernel,
        out_shape=jax.ShapeDtypeStruct((8, 2 * OUTER, INNER), F32),
        in_specs=vmem_specs(4),
        out_specs=pl.BlockSpec(memory_space=pltpu.VMEM),
        scratch_shapes=[pltpu.VMEM((2, 8, 2 * OUTER, INNER), BF16)],
        compiler_params=pltpu.CompilerParams(vmem_limit_bytes=VMEM),
        cost_estimate=pl.CostEstimate(
            flops=2 * 3 * 8 * (128 * 256 * 256 + 256 * 256 * 512), bytes_accessed=5 * MIB, transcendentals=0
        ),
    )(h, first, turn, twiddle)


def convolve_kernel(x_ref, h_ref, gain_ref, table_ref, twiddle_ref, out_ref, wide, result, work):
    c, s = twiddle_ref[0], twiddle_ref[1]
    turn, first, last = table_ref[:, :512], table_ref[:, 512:640], table_ref[:128, 640:]
    wide[...] = x_ref[...].astype(F32)
    for ch in range(8):
        row = wide[:, ch, :]
        x = jnp.concatenate([row[:, q * 256 : q * 256 + 256] for q in range(4)], 0).astype(BF16)
        work[ch] = turned_forward(dot(first, x), c, s).astype(BF16)
    for ch in range(8):
        xr, xi = joined_forward(dot(work[ch], turn))
        hr, hi = h_ref[ch, :OUTER], h_ref[ch, OUTER:]
        work[ch] = jnp.concatenate([xr * hr - xi * hi, xr * hi + xi * hr], 0).astype(BF16)
    for ch in range(8):
        r = dot(work[ch], turn)
        br = r[:OUTER, :INNER] - r[OUTER:, INNER:]
        bi = r[:OUTER, INNER:] + r[OUTER:, :INNER]
        work[ch] = jnp.concatenate([br * c - bi * s, bi * c + br * s], 0).astype(BF16)
    for ch in range(8):
        y = dot(last, work[ch])
        result[:, ch, :] = jnp.concatenate([y[q * 32 : q * 32 + 32] for q in range(4)], 1)
    out_ref[...] = (result[...] + gain_ref[...][None] * wide[...]).astype(BF16)


def convolve(x, h, gain, table, twiddle):
    return pl.pallas_call(
        convolve_kernel,
        out_shape=jax.ShapeDtypeStruct((32, 8, ROWS), BF16),
        in_specs=vmem_specs(5),
        out_specs=pl.BlockSpec(memory_space=pltpu.VMEM),
        scratch_shapes=[pltpu.VMEM((32, 8, ROWS), F32)] * 2
        + [pltpu.VMEM((8, 2 * OUTER, INNER), BF16)],
        compiler_params=pltpu.CompilerParams(vmem_limit_bytes=VMEM),
        cost_estimate=pl.CostEstimate(
            flops=2 * 8 * 2 * (128 * 256 * 256 + 256 * 256 * 512), bytes_accessed=5 * MIB, transcendentals=0
        ),
    )(x, h, gain, table, twiddle)


def finish_kernel(conv_ref, gate_ref, out_ref):
    conv = conv_ref[...].astype(F32).reshape(256, 256).T
    out_ref[...] = (conv * gate_ref[...].astype(F32)).astype(BF16)


def finish(conv, gate):
    return pl.pallas_call(
        finish_kernel,
        grid=(4,),
        out_shape=jax.ShapeDtypeStruct((ROWS, 256), BF16),
        in_specs=[
            pl.BlockSpec((32, 8, 256), lambda r: (0, 0, r)),
            pl.BlockSpec((256, 256), lambda r: (r, 0)),
        ],
        out_specs=pl.BlockSpec((256, 256), lambda r: (r, 0)),
        compiler_params=pltpu.CompilerParams(vmem_limit_bytes=8 * MIB),
        cost_estimate=pl.CostEstimate(flops=1024 * 256, bytes_accessed=2 * MIB, transcendentals=0),
    )(conv, gate)


def next_shard(x):
    return lax.ppermute(x, "ctx", [(i, i + 1) for i in range(31)])


def body(tokens, proj_weight, short_taps, long_filter, skip_gain):
    ctx, tp = lax.axis_index("ctx"), lax.axis_index("tp")
    even = ctx % 2 == 0
    first, turn, packed, twiddle = (jnp.asarray(t) for t in tables())

    q, k, v = (proj_weight[:, g] for g in range(3))
    left, right = q[:, :128], q[:, 128:]
    keep = jnp.concatenate([jnp.where(even, k, v), jnp.where(even, left, right)], 1)
    give = jnp.concatenate([jnp.where(even, v, k), jnp.where(even, right, left)], 1)
    got = lax.ppermute(give, "ctx", OTHER_CORE)
    block = jnp.concatenate([jnp.where(even, keep, got), jnp.where(even, got, keep)], 0)
    got = lax.ppermute(block, "ctx", OTHER_XHI)
    low = (ctx // 2) % 2 == 0
    block = jnp.concatenate([jnp.where(low, block, got), jnp.where(low, got, block)], 0)
    spectrum = filter_spectrum(long_filter.reshape(8, OUTER, INNER), first, turn, twiddle)

    halo = next_shard(tokens[ROWS - HALO :])
    a0 = jnp.concatenate([tokens, halo], 0)
    ap, am = from_up(a0), from_down(a0)
    b0 = other_xlo(tied(a0, block)[0])
    u1, d1 = from_above(block), from_below(block)
    w1, v1 = tied(u1, d1, ap, am)[:2]
    u2, d2 = from_above(w1), from_below(v1)
    a2 = from_up(ap)
    w2, v2 = tied(u2, d2, b0)[:2]
    bm, bp = from_down(b0), other_xlo(ap)
    u3, d3 = from_above(w2), from_below(v2)
    u4 = from_above(tied(u3, a2)[0])
    bm, bp, a2 = tied(bm, bp, a2)
    parts = (bp[:HALF], bm[HALF:])
    b2 = (from_up(parts[0]), from_down(parts[1]))
    u4, d3 = tied(u4, d3, a2, *parts)[:2]
    own = jnp.stack([block, u1, u2, u3, u4, d3, d2, d1])

    xlo, y = tp // 4, tp % 4
    mine, others = xlo * 4, (1 - xlo) * 4
    shift = lambda n: (y + n) % 4
    places = jnp.stack(
        [
            mine + y,
            mine + shift(1),
            mine + shift(3),
            others + y,
            others + shift(1),
            others + shift(3),
            mine + shift(2),
            others + shift(2),
        ]
    ).astype(jnp.int32)
    places = (places - ctx // 4) % 8
    sib = lax.ppermute(own, "ctx", OTHER_CORE)
    units = ((a0,), (ap,), (am,), (b0,), (bp,), (bm,), (a2,))
    own_acc = partial_products(places, units, own)
    taps = short_taps.transpose(1, 0, 2)
    taps_kv = jnp.where(even, taps[1:3], taps[2:0:-1])
    gated = gated_input(places, units + (b2,), own_acc, own, sib, taps_kv)

    owned = lax.all_to_all(gated, "ctx", 0, 0)
    convolved = convolve(owned, spectrum, skip_gain[:, None], packed, twiddle)
    returned = lax.all_to_all(convolved, "ctx", 0, 0)

    flag = even.astype(jnp.int32).reshape(1)
    gate = query_gate(places, flag, units + (b2,), own, sib, taps[0])
    return finish(returned, gate)


def solution(mesh):
    placed = (
        P("ctx", "tp"),
        P("ctx", None, "tp"),
        P(None, None, "tp"),
        P(("tp", "ctx"), None),
        P(("tp", "ctx")),
    )
    return jax.shard_map(
        body, mesh=mesh, in_specs=placed, out_specs=P("ctx", "tp"), check_vma=False
    )
```

time: 183 us -> 159 us (0.87)
  waiting for transfers between devices: 42.1 us -> 66.8 us
  Pallas kernels: 52.6 us -> 32.7 us
  between operations: 13.6 us -> 0.28 us
  blocking collectives: 12.1 us -> 0 us
    ppermute x5 -> x3, waiting for transfers between devices: 0.01 us -> 22.6 us  [from_up(): return lax.ppermute(x, 'tp', FROM_UP)]
    ppermute x1 -> x9, waiting for transfers between devices: 0.49 us -> 21.6 us  [the longest x4 16.4 us: from_above(): return lax.ppermute(x, 'ctx', FROM_ABOVE)]
    ppermute x4 -> x2, waiting for transfers between devices: 15.5 us -> 1.49 us  [other_xlo(): return lax.ppermute(x, 'tp', OTHER_XLO)]
    ppermute x1 -> x9, starting transfers between devices: 1.29 us -> 14.6 us  [the longest x4 9.54 us: from_above(): return lax.ppermute(x, 'ctx', FROM_ABOVE)]
    pallas_call x6 -> x4, Pallas kernels: 34.8 us -> 21.9 us  [the longest x1 7.79 us: gated_input(): pl.pallas_call(functools.partial(gated_kernel, [len(unit) for unit in uni...]
    all_gather x1 -> x0, blocking collectives: 12.1 us -> none  [body(): lax.all_gather(proj_weight.transpose(1, 0, 2), 'ctx', axis_index_groups=F...]
    all_to_all x1, waiting for transfers between devices: 0.01 us -> 9.94 us  [body(): returned = lax.all_to_all(convolved, 'ctx', 0, 0)]
    all_to_all x1, waiting for transfers between devices: 16.3 us -> 8.22 us  [body(): owned = lax.all_to_all(gated, 'ctx', 0, 0)]
  transfers between devices with their start and end apart: 21 -> 21, of which waited for: 10 -> 14; matrix products, arithmetic and copies ran while one was open for 3% -> 6% of each run, Pallas kernels for 17% -> 11%
where the time goes in v2:
time: 159 us; the launch traced here: 158 us
  waiting for transfers between devices  66.8 us (42%)
  starting transfers between devices  45 us (28%)
  Pallas kernels  32.7 us (21%)
  local copies, waits for them, and re-layouts  10.8 us (7%)
  other arithmetic  2.28 us (1%)
    ppermute x3, waiting for transfers between devices, from_up(): return lax.ppermute(x, 'tp', FROM_UP)  22.6 us
    ppermute x4, waiting for transfers between devices, from_above(): return lax.ppermute(x, 'ctx', FROM_ABOVE)  16.4 us
    all_to_all x1, waiting for transfers between devices, body(): returned = lax.all_to_all(convolved, 'ctx', 0, 0)  9.94 us
    ppermute x4, starting transfers between devices, from_above(): return lax.ppermute(x, 'ctx', FROM_ABOVE)  9.54 us
    ppermute x3, starting transfers between devices, from_up(): return lax.ppermute(x, 'tp', FROM_UP)  9.47 us
    all_to_all x1, starting transfers between devices, body(): owned = lax.all_to_all(gated, 'ctx', 0, 0)  9.38 us
    all_to_all x1, waiting for transfers between devices, body(): owned = lax.all_to_all(gated, 'ctx', 0, 0)  8.22 us
    pallas_call x1, Pallas kernels, gated_input(): pl.pallas_call(functools.partial(gated_kernel, [len(unit) for unit in uni...  7.79 us
  transfers between devices with their start and end apart: 21, of which 14 were waited for; matrix products, arithmetic and copies ran while one was open for 6% of the time, Pallas kernels for 11%

profile of v2, /device:TPU:1, one launch (start us, length us, event | category | flops | bytes accessed | tf_op | source)
XLA Modules:
  0.0 157.8 jit_solution(9510050394644658937)
XLA Ops:
  1.0 3.3 %collective-permute-start.3 = (bf16[128,384]{1,0:T(8,128)(2,1)S(1)}, bf16[128,384]{1,0:T(8,128)(2,1)S(1)}, u32[]{:S(2)}, u32[]{:S(2)}) collective-permute-start(bf16[128,384]{1,0:T(8,128)(2,1)S(1)} %pad_maximum_fusion.3), channel_id=1, source_target_pairs={{0,8},{8,0},{16,24},{24,16},{32,40},{40,32},{48,56},{56,48},{64,72... | collective-permute-start | bytes 294920 | tf_op jit(solution)/shard_map/ppermute | solution.py:360
  5.0 2.8 %collective-permute-start = (bf16[16,512]{1,0:T(8,128)(2,1)S(1)}, bf16[16,512]{1,0:T(8,128)(2,1)S(1)}, u32[]{:S(2)}, u32[]{:S(2)}) collective-permute-start(bf16[16,512]{1,0:T(8,128)(2,1)S(1)} %slice.31), channel_id=1, source_target_pairs={{0,8},{8,16},{16,24},{24,32},{32,40},{40,48},{48,56},{56,64},{64,7... | collective-permute-start | bytes 49160 | tf_op jit(solution)/shard_map/ppermute | solution.py:348
  7.8 1.3 constant_dynamic-update-slice_fusion.1
  9.2 1.7 %collective-permute-start.4 = (bf16[256,384]{1,0:T(8,128)(2,1)S(1)}, bf16[256,384]{1,0:T(8,128)(2,1)S(1)}, u32[]{:S(2)}, u32[]{:S(2)}) collective-permute-start(bf16[256,384]{1,0:T(8,128)(2,1)S(1)} %pad_maximum_fusion.1), channel_id=1, source_target_pairs={{0,16},{8,24},{16,0},{24,8},{32,48},{40,56},{48,32},{56,40},{64,80... | collective-permute-start | bytes 589832 | tf_op jit(solution)/shard_map/ppermute | solution.py:362
  10.9 2.8 %collective-permute-start.1 = (bf16[1040,512]{1,0:T(8,128)(2,1)S(1)}, bf16[1040,512]{1,0:T(8,128)(2,1)}, u32[]{:S(2)}, u32[]{:S(2)}) collective-permute-start(bf16[1040,512]{1,0:T(8,128)(2,1)S(1)} %constant_dynamic-update-slice_fusion.refs_0_), channel_id=1, source_target_pairs={{0,3},{1,0},{2,1},{3,2},{4,7},{5,4},{6,5},{7,6},{8,11},{9,8},{10,9... | collective-permute-start | bytes 3194888 | tf_op jit(solution)/shard_map/ppermute | solution.py:39
  13.7 4.0 %collective-permute-done.4 = bf16[256,384]{1,0:T(8,128)(2,1)S(1)} collective-permute-done((bf16[256,384]{1,0:T(8,128)(2,1)S(1)}, bf16[256,384]{1,0:T(8,128)(2,1)S(1)}, u32[]{:S(2)}, u32[]{:S(2)}) %collective-permute-start.4) | collective-permute-done | bytes 196640 | tf_op jit(solution)/shard_map/ppermute | solution.py:362
  17.9 4.9 %collective-permute-start.11 = (bf16[512,384]{1,0:T(8,128)(2,1)S(1)}, bf16[512,384]{1,0:T(8,128)(2,1)S(1)}, u32[]{:S(2)}, u32[]{:S(2)}) collective-permute-start(bf16[512,384]{1,0:T(8,128)(2,1)S(1)} %pad_maximum_fusion), channel_id=1, source_target_pairs={{0,224},{8,232},{16,240},{24,248},{32,0},{40,8},{48,16},{56,24},{6... | collective-permute-start | bytes 1179656 | tf_op jit(solution)/shard_map/ppermute | solution.py:47
  22.8 14.0 %collective-permute-done.1.refs_1_ = bf16[1040,512]{1,0:T(8,128)(2,1)} collective-permute-done((bf16[1040,512]{1,0:T(8,128)(2,1)S(1)}, bf16[1040,512]{1,0:T(8,128)(2,1)}, u32[]{:S(2)}, u32[]{:S(2)}) %collective-permute-start.1) | collective-permute-done | bytes 1064992 | tf_op jit(solution)/shard_map/ppermute | solution.py:39
  36.8 3.3 %collective-permute-start.8 = (bf16[1040,512]{1,0:T(8,128)(2,1)}, bf16[1040,512]{1,0:T(8,128)(2,1)S(1)}, u32[]{:S(2)}, u32[]{:S(2)}) collective-permute-start(bf16[1040,512]{1,0:T(8,128)(2,1)} %collective-permute-done.1.refs_1_), channel_id=1, source_target_pairs={{0,3},{1,0},{2,1},{3,2},{4,7},{5,4},{6,5},{7,6},{8,11},{9,8},{10,9... | collective-permute-start | bytes 3194888 | tf_op jit(solution)/shard_map/ppermute | solution.py:39
  40.4 2.4 %collective-permute-start.13 = (bf16[512,384]{1,0:T(8,128)(2,1)S(1)}, bf16[512,384]{1,0:T(8,128)(2,1)S(1)}, u32[]{:S(2)}, u32[]{:S(2)}) collective-permute-start(bf16[512,384]{1,0:T(8,128)(2,1)S(1)} %collective-permute-done.11), channel_id=1, source_target_pairs={{0,224},{8,232},{16,240},{24,248},{32,0},{40,8},{48,16},{56,24},{6... | collective-permute-start | bytes 1179656 | tf_op jit(solution)/shard_map/ppermute | solution.py:47
  43.3 7.2 %collective-permute-done.13 = bf16[512,384]{1,0:T(8,128)(2,1)S(1)} collective-permute-done((bf16[512,384]{1,0:T(8,128)(2,1)S(1)}, bf16[512,384]{1,0:T(8,128)(2,1)S(1)}, u32[]{:S(2)}, u32[]{:S(2)}) %collective-permute-start.13) | collective-permute-done | bytes 393248 | tf_op jit(solution)/shard_map/ppermute | solution.py:47
  50.6 1.2 collective-permute-done.14
  51.8 1.5 collective-permute-start.15
  53.6 5.2 %collective-permute-done.15 = bf16[512,384]{1,0:T(8,128)(2,1)S(1)} collective-permute-done((bf16[512,384]{1,0:T(8,128)(2,1)S(1)}, bf16[512,384]{1,0:T(8,128)(2,1)S(1)}, u32[]{:S(2)}, u32[]{:S(2)}) %collective-permute-start.15) | collective-permute-done | bytes 393248 | tf_op jit(solution)/shard_map/ppermute | solution.py:47
  58.8 4.1 %collective-permute-done.8.refs_6_ = bf16[1040,512]{1,0:T(8,128)(2,1)S(1)} collective-permute-done((bf16[1040,512]{1,0:T(8,128)(2,1)}, bf16[1040,512]{1,0:T(8,128)(2,1)S(1)}, u32[]{:S(2)}, u32[]{:S(2)}) %collective-permute-start.8) | collective-permute-done | bytes 1064992 | tf_op jit(solution)/shard_map/ppermute | solution.py:39
  63.7 1.5 collective-permute-done.7.refs_4_
  65.2 1.4 collective-permute-done.6.refs_5_
  68.4 4.0 %collective-permute-done.16 = bf16[512,384]{1,0:T(8,128)(2,1)S(1)} collective-permute-done((bf16[512,384]{1,0:T(8,128)(2,1)S(1)}, bf16[512,384]{1,0:T(8,128)(2,1)S(1)}, u32[]{:S(2)}, u32[]{:S(2)}) %collective-permute-start.16) | collective-permute-done | bytes 393248 | tf_op jit(solution)/shard_map/ppermute | solution.py:47
  72.7 2.4 %collective-permute-start.18 = (bf16[8,512,384]{2,1,0:T(8,128)(2,1)S(1)}, bf16[8,512,384]{2,1,0:T(8,128)(2,1)}, u32[]{:S(2)}, u32[]{:S(2)}) collective-permute-start(bf16[8,512,384]{2,1,0:T(8,128)(2,1)S(1)} %bitcast_dynamic-update-slice_fusion.refs_7_.refs_10_.refs_9_), channel_id=1, source_target_pairs={{0,8},{8,0},{16,24},{24,16},{32,40},{40,32},{48,56},{56,48},{64,72... | collective-permute-start | bytes 9437192 | tf_op jit(solution)/shard_map/ppermute | solution.py:401
  75.3 3.4 %collective-permute-start.9 = (bf16[512,512]{1,0:T(8,128)(2,1)}, bf16[512,512]{1,0:T(8,128)(2,1)S(1)}, u32[]{:S(2)}, u32[]{:S(2)}) collective-permute-start(bf16[512,512]{1,0:T(8,128)(2,1)} %slice.37), channel_id=1, source_target_pairs={{0,3},{1,0},{2,1},{3,2},{4,7},{5,4},{6,5},{7,6},{8,11},{9,8},{10,9... | collective-permute-start | bytes 1572872 | tf_op jit(solution)/shard_map/ppermute | solution.py:39
  79.8 5.9 %shard_map.91.refs_9_ = f32[1040,256]{1,0:T(8,128)} custom-call(s32[8]{0:T(128)} %and_select_fusion.places, bf16[1040,512]{1,0:T(8,128)(2,1)} %copy-done.2, bf16[1040,512]{1,0:T(8,128)(2,1)} %collective-permute-done.1.refs_1_, bf16[1040,512]{1,0:T(8,128)(2,1)} %copy-done.5, bf16[1040,512]{1,0:T(8,128)(2,1)} %copy-done.6, bf16[1040,512]{1,0:T(8,128)(2,1)} %copy-done.4, ...), custom_call_target="tpu_custom_call" | custom-call | flops 1879048192 | bytes 11534336 | tf_op jit(solution)/shard_map/pallas_call | solution.py:134
  85.7 4.5 %collective-permute-done.9.refs_7_ = bf16[512,512]{1,0:T(8,128)(2,1)S(1)} collective-permute-done((bf16[512,512]{1,0:T(8,128)(2,1)}, bf16[512,512]{1,0:T(8,128)(2,1)S(1)}, u32[]{:S(2)}, u32[]{:S(2)}) %collective-permute-start.9) | collective-permute-done | bytes 524320 | tf_op jit(solution)/shard_map/ppermute | solution.py:39
  92.1 7.8 %shard_map.92 = bf16[32,8,1024]{2,1,0:T(8,128)(2,1)} custom-call(s32[8]{0:T(128)} %and_select_fusion.places, bf16[1040,512]{1,0:T(8,128)(2,1)} %copy-done.2, bf16[1040,512]{1,0:T(8,128)(2,1)} %collective-permute-done.1.refs_1_, bf16[1040,512]{1,0:T(8,128)(2,1)} %copy-done.5, bf16[1040,512]{1,0:T(8,128)(2,1)} %copy-done.6, bf16[1040,512]{1,0:T(8,128)(2,1)} %copy-done.4, ...), custom_call_target="tpu_custom_call" | custom-call | flops 2415919104 | bytes 13631488 | tf_op jit(solution)/shard_map/pallas_call | solution.py:179
  99.9 9.4 %all-to-all-start = ((bf16[32,8,1024]{2,1,0:T(8,128)(2,1)}), bf16[32,8,1024]{2,1,0:T(8,128)(2,1)S(1)}, u32[]{:S(2)}, u32[]{:S(2)}) async-start(bf16[32,8,1024]{2,1,0:T(8,128)(2,1)} %shard_map.92), calls=%async_computation | async-start | bytes 1048576 | tf_op jit(solution)/shard_map/all_to_all | solution.py:408
  109.3 2.5 %copy.15 = f32[1,8,128,256]{3,2,1,0:T(8,128)} copy(f32[1,8,128,256]{3,1,2,0:T(8,128)} %bitcast.41) | data formatting | bytes 2097152
  112.5 5.6 %shard_map.93.h_ref = f32[8,256,256]{2,1,0:T(8,128)} custom-call(f32[8,128,256]{2,1,0:T(8,128)} %bitcast.42, bf16[2,256,128]{2,1,0:T(8,128)(2,1)} %constant.105.clone.first_ref, bf16[2,256,512]{2,1,0:T(8,128)(2,1)} %constant.106.clone.turn_ref, f32[2,128,256]{2,1,0:T(8,128)} %constant.108.clone.twiddle_ref), custom_call_target="tpu_custom_call" | custom-call | flops 2013265920 | bytes 5242880 | tf_op jit(solution)/shard_map/pallas_call | solution.py:276
  118.1 8.2 %all-to-all-done.x_ref = bf16[32,8,1024]{2,1,0:T(8,128)(2,1)S(1)} async-done(((bf16[32,8,1024]{2,1,0:T(8,128)(2,1)}), bf16[32,8,1024]{2,1,0:T(8,128)(2,1)S(1)}, u32[]{:S(2)}, u32[]{:S(2)}) %all-to-all-start) | async-done | bytes 524320 | tf_op jit(solution)/shard_map/all_to_all | solution.py:408
  127.1 5.2 %shard_map.94 = bf16[32,8,1024]{2,1,0:T(8,128)(2,1)} custom-call(bf16[32,8,1024]{2,1,0:T(8,128)(2,1)} %copy-done.10, f32[8,256,256]{2,1,0:T(8,128)} %shard_map.93.h_ref, f32[8,1]{1,0:T(8,128)} %copy.11.gain_ref, bf16[256,896]{1,0:T(8,128)(2,1)} %constant.107.clone.table_ref, f32[2,128,256]{2,1,0:T(8,128)} %constant.108.clone.twiddle_ref), custom_call_target="tpu_custom_call" | custom-call | flops 1342177280 | bytes 5242880 | tf_op jit(solution)/shard_map/pallas_call | solution.py:313
  132.3 5.7 %all-to-all-start.1 = ((bf16[32,8,1024]{2,1,0:T(8,128)(2,1)}), bf16[32,8,1024]{2,1,0:T(8,128)(2,1)S(1)}, u32[]{:S(2)}, u32[]{:S(2)}) async-start(bf16[32,8,1024]{2,1,0:T(8,128)(2,1)} %shard_map.94), calls=%async_computation.1 | async-start | bytes 1048576 | tf_op jit(solution)/shard_map/all_to_all | solution.py:410
  138.6 6.5 %shard_map.95.gate_ref = bf16[1024,256]{1,0:T(8,128)(2,1)} custom-call(s32[8]{0:T(128)} %and_select_fusion.places, s32[1]{0:T(128)} %bitcast.21.even, bf16[1040,512]{1,0:T(8,128)(2,1)} %copy-done.2, bf16[1040,512]{1,0:T(8,128)(2,1)} %collective-permute-done.1.refs_1_, bf16[1040,512]{1,0:T(8,128)(2,1)} %copy-done.5, bf16[1040,512]{1,0:T(8,128)(2,1)} %copy-done.6, ...), custom_call_target="tpu_custom_call" | custom-call | flops 2147483648 | bytes 12582912 | tf_op jit(solution)/shard_map/pallas_call | solution.py:214
  145.1 9.9 %all-to-all-done.1.conv_ref = bf16[32,8,1024]{2,1,0:T(8,128)(2,1)S(1)} async-done(((bf16[32,8,1024]{2,1,0:T(8,128)(2,1)}), bf16[32,8,1024]{2,1,0:T(8,128)(2,1)S(1)}, u32[]{:S(2)}, u32[]{:S(2)}) %all-to-all-start.1) | async-done | bytes 524320 | tf_op jit(solution)/shard_map/all_to_all | solution.py:410
  156.1 1.7 %shard_map.96 = bf16[1024,256]{1,0:T(8,128)(2,1)} custom-call(bf16[32,8,1024]{2,1,0:T(8,128)(2,1)S(1)} %all-to-all-done.1.conv_ref, bf16[1024,256]{1,0:T(8,128)(2,1)S(1)} %copy-done), custom_call_target="tpu_custom_call" | custom-call | flops 262144 | bytes 2097152 | tf_op jit(solution)/shard_map/pallas_call | solution.py:333
  (70 shorter events, 12.1 us)
Async XLA Ops:
  1.0 8.2 %collective-permute-start.3 = (bf16[128,384]{1,0:T(8,128)(2,1)S(1)}, bf16[128,384]{1,0:T(8,128)(2,1)S(1)}, u32[]{:S(2)}, u32[]{:S(2)}) collective-permute-start(bf16[128,384]{1,0:T(8,128)(2,1)S(1)} %pad_maximum_fusion.3), channel_id=1, source_target_pairs={{0,8},{8,0},{16,24},{24,16},{32,40},{40,32},{48,56},{56,48},{64,72... | collective-permute-start | bytes 294920 | tf_op jit(solution)/shard_map/ppermute | solution.py:360
  5.0 5.9 %collective-permute-start = (bf16[16,512]{1,0:T(8,128)(2,1)S(1)}, bf16[16,512]{1,0:T(8,128)(2,1)S(1)}, u32[]{:S(2)}, u32[]{:S(2)}) collective-permute-start(bf16[16,512]{1,0:T(8,128)(2,1)S(1)} %slice.31), channel_id=1, source_target_pairs={{0,8},{8,16},{16,24},{24,32},{32,40},{40,48},{48,56},{56,64},{64,7... | collective-permute-start | bytes 49160 | tf_op jit(solution)/shard_map/ppermute | solution.py:348
  9.2 8.5 %collective-permute-start.4 = (bf16[256,384]{1,0:T(8,128)(2,1)S(1)}, bf16[256,384]{1,0:T(8,128)(2,1)S(1)}, u32[]{:S(2)}, u32[]{:S(2)}) collective-permute-start(bf16[256,384]{1,0:T(8,128)(2,1)S(1)} %pad_maximum_fusion.1), channel_id=1, source_target_pairs={{0,16},{8,24},{16,0},{24,8},{32,48},{40,56},{48,32},{56,40},{64,80... | collective-permute-start | bytes 589832 | tf_op jit(solution)/shard_map/ppermute | solution.py:362
  10.9 40.9 %copy-start.2 = (bf16[1040,512]{1,0:T(8,128)(2,1)}, bf16[1040,512]{1,0:T(8,128)(2,1)S(1)}, u32[]{:S(2)}) copy-start(bf16[1040,512]{1,0:T(8,128)(2,1)S(1)} %constant_dynamic-update-slice_fusion.refs_0_) | copy-start | bytes 3194884
  10.9 25.9 %collective-permute-start.1 = (bf16[1040,512]{1,0:T(8,128)(2,1)S(1)}, bf16[1040,512]{1,0:T(8,128)(2,1)}, u32[]{:S(2)}, u32[]{:S(2)}) collective-permute-start(bf16[1040,512]{1,0:T(8,128)(2,1)S(1)} %constant_dynamic-update-slice_fusion.refs_0_), channel_id=1, source_target_pairs={{0,3},{1,0},{2,1},{3,2},{4,7},{5,4},{6,5},{7,6},{8,11},{9,8},{10,9... | collective-permute-start | bytes 3194888 | tf_op jit(solution)/shard_map/ppermute | solution.py:39
  13.7 26.7 %collective-permute-start.2 = (bf16[1040,512]{1,0:T(8,128)(2,1)S(1)}, bf16[1040,512]{1,0:T(8,128)(2,1)S(1)}, u32[]{:S(2)}, u32[]{:S(2)}) collective-permute-start(bf16[1040,512]{1,0:T(8,128)(2,1)S(1)} %constant_dynamic-update-slice_fusion.refs_0_), channel_id=1, source_target_pairs={{0,1},{1,2},{2,3},{3,0},{4,5},{5,6},{6,7},{7,4},{8,9},{9,10},{10,1... | collective-permute-start | bytes 3194888 | tf_op jit(solution)/shard_map/ppermute | solution.py:43
  17.8 25.5 %collective-permute-start.5 = (bf16[1040,512]{1,0:T(8,128)(2,1)S(1)}, bf16[1040,512]{1,0:T(8,128)(2,1)S(1)}, u32[]{:S(2)}, u32[]{:S(2)}) collective-permute-start(bf16[1040,512]{1,0:T(8,128)(2,1)S(1)} %constant_dynamic-update-slice_fusion.refs_0_), channel_id=1, source_target_pairs={{0,4},{1,5},{2,6},{3,7},{4,0},{5,1},{6,2},{7,3},{8,12},{9,13},{10,... | collective-permute-start | bytes 3194888 | tf_op jit(solution)/shard_map/ppermute | solution.py:35
  17.9 22.2 %collective-permute-start.11 = (bf16[512,384]{1,0:T(8,128)(2,1)S(1)}, bf16[512,384]{1,0:T(8,128)(2,1)S(1)}, u32[]{:S(2)}, u32[]{:S(2)}) collective-permute-start(bf16[512,384]{1,0:T(8,128)(2,1)S(1)} %pad_maximum_fusion), channel_id=1, source_target_pairs={{0,224},{8,232},{16,240},{24,248},{32,0},{40,8},{48,16},{56,24},{6... | collective-permute-start | bytes 1179656 | tf_op jit(solution)/shard_map/ppermute | solution.py:47
  22.8 17.3 %collective-permute-start.12 = (bf16[512,384]{1,0:T(8,128)(2,1)S(1)}, bf16[512,384]{1,0:T(8,128)(2,1)S(1)}, u32[]{:S(2)}, u32[]{:S(2)}) collective-permute-start(bf16[512,384]{1,0:T(8,128)(2,1)S(1)} %pad_maximum_fusion), channel_id=1, source_target_pairs={{0,32},{8,40},{16,48},{24,56},{32,64},{40,72},{48,80},{56,88},{64,... | collective-permute-start | bytes 1179656 | tf_op jit(solution)/shard_map/ppermute | solution.py:51
  36.8 26.1 %collective-permute-start.8 = (bf16[1040,512]{1,0:T(8,128)(2,1)}, bf16[1040,512]{1,0:T(8,128)(2,1)S(1)}, u32[]{:S(2)}, u32[]{:S(2)}) collective-permute-start(bf16[1040,512]{1,0:T(8,128)(2,1)} %collective-permute-done.1.refs_1_), channel_id=1, source_target_pairs={{0,3},{1,0},{2,1},{3,2},{4,7},{5,4},{6,5},{7,6},{8,11},{9,8},{10,9... | collective-permute-start | bytes 3194888 | tf_op jit(solution)/shard_map/ppermute | solution.py:39
  40.4 24.8 %copy-start.5 = (bf16[1040,512]{1,0:T(8,128)(2,1)}, bf16[1040,512]{1,0:T(8,128)(2,1)S(1)}, u32[]{:S(2)}) copy-start(bf16[1040,512]{1,0:T(8,128)(2,1)S(1)} %collective-permute-done.2.refs_2_) | copy-start | bytes 3194884
  40.4 10.2 %collective-permute-start.13 = (bf16[512,384]{1,0:T(8,128)(2,1)S(1)}, bf16[512,384]{1,0:T(8,128)(2,1)S(1)}, u32[]{:S(2)}, u32[]{:S(2)}) collective-permute-start(bf16[512,384]{1,0:T(8,128)(2,1)S(1)} %collective-permute-done.11), channel_id=1, source_target_pairs={{0,224},{8,232},{16,240},{24,248},{32,0},{40,8},{48,16},{56,24},{6... | collective-permute-start | bytes 1179656 | tf_op jit(solution)/shard_map/ppermute | solution.py:47
  42.8 9.0 %collective-permute-start.14 = (bf16[512,384]{1,0:T(8,128)(2,1)S(1)}, bf16[512,384]{1,0:T(8,128)(2,1)S(1)}, u32[]{:S(2)}, u32[]{:S(2)}) collective-permute-start(bf16[512,384]{1,0:T(8,128)(2,1)S(1)} %collective-permute-done.12), channel_id=1, source_target_pairs={{0,32},{8,40},{16,48},{24,56},{32,64},{40,72},{48,80},{56,88},{64,... | collective-permute-start | bytes 1179656 | tf_op jit(solution)/shard_map/ppermute | solution.py:51
  42.8 22.4 %collective-permute-start.7 = (bf16[1040,512]{1,0:T(8,128)(2,1)}, bf16[1040,512]{1,0:T(8,128)(2,1)S(1)}, u32[]{:S(2)}, u32[]{:S(2)}) collective-permute-start(bf16[1040,512]{1,0:T(8,128)(2,1)} %collective-permute-done.1.refs_1_), channel_id=1, source_target_pairs={{0,4},{1,5},{2,6},{3,7},{4,0},{5,1},{6,2},{7,3},{8,12},{9,13},{10,... | collective-permute-start | bytes 3194888 | tf_op jit(solution)/shard_map/ppermute | solution.py:35
  43.3 29.2 %copy-start.6 = (bf16[1040,512]{1,0:T(8,128)(2,1)}, bf16[1040,512]{1,0:T(8,128)(2,1)S(1)}, u32[]{:S(2)}) copy-start(bf16[1040,512]{1,0:T(8,128)(2,1)S(1)} %collective-permute-done.5.refs_3_) | copy-start | bytes 3194884
  43.3 23.3 %collective-permute-start.6 = (bf16[1040,512]{1,0:T(8,128)(2,1)S(1)}, bf16[1040,512]{1,0:T(8,128)(2,1)S(1)}, u32[]{:S(2)}, u32[]{:S(2)}) collective-permute-start(bf16[1040,512]{1,0:T(8,128)(2,1)S(1)} %collective-permute-done.5.refs_3_), channel_id=1, source_target_pairs={{0,1},{1,2},{2,3},{3,0},{4,5},{5,6},{6,7},{7,4},{8,9},{9,10},{10,1... | collective-permute-start | bytes 3194888 | tf_op jit(solution)/shard_map/ppermute | solution.py:43
  51.8 6.9 %collective-permute-start.15 = (bf16[512,384]{1,0:T(8,128)(2,1)S(1)}, bf16[512,384]{1,0:T(8,128)(2,1)S(1)}, u32[]{:S(2)}, u32[]{:S(2)}) collective-permute-start(bf16[512,384]{1,0:T(8,128)(2,1)S(1)} %collective-permute-done.13), channel_id=1, source_target_pairs={{0,224},{8,232},{16,240},{24,248},{32,0},{40,8},{48,16},{56,24},{6... | collective-permute-start | bytes 1179656 | tf_op jit(solution)/shard_map/ppermute | solution.py:47
  53.5 14.9 %collective-permute-start.17 = (bf16[512,384]{1,0:T(8,128)(2,1)S(1)}, bf16[512,384]{1,0:T(8,128)(2,1)S(1)}, u32[]{:S(2)}, u32[]{:S(2)}) collective-permute-start(bf16[512,384]{1,0:T(8,128)(2,1)S(1)} %collective-permute-done.14), channel_id=1, source_target_pairs={{0,32},{8,40},{16,48},{24,56},{32,64},{40,72},{48,80},{56,88},{64,... | collective-permute-start | bytes 1179656 | tf_op jit(solution)/shard_map/ppermute | solution.py:51
  62.9 9.8 %copy-start.7 = (bf16[1040,512]{1,0:T(8,128)(2,1)}, bf16[1040,512]{1,0:T(8,128)(2,1)S(1)}, u32[]{:S(2)}) copy-start(bf16[1040,512]{1,0:T(8,128)(2,1)S(1)} %collective-permute-done.8.refs_6_) | copy-start | bytes 3194884
  62.9 9.5 %collective-permute-start.16 = (bf16[512,384]{1,0:T(8,128)(2,1)S(1)}, bf16[512,384]{1,0:T(8,128)(2,1)S(1)}, u32[]{:S(2)}, u32[]{:S(2)}) collective-permute-start(bf16[512,384]{1,0:T(8,128)(2,1)S(1)} %collective-permute-done.15), channel_id=1, source_target_pairs={{0,224},{8,232},{16,240},{24,248},{32,0},{40,8},{48,16},{56,24},{6... | collective-permute-start | bytes 1179656 | tf_op jit(solution)/shard_map/ppermute | solution.py:47
  63.7 11.5 %copy-start.11 = (f32[3,3,256]{2,1,0:T(4,128)S(1)}, f32[3,3,256]{2,1,0:T(4,128)}, u32[]{:S(2)}) copy-start(f32[3,3,256]{2,1,0:T(4,128)} %param.11) | copy-start | bytes 27652
  65.2 7.5 %copy-start.4 = (bf16[1040,512]{1,0:T(8,128)(2,1)}, bf16[1040,512]{1,0:T(8,128)(2,1)S(1)}, u32[]{:S(2)}) copy-start(bf16[1040,512]{1,0:T(8,128)(2,1)S(1)} %collective-permute-done.7.refs_4_) | copy-start | bytes 3194884
  66.7 6.0 %copy-start.3 = (bf16[1040,512]{1,0:T(8,128)(2,1)}, bf16[1040,512]{1,0:T(8,128)(2,1)S(1)}, u32[]{:S(2)}) copy-start(bf16[1040,512]{1,0:T(8,128)(2,1)S(1)} %collective-permute-done.6.refs_5_) | copy-start | bytes 3194884
  72.7 7.1 %copy-start.1 = (bf16[8,512,384]{2,1,0:T(8,128)(2,1)}, bf16[8,512,384]{2,1,0:T(8,128)(2,1)S(1)}, u32[]{:S(2)}) copy-start(bf16[8,512,384]{2,1,0:T(8,128)(2,1)S(1)} %bitcast_dynamic-update-slice_fusion.refs_7_.refs_10_.refs_9_) | copy-start | bytes 9437188
  72.7 18.6 %collective-permute-start.18 = (bf16[8,512,384]{2,1,0:T(8,128)(2,1)S(1)}, bf16[8,512,384]{2,1,0:T(8,128)(2,1)}, u32[]{:S(2)}, u32[]{:S(2)}) collective-permute-start(bf16[8,512,384]{2,1,0:T(8,128)(2,1)S(1)} %bitcast_dynamic-update-slice_fusion.refs_7_.refs_10_.refs_9_), channel_id=1, source_target_pairs={{0,8},{8,0},{16,24},{24,16},{32,40},{40,32},{48,56},{56,48},{64,72... | collective-permute-start | bytes 9437192 | tf_op jit(solution)/shard_map/ppermute | solution.py:401
  75.2 16.1 %collective-permute-start.10 = (bf16[528,512]{1,0:T(8,128)(2,1)}, bf16[528,512]{1,0:T(8,128)(2,1)S(1)}, u32[]{:S(2)}, u32[]{:S(2)}) collective-permute-start(bf16[528,512]{1,0:T(8,128)(2,1)} %slice.38), channel_id=1, source_target_pairs={{0,1},{1,2},{2,3},{3,0},{4,5},{5,6},{6,7},{7,4},{8,9},{9,10},{10,1... | collective-permute-start | bytes 1622024 | tf_op jit(solution)/shard_map/ppermute | solution.py:43
  75.3 14.9 %collective-permute-start.9 = (bf16[512,512]{1,0:T(8,128)(2,1)}, bf16[512,512]{1,0:T(8,128)(2,1)S(1)}, u32[]{:S(2)}, u32[]{:S(2)}) collective-permute-start(bf16[512,512]{1,0:T(8,128)(2,1)} %slice.37), channel_id=1, source_target_pairs={{0,3},{1,0},{2,1},{3,2},{4,7},{5,4},{6,5},{7,6},{8,11},{9,8},{10,9... | collective-permute-start | bytes 1572872 | tf_op jit(solution)/shard_map/ppermute | solution.py:39
  90.2 1.2 copy-start.9
  99.9 11.9 %copy-start.12 = (f32[8]{0:T(128)S(1)}, f32[8]{0:T(128)}, u32[]{:S(2)}) copy-start(f32[8]{0:T(128)} %param.13) | copy-start | bytes 100
  99.9 26.4 %all-to-all-start = ((bf16[32,8,1024]{2,1,0:T(8,128)(2,1)}), bf16[32,8,1024]{2,1,0:T(8,128)(2,1)S(1)}, u32[]{:S(2)}, u32[]{:S(2)}) async-start(bf16[32,8,1024]{2,1,0:T(8,128)(2,1)} %shard_map.92), calls=%async_computation | async-start | bytes 1048576 | tf_op jit(solution)/shard_map/all_to_all | solution.py:408
  132.3 22.7 %all-to-all-start.1 = ((bf16[32,8,1024]{2,1,0:T(8,128)(2,1)}), bf16[32,8,1024]{2,1,0:T(8,128)(2,1)S(1)}, u32[]{:S(2)}, u32[]{:S(2)}) async-start(bf16[32,8,1024]{2,1,0:T(8,128)(2,1)} %shard_map.94), calls=%async_computation.1 | async-start | bytes 1048576 | tf_op jit(solution)/shard_map/all_to_all | solution.py:410
  155.0 1.0 copy-start
  (2 other events, 1.6 us)

commit v3 on v2

--- a/solution.py
+++ b/solution.py
@@ -63,15 +63,32 @@
     return [pl.BlockSpec(memory_space=pltpu.VMEM)] * count
 
 
+class WeightCopy:
+    def __init__(self, place, pair, cols, buf, sem):
+        self.place = place
+        self.near = lambda: pltpu.make_async_copy(pair[0].at[jnp.minimum(place, 6), :, cols], buf, sem)
+        self.far = lambda: pltpu.make_async_copy(pair[1].at[:, cols], buf, sem)
+
+    def start(self):
+        lax.cond(self.place < 7, lambda: self.near().start(), lambda: self.far().start())
+
+    def wait(self):
+        self.far().wait()
+
+
 def unit_copies(places, u, units, weights, a_buf, b_buf, w_bufs, sems):
     unit = units[u]
     if len(unit) == 1:
         a, b = unit[0].at[pl.ds(0, HALF)], unit[0].at[pl.ds(HALF, HALF + HALO)]
     else:
         a, b = unit
-    pairs = [(a, a_buf.at[u]), (b, b_buf.at[u])]
-    pairs += [(w.at[places[u], :, cols], buf.at[u]) for (w, cols), buf in zip(weights, w_bufs)]
-    return [pltpu.make_async_copy(*pair, sems.at[u, n]) for n, pair in enumerate(pairs)]
+    copies = [
+        pltpu.make_async_copy(a, a_buf.at[u], sems.at[u, 0]),
+        pltpu.make_async_copy(b, b_buf.at[u], sems.at[u, 1]),
+    ]
+    for n, ((pair, cols), buf) in enumerate(zip(weights, w_bufs)):
+        copies.append(WeightCopy(places[u], pair, cols, buf.at[u], sems.at[u, 2 + n]))
+    return copies
 
 
 def grouped(refs, sizes):
@@ -126,22 +143,22 @@
 
 
 def partial_kernel(sizes, places, *refs):
-    units, (w_ref, out_ref, a_buf, b_buf, w_buf, sems) = grouped(refs, sizes)
-    sum_units(places, 7, units, [(w_ref, KV)], lambda w: w[0], out_ref, a_buf, b_buf, [w_buf], sems)
+    units, (near, far, out_ref, a_buf, b_buf, w_buf, sems) = grouped(refs, sizes)
+    sum_units(places, 7, units, [((near, far), KV)], lambda w: w[0], out_ref, a_buf, b_buf, [w_buf], sems)
 
 
 def partial_products(places, units, w):
     return pl.pallas_call(
         functools.partial(partial_kernel, [len(unit) for unit in units]),
         out_shape=jax.ShapeDtypeStruct((HALO + ROWS, 256), F32),
-        in_specs=[SMEM] + [ANY] * (len(flat(units)) + 1),
+        in_specs=[SMEM] + [ANY] * (len(flat(units)) + 2),
         out_specs=pl.BlockSpec(memory_space=pltpu.VMEM),
         scratch_shapes=unit_scratch(7, [256]),
         compiler_params=pltpu.CompilerParams(vmem_limit_bytes=VMEM),
         cost_estimate=pl.CostEstimate(
             flops=2 * 7 * 1024 * 512 * 256, bytes_accessed=11 * MIB, transcendentals=0
         ),
-    )(places, *flat(units), w)
+    )(places, *flat(units), *w)
 
 
 def filtered(branch, taps, start, size):
@@ -157,13 +174,13 @@
 
 def gated_kernel(sizes, places, *refs):
     units, refs = grouped(refs, sizes)
-    acc_ref, own_ref, sib_ref, taps_ref, out_ref, a_buf, b_buf, w_buf, sems = refs[:9]
-    own_buf, own_sems, mine, theirs = refs[9:]
+    acc_ref, own0, own1, sib0, sib1, taps_ref, out_ref, a_buf, b_buf, w_buf, sems = refs[:11]
+    own_buf, own_sems, mine, theirs = refs[11:]
     copies = [
         pltpu.make_async_copy(acc_ref, mine, own_sems.at[0]),
-        pltpu.make_async_copy(own_ref.at[places[7], :, KV], own_buf, own_sems.at[1]),
+        WeightCopy(places[7], (own0, own1), KV, own_buf, own_sems.at[1]),
     ]
-    sum_units(places, 8, units, [(sib_ref, KV)], lambda w: w[0], theirs, a_buf, b_buf, [w_buf], sems, copies)
+    sum_units(places, 8, units, [((sib0, sib1), KV)], lambda w: w[0], theirs, a_buf, b_buf, [w_buf], sems, copies)
     for copy in copies:
         copy.wait()
     add_products(mine, False, a_buf[7], b_buf[7], own_buf[...])
@@ -179,7 +196,7 @@
     return pl.pallas_call(
         functools.partial(gated_kernel, [len(unit) for unit in units]),
         out_shape=jax.ShapeDtypeStruct((32, 8, ROWS), BF16),
-        in_specs=[SMEM] + [ANY] * (len(flat(units)) + 3) + vmem_specs(1),
+        in_specs=[SMEM] + [ANY] * (len(flat(units)) + 5) + vmem_specs(1),
         out_specs=pl.BlockSpec(memory_space=pltpu.VMEM),
         scratch_shapes=unit_scratch(8, [256])
         + [
@@ -192,19 +209,19 @@
         cost_estimate=pl.CostEstimate(
             flops=2 * 9 * 1024 * 512 * 256, bytes_accessed=13 * MIB, transcendentals=0
         ),
-    )(places, *flat(units), acc, own, sib, taps)
+    )(places, *flat(units), acc, *own, *sib, taps)
 
 
 def query_kernel(sizes, places, even, *refs):
     units, refs = grouped(refs, sizes)
-    own_ref, sib_ref, taps_ref, out_ref, a_buf, b_buf, own_buf, sib_buf, sems, total = refs
+    own0, own1, sib0, sib1, taps_ref, out_ref, a_buf, b_buf, own_buf, sib_buf, sems, total = refs
     first_core = even[0] == 1
 
     def joined(w):
         own, sib = w
         return jnp.concatenate([jnp.where(first_core, own, sib), jnp.where(first_core, sib, own)], 1)
 
-    sum_units(places, 8, units, [(own_ref, QUERY), (sib_ref, QUERY)], joined, total, a_buf, b_buf, [own_buf, sib_buf], sems)
+    sum_units(places, 8, units, [((own0, own1), QUERY), ((sib0, sib1), QUERY)], joined, total, a_buf, b_buf, [own_buf, sib_buf], sems)
     rounded(total)
     for r in range(ROWS // 256):
         out_ref[r * 256 : r * 256 + 256, :] = filtered(total, taps_ref[...], r * 256, 256).astype(BF16)
@@ -214,14 +231,14 @@
     return pl.pallas_call(
         functools.partial(query_kernel, [len(unit) for unit in units]),
         out_shape=jax.ShapeDtypeStruct((ROWS, 256), BF16),
-        in_specs=[SMEM] * 2 + [ANY] * (len(flat(units)) + 2) + vmem_specs(1),
+        in_specs=[SMEM] * 2 + [ANY] * (len(flat(units)) + 4) + vmem_specs(1),
         out_specs=pl.BlockSpec(memory_space=pltpu.VMEM),
         scratch_shapes=unit_scratch(8, [128, 128]) + [pltpu.VMEM((HALO + ROWS, 256), F32)],
         compiler_params=pltpu.CompilerParams(vmem_limit_bytes=VMEM),
         cost_estimate=pl.CostEstimate(
             flops=2 * 8 * 1024 * 512 * 256, bytes_accessed=12 * MIB, transcendentals=0
         ),
-    )(places, even, *flat(units), own, sib, taps)
+    )(places, even, *flat(units), *own, *sib, taps)
 
 
 def two_parts(table):
@@ -375,12 +392,10 @@
     w2, v2 = tied(u2, d2, b0)[:2]
     bm, bp = from_down(b0), other_xlo(ap)
     u3, d3 = from_above(w2), from_below(v2)
-    u4 = from_above(tied(u3, a2)[0])
-    bm, bp, a2 = tied(bm, bp, a2)
-    parts = (bp[:HALF], bm[HALF:])
-    b2 = (from_up(parts[0]), from_down(parts[1]))
-    u4, d3 = tied(u4, d3, a2, *parts)[:2]
-    own = jnp.stack([block, u1, u2, u3, u4, d3, d2, d1])
+    a2, bm, bp, u3, d3 = tied(a2, bm, bp, u3, d3)
+    b2 = (from_up(bp[:HALF]), from_down(bm[HALF:]))
+    far = jnp.concatenate([from_above(u3[:256]), from_below(d3[256:])], 0)
+    own = (jnp.stack([block, u1, u2, u3, d3, d2, d1]), far)
 
     xlo, y = tp // 4, tp % 4
     mine, others = xlo * 4, (1 - xlo) * 4
@@ -398,7 +413,8 @@
         ]
     ).astype(jnp.int32)
     places = (places - ctx // 4) % 8
-    sib = lax.ppermute(own, "ctx", OTHER_CORE)
+    places = jnp.where(places == 4, 7, jnp.where(places > 4, places - 1, places))
+    sib = tuple(lax.ppermute(w, "ctx", OTHER_CORE) for w in own)
     units = ((a0,), (ap,), (am,), (b0,), (bp,), (bm,), (a2,))
     own_acc = partial_products(places, units, own)
     taps = short_taps.transpose(1, 0, 2)

time: 159 us -> 157 us (0.987)
  waiting for transfers between devices: 66.8 us -> 58.5 us
  starting transfers between devices: 45 us -> 49.5 us
    ppermute x3, waiting for transfers between devices: 22.6 us -> 15.1 us  [from_up(): return lax.ppermute(x, 'tp', FROM_UP)]
    ppermute x3 -> x4, waiting for transfers between devices: 1.24 us -> 6.34 us  [from_below(): return lax.ppermute(x, 'ctx', FROM_BELOW)]
    ppermute x4, starting transfers between devices: 9.54 us -> 12.9 us  [from_above(): return lax.ppermute(x, 'ctx', FROM_ABOVE)]
    ppermute x4, waiting for transfers between devices: 16.4 us -> 14.2 us  [from_above(): return lax.ppermute(x, 'ctx', FROM_ABOVE)]
    ppermute x3, starting transfers between devices: 0.03 us -> 2.02 us  [from_down(): return lax.ppermute(x, 'tp', FROM_DOWN)]
    ppermute x3, starting transfers between devices: 9.47 us -> 7.53 us  [from_up(): return lax.ppermute(x, 'tp', FROM_UP)]
    ppermute x1 -> x2, starting transfers between devices: 2.42 us -> 4.27 us  [body(): sib = tuple((lax.ppermute(w, 'ctx', OTHER_CORE) for w in own))]
    ppermute x3, waiting for transfers between devices: 2.88 us -> 1.15 us  [from_down(): return lax.ppermute(x, 'tp', FROM_DOWN)]
  transfers between devices with their start and end apart: 21 -> 23, of which waited for: 14 -> 12; matrix products, arithmetic and copies ran while one was open for 6% -> 6% of each run, Pallas kernels for 11% -> 12%
where the time goes in v3:
time: 157 us; the launch traced here: 156 us
  waiting for transfers between devices  58.5 us (37%)
  starting transfers between devices  49.5 us (32%)
  Pallas kernels  32.8 us (21%)
  local copies, waits for them, and re-layouts  12.2 us (8%)
  other arithmetic  2.35 us (1%)
    ppermute x3, waiting for transfers between devices, from_up(): return lax.ppermute(x, 'tp', FROM_UP)  15.1 us
    ppermute x4, waiting for transfers between devices, from_above(): return lax.ppermute(x, 'ctx', FROM_ABOVE)  14.2 us
    ppermute x4, starting transfers between devices, from_above(): return lax.ppermute(x, 'ctx', FROM_ABOVE)  12.9 us
    all_to_all x1, waiting for transfers between devices, body(): returned = lax.all_to_all(convolved, 'ctx', 0, 0)  9.8 us
    all_to_all x1, waiting for transfers between devices, body(): owned = lax.all_to_all(gated, 'ctx', 0, 0)  8.32 us
    pallas_call x1, Pallas kernels, gated_input(): pl.pallas_call(functools.partial(gated_kernel, [len(unit) for unit in uni...  7.85 us
    unnamed x41, local copies, waits for them, and re-layouts  7.85 us
    all_to_all x1, starting transfers between devices, body(): owned = lax.all_to_all(gated, 'ctx', 0, 0)  7.83 us
  transfers between devices with their start and end apart: 23, of which 12 were waited for; matrix products, arithmetic and copies ran while one was open for 6% of the time, Pallas kernels for 12%

profile of v3, /device:TPU:1, one launch (start us, length us, event | category | flops | bytes accessed | tf_op | source)
XLA Modules:
  0.0 155.8 jit_solution(11374786274589245668)
XLA Ops:
  1.0 3.3 %collective-permute-start.3 = (bf16[128,384]{1,0:T(8,128)(2,1)S(1)}, bf16[128,384]{1,0:T(8,128)(2,1)S(1)}, u32[]{:S(2)}, u32[]{:S(2)}) collective-permute-start(bf16[128,384]{1,0:T(8,128)(2,1)S(1)} %pad_maximum_fusion.3), channel_id=1, source_target_pairs={{0,8},{8,0},{16,24},{24,16},{32,40},{40,32},{48,56},{56,48},{64,72... | collective-permute-start | bytes 294920 | tf_op jit(solution)/shard_map/ppermute | solution.py:377
  5.0 2.8 %collective-permute-start = (bf16[16,512]{1,0:T(8,128)(2,1)S(1)}, bf16[16,512]{1,0:T(8,128)(2,1)S(1)}, u32[]{:S(2)}, u32[]{:S(2)}) collective-permute-start(bf16[16,512]{1,0:T(8,128)(2,1)S(1)} %slice.37), channel_id=1, source_target_pairs={{0,8},{8,16},{16,24},{24,32},{32,40},{40,48},{48,56},{56,64},{64,7... | collective-permute-start | bytes 49160 | tf_op jit(solution)/shard_map/ppermute | solution.py:365
  7.9 1.7 %collective-permute-start.4 = (bf16[256,384]{1,0:T(8,128)(2,1)S(1)}, bf16[256,384]{1,0:T(8,128)(2,1)S(1)}, u32[]{:S(2)}, u32[]{:S(2)}) collective-permute-start(bf16[256,384]{1,0:T(8,128)(2,1)S(1)} %pad_maximum_fusion.1), channel_id=1, source_target_pairs={{0,16},{8,24},{16,0},{24,8},{32,48},{40,56},{48,32},{56,40},{64,80... | collective-permute-start | bytes 589832 | tf_op jit(solution)/shard_map/ppermute | solution.py:379
  9.6 1.3 constant_dynamic-update-slice_fusion.1
  10.9 2.8 %collective-permute-start.1 = (bf16[1040,512]{1,0:T(8,128)(2,1)S(1)}, bf16[1040,512]{1,0:T(8,128)(2,1)S(1)}, u32[]{:S(2)}, u32[]{:S(2)}) collective-permute-start(bf16[1040,512]{1,0:T(8,128)(2,1)S(1)} %constant_dynamic-update-slice_fusion.refs_0_), channel_id=1, source_target_pairs={{0,3},{1,0},{2,1},{3,2},{4,7},{5,4},{6,5},{7,6},{8,11},{9,8},{10,9... | collective-permute-start | bytes 3194888 | tf_op jit(solution)/shard_map/ppermute | solution.py:39
  13.8 2.6 %collective-permute-done.4 = bf16[256,384]{1,0:T(8,128)(2,1)S(1)} collective-permute-done((bf16[256,384]{1,0:T(8,128)(2,1)S(1)}, bf16[256,384]{1,0:T(8,128)(2,1)S(1)}, u32[]{:S(2)}, u32[]{:S(2)}) %collective-permute-start.4) | collective-permute-done | bytes 196640 | tf_op jit(solution)/shard_map/ppermute | solution.py:379
  17.2 5.6 %collective-permute-start.9 = (bf16[512,384]{1,0:T(8,128)(2,1)S(1)}, bf16[512,384]{1,0:T(8,128)(2,1)S(1)}, u32[]{:S(2)}, u32[]{:S(2)}) collective-permute-start(bf16[512,384]{1,0:T(8,128)(2,1)S(1)} %pad_maximum_fusion), channel_id=1, source_target_pairs={{0,224},{8,232},{16,240},{24,248},{32,0},{40,8},{48,16},{56,24},{6... | collective-permute-start | bytes 1179656 | tf_op jit(solution)/shard_map/ppermute | solution.py:47
  22.8 14.1 %collective-permute-done.1.refs_1_ = bf16[1040,512]{1,0:T(8,128)(2,1)S(1)} collective-permute-done((bf16[1040,512]{1,0:T(8,128)(2,1)S(1)}, bf16[1040,512]{1,0:T(8,128)(2,1)S(1)}, u32[]{:S(2)}, u32[]{:S(2)}) %collective-permute-start.1) | collective-permute-done | bytes 1064992 | tf_op jit(solution)/shard_map/ppermute | solution.py:39
  36.9 3.2 %collective-permute-start.6 = (bf16[1040,512]{1,0:T(8,128)(2,1)S(1)}, bf16[1040,512]{1,0:T(8,128)(2,1)S(1)}, u32[]{:S(2)}, u32[]{:S(2)}) collective-permute-start(bf16[1040,512]{1,0:T(8,128)(2,1)S(1)} %collective-permute-done.1.refs_1_), channel_id=1, source_target_pairs={{0,3},{1,0},{2,1},{3,2},{4,7},{5,4},{6,5},{7,6},{8,11},{9,8},{10,9... | collective-permute-start | bytes 3194888 | tf_op jit(solution)/shard_map/ppermute | solution.py:39
  42.5 5.2 %collective-permute-start.11 = (bf16[512,384]{1,0:T(8,128)(2,1)S(1)}, bf16[512,384]{1,0:T(8,128)(2,1)S(1)}, u32[]{:S(2)}, u32[]{:S(2)}) collective-permute-start(bf16[512,384]{1,0:T(8,128)(2,1)S(1)} %collective-permute-done.9), channel_id=1, source_target_pairs={{0,224},{8,232},{16,240},{24,248},{32,0},{40,8},{48,16},{56,24},{6... | collective-permute-start | bytes 1179656 | tf_op jit(solution)/shard_map/ppermute | solution.py:47
  47.8 7.4 %collective-permute-done.11 = bf16[512,384]{1,0:T(8,128)(2,1)S(1)} collective-permute-done((bf16[512,384]{1,0:T(8,128)(2,1)S(1)}, bf16[512,384]{1,0:T(8,128)(2,1)S(1)}, u32[]{:S(2)}, u32[]{:S(2)}) %collective-permute-start.11) | collective-permute-done | bytes 393248 | tf_op jit(solution)/shard_map/ppermute | solution.py:47
  55.2 3.1 %collective-permute-done.12 = bf16[512,384]{1,0:T(8,128)(2,1)S(1)} collective-permute-done((bf16[512,384]{1,0:T(8,128)(2,1)S(1)}, bf16[512,384]{1,0:T(8,128)(2,1)S(1)}, u32[]{:S(2)}, u32[]{:S(2)}) %collective-permute-start.12) | collective-permute-done | bytes 393248 | tf_op jit(solution)/shard_map/ppermute | solution.py:51
  58.6 1.2 collective-permute-start.14
  59.9 6.8 %collective-permute-done.13 = bf16[512,384]{1,0:T(8,128)(2,1)S(1)} collective-permute-done((bf16[512,384]{1,0:T(8,128)(2,1)S(1)}, bf16[512,384]{1,0:T(8,128)(2,1)S(1)}, u32[]{:S(2)}, u32[]{:S(2)}) %collective-permute-start.13) | collective-permute-done | bytes 393248 | tf_op jit(solution)/shard_map/ppermute | solution.py:47
  66.7 1.5 collective-permute-done.14
  69.3 3.1 %collective-permute-start.19 = (bf16[7,512,384]{2,1,0:T(8,128)(2,1)S(1)}, bf16[7,512,384]{2,1,0:T(8,128)(2,1)}, u32[]{:S(2)}, u32[]{:S(2)}) collective-permute-start(bf16[7,512,384]{2,1,0:T(8,128)(2,1)S(1)} %bitcast_dynamic-update-slice_fusion.refs_7_.refs_10_.refs_9_), channel_id=1, source_target_pairs={{0,8},{8,0},{16,24},{24,16},{32,40},{40,32},{48,56},{56,48},{64,72... | collective-permute-start | bytes 8257544 | tf_op jit(solution)/shard_map/ppermute | solution.py:417
  72.5 1.9 %collective-permute-start.17 = (bf16[256,384]{1,0:T(8,128)(2,1)S(1)}, bf16[256,384]{1,0:T(8,128)(2,1)S(1)}, u32[]{:S(2)}, u32[]{:S(2)}) collective-permute-start(bf16[256,384]{1,0:T(8,128)(2,1)S(1)} %slice.45), channel_id=1, source_target_pairs={{0,224},{8,232},{16,240},{24,248},{32,0},{40,8},{48,16},{56,24},{6... | collective-permute-start | bytes 589832 | tf_op jit(solution)/shard_map/ppermute | solution.py:47
  76.1 1.3 collective-permute-start.16
  78.5 1.5 collective-permute-start.15
  80.0 1.7 %collective-permute-done.18 = bf16[256,384]{1,0:T(8,128)(2,1)S(1)} collective-permute-done((bf16[256,384]{1,0:T(8,128)(2,1)S(1)}, bf16[256,384]{1,0:T(8,128)(2,1)S(1)}, u32[]{:S(2)}, u32[]{:S(2)}) %collective-permute-start.18) | collective-permute-done | bytes 196640 | tf_op jit(solution)/shard_map/ppermute | solution.py:51
  81.8 1.2 collective-permute-start.20
  83.6 5.9 %shard_map.91.refs_9_ = f32[1040,256]{1,0:T(8,128)} custom-call(s32[8]{0:T(128)} %compare_select_fusion.3.places, bf16[1040,512]{1,0:T(8,128)(2,1)} %copy-done.2, bf16[1040,512]{1,0:T(8,128)(2,1)} %copy-done.5, bf16[1040,512]{1,0:T(8,128)(2,1)} %copy-done.7, bf16[1040,512]{1,0:T(8,128)(2,1)} %copy-done.6, bf16[1040,512]{1,0:T(8,128)(2,1)} %copy-done.4, ...), custom_call_target="tpu_custom_call" | custom-call | flops 1879048192 | bytes 11534336 | tf_op jit(solution)/shard_map/pallas_call | solution.py:151
  91.6 7.8 %shard_map.92 = bf16[32,8,1024]{2,1,0:T(8,128)(2,1)} custom-call(s32[8]{0:T(128)} %compare_select_fusion.3.places, bf16[1040,512]{1,0:T(8,128)(2,1)} %copy-done.2, bf16[1040,512]{1,0:T(8,128)(2,1)} %copy-done.5, bf16[1040,512]{1,0:T(8,128)(2,1)} %copy-done.7, bf16[1040,512]{1,0:T(8,128)(2,1)} %copy-done.6, bf16[1040,512]{1,0:T(8,128)(2,1)} %copy-done.4, ...), custom_call_target="tpu_custom_call" | custom-call | flops 2415919104 | bytes 13631488 | tf_op jit(solution)/shard_map/pallas_call | solution.py:196
  99.5 7.8 %all-to-all-start = ((bf16[32,8,1024]{2,1,0:T(8,128)(2,1)}), bf16[32,8,1024]{2,1,0:T(8,128)(2,1)S(1)}, u32[]{:S(2)}, u32[]{:S(2)}) async-start(bf16[32,8,1024]{2,1,0:T(8,128)(2,1)} %shard_map.92), calls=%async_computation | async-start | bytes 1048576 | tf_op jit(solution)/shard_map/all_to_all | solution.py:424
  107.3 2.5 %copy.15 = f32[1,8,128,256]{3,2,1,0:T(8,128)} copy(f32[1,8,128,256]{3,1,2,0:T(8,128)} %bitcast.39) | data formatting | bytes 2097152
  110.5 5.5 %shard_map.93.h_ref = f32[8,256,256]{2,1,0:T(8,128)} custom-call(f32[8,128,256]{2,1,0:T(8,128)} %bitcast.40, bf16[2,256,128]{2,1,0:T(8,128)(2,1)} %constant.109.clone.first_ref, bf16[2,256,512]{2,1,0:T(8,128)(2,1)} %constant.110.clone.turn_ref, f32[2,128,256]{2,1,0:T(8,128)} %constant.112.clone.twiddle_ref), custom_call_target="tpu_custom_call" | custom-call | flops 2013265920 | bytes 5242880 | tf_op jit(solution)/shard_map/pallas_call | solution.py:293
  116.0 8.3 %all-to-all-done.x_ref = bf16[32,8,1024]{2,1,0:T(8,128)(2,1)S(1)} async-done(((bf16[32,8,1024]{2,1,0:T(8,128)(2,1)}), bf16[32,8,1024]{2,1,0:T(8,128)(2,1)S(1)}, u32[]{:S(2)}, u32[]{:S(2)}) %all-to-all-start) | async-done | bytes 524320 | tf_op jit(solution)/shard_map/all_to_all | solution.py:424
  125.2 5.2 %shard_map.94 = bf16[32,8,1024]{2,1,0:T(8,128)(2,1)} custom-call(bf16[32,8,1024]{2,1,0:T(8,128)(2,1)} %copy-done.13, f32[8,256,256]{2,1,0:T(8,128)} %shard_map.93.h_ref, f32[8,1]{1,0:T(8,128)} %copy.11.gain_ref, bf16[256,896]{1,0:T(8,128)(2,1)} %constant.111.clone.table_ref, f32[2,128,256]{2,1,0:T(8,128)} %constant.112.clone.twiddle_ref), custom_call_target="tpu_custom_call" | custom-call | flops 1342177280 | bytes 5242880 | tf_op jit(solution)/shard_map/pallas_call | solution.py:330
  130.4 5.6 %all-to-all-start.1 = ((bf16[32,8,1024]{2,1,0:T(8,128)(2,1)}), bf16[32,8,1024]{2,1,0:T(8,128)(2,1)S(1)}, u32[]{:S(2)}, u32[]{:S(2)}) async-start(bf16[32,8,1024]{2,1,0:T(8,128)(2,1)} %shard_map.94), calls=%async_computation.1 | async-start | bytes 1048576 | tf_op jit(solution)/shard_map/all_to_all | solution.py:426
  136.6 6.6 %shard_map.95.gate_ref = bf16[1024,256]{1,0:T(8,128)(2,1)} custom-call(s32[8]{0:T(128)} %compare_select_fusion.3.places, s32[1]{0:T(128)} %bitcast.20.even, bf16[1040,512]{1,0:T(8,128)(2,1)} %copy-done.2, bf16[1040,512]{1,0:T(8,128)(2,1)} %copy-done.5, bf16[1040,512]{1,0:T(8,128)(2,1)} %copy-done.7, bf16[1040,512]{1,0:T(8,128)(2,1)} %copy-done.6, ...), custom_call_target="tpu_custom_call" | custom-call | flops 2147483648 | bytes 12582912 | tf_op jit(solution)/shard_map/pallas_call | solution.py:231
  143.3 9.8 %all-to-all-done.1.conv_ref = bf16[32,8,1024]{2,1,0:T(8,128)(2,1)S(1)} async-done(((bf16[32,8,1024]{2,1,0:T(8,128)(2,1)}), bf16[32,8,1024]{2,1,0:T(8,128)(2,1)S(1)}, u32[]{:S(2)}, u32[]{:S(2)}) %all-to-all-start.1) | async-done | bytes 524320 | tf_op jit(solution)/shard_map/all_to_all | solution.py:426
  154.1 1.7 %shard_map.96 = bf16[1024,256]{1,0:T(8,128)(2,1)} custom-call(bf16[32,8,1024]{2,1,0:T(8,128)(2,1)S(1)} %all-to-all-done.1.conv_ref, bf16[1024,256]{1,0:T(8,128)(2,1)S(1)} %copy-done), custom_call_target="tpu_custom_call" | custom-call | flops 262144 | bytes 2097152 | tf_op jit(solution)/shard_map/pallas_call | solution.py:350
  (83 shorter events, 15.2 us)
Async XLA Ops:
  1.0 6.9 %collective-permute-start.3 = (bf16[128,384]{1,0:T(8,128)(2,1)S(1)}, bf16[128,384]{1,0:T(8,128)(2,1)S(1)}, u32[]{:S(2)}, u32[]{:S(2)}) collective-permute-start(bf16[128,384]{1,0:T(8,128)(2,1)S(1)} %pad_maximum_fusion.3), channel_id=1, source_target_pairs={{0,8},{8,0},{16,24},{24,16},{32,40},{40,32},{48,56},{56,48},{64,72... | collective-permute-start | bytes 294920 | tf_op jit(solution)/shard_map/ppermute | solution.py:377
  5.0 5.9 %collective-permute-start = (bf16[16,512]{1,0:T(8,128)(2,1)S(1)}, bf16[16,512]{1,0:T(8,128)(2,1)S(1)}, u32[]{:S(2)}, u32[]{:S(2)}) collective-permute-start(bf16[16,512]{1,0:T(8,128)(2,1)S(1)} %slice.37), channel_id=1, source_target_pairs={{0,8},{8,16},{16,24},{24,32},{32,40},{40,48},{48,56},{56,64},{64,7... | collective-permute-start | bytes 49160 | tf_op jit(solution)/shard_map/ppermute | solution.py:365
  7.9 8.5 %collective-permute-start.4 = (bf16[256,384]{1,0:T(8,128)(2,1)S(1)}, bf16[256,384]{1,0:T(8,128)(2,1)S(1)}, u32[]{:S(2)}, u32[]{:S(2)}) collective-permute-start(bf16[256,384]{1,0:T(8,128)(2,1)S(1)} %pad_maximum_fusion.1), channel_id=1, source_target_pairs={{0,16},{8,24},{16,0},{24,8},{32,48},{40,56},{48,32},{56,40},{64,80... | collective-permute-start | bytes 589832 | tf_op jit(solution)/shard_map/ppermute | solution.py:379
  10.9 36.8 %copy-start.2 = (bf16[1040,512]{1,0:T(8,128)(2,1)}, bf16[1040,512]{1,0:T(8,128)(2,1)S(1)}, u32[]{:S(2)}) copy-start(bf16[1040,512]{1,0:T(8,128)(2,1)S(1)} %constant_dynamic-update-slice_fusion.refs_0_) | copy-start | bytes 3194884
  10.9 25.9 %collective-permute-start.1 = (bf16[1040,512]{1,0:T(8,128)(2,1)S(1)}, bf16[1040,512]{1,0:T(8,128)(2,1)S(1)}, u32[]{:S(2)}, u32[]{:S(2)}) collective-permute-start(bf16[1040,512]{1,0:T(8,128)(2,1)S(1)} %constant_dynamic-update-slice_fusion.refs_0_), channel_id=1, source_target_pairs={{0,3},{1,0},{2,1},{3,2},{4,7},{5,4},{6,5},{7,6},{8,11},{9,8},{10,9... | collective-permute-start | bytes 3194888 | tf_op jit(solution)/shard_map/ppermute | solution.py:39
  16.5 55.9 %copy-start.14 = (f32[3,3,256]{2,1,0:T(4,128)S(1)}, f32[3,3,256]{2,1,0:T(4,128)}, u32[]{:S(2)}) copy-start(f32[3,3,256]{2,1,0:T(4,128)} %param.11) | copy-start | bytes 27652
  16.5 24.7 %collective-permute-start.5 = (bf16[1040,512]{1,0:T(8,128)(2,1)S(1)}, bf16[1040,512]{1,0:T(8,128)(2,1)S(1)}, u32[]{:S(2)}, u32[]{:S(2)}) collective-permute-start(bf16[1040,512]{1,0:T(8,128)(2,1)S(1)} %constant_dynamic-update-slice_fusion.refs_0_), channel_id=1, source_target_pairs={{0,4},{1,5},{2,6},{3,7},{4,0},{5,1},{6,2},{7,3},{8,12},{9,13},{10,... | collective-permute-start | bytes 3194888 | tf_op jit(solution)/shard_map/ppermute | solution.py:35
  16.6 25.9 %collective-permute-start.2 = (bf16[1040,512]{1,0:T(8,128)(2,1)S(1)}, bf16[1040,512]{1,0:T(8,128)(2,1)S(1)}, u32[]{:S(2)}, u32[]{:S(2)}) collective-permute-start(bf16[1040,512]{1,0:T(8,128)(2,1)S(1)} %constant_dynamic-update-slice_fusion.refs_0_), channel_id=1, source_target_pairs={{0,1},{1,2},{2,3},{3,0},{4,5},{5,6},{6,7},{7,4},{8,9},{9,10},{10,1... | collective-permute-start | bytes 3194888 | tf_op jit(solution)/shard_map/ppermute | solution.py:43
  17.2 22.8 %collective-permute-start.9 = (bf16[512,384]{1,0:T(8,128)(2,1)S(1)}, bf16[512,384]{1,0:T(8,128)(2,1)S(1)}, u32[]{:S(2)}, u32[]{:S(2)}) collective-permute-start(bf16[512,384]{1,0:T(8,128)(2,1)S(1)} %pad_maximum_fusion), channel_id=1, source_target_pairs={{0,224},{8,232},{16,240},{24,248},{32,0},{40,8},{48,16},{56,24},{6... | collective-permute-start | bytes 1179656 | tf_op jit(solution)/shard_map/ppermute | solution.py:47
  22.8 18.6 %collective-permute-start.10 = (bf16[512,384]{1,0:T(8,128)(2,1)S(1)}, bf16[512,384]{1,0:T(8,128)(2,1)S(1)}, u32[]{:S(2)}, u32[]{:S(2)}) collective-permute-start(bf16[512,384]{1,0:T(8,128)(2,1)S(1)} %pad_maximum_fusion), channel_id=1, source_target_pairs={{0,32},{8,40},{16,48},{24,56},{32,64},{40,72},{48,80},{56,88},{64,... | collective-permute-start | bytes 1179656 | tf_op jit(solution)/shard_map/ppermute | solution.py:51
  36.8 31.7 %copy-start.5 = (bf16[1040,512]{1,0:T(8,128)(2,1)}, bf16[1040,512]{1,0:T(8,128)(2,1)S(1)}, u32[]{:S(2)}) copy-start(bf16[1040,512]{1,0:T(8,128)(2,1)S(1)} %collective-permute-done.1.refs_1_) | copy-start | bytes 3194884
  36.9 31.4 %collective-permute-start.6 = (bf16[1040,512]{1,0:T(8,128)(2,1)S(1)}, bf16[1040,512]{1,0:T(8,128)(2,1)S(1)}, u32[]{:S(2)}, u32[]{:S(2)}) collective-permute-start(bf16[1040,512]{1,0:T(8,128)(2,1)S(1)} %collective-permute-done.1.refs_1_), channel_id=1, source_target_pairs={{0,3},{1,0},{2,1},{3,2},{4,7},{5,4},{6,5},{7,6},{8,11},{9,8},{10,9... | collective-permute-start | bytes 3194888 | tf_op jit(solution)/shard_map/ppermute | solution.py:39
  40.0 28.2 %collective-permute-start.8 = (bf16[1040,512]{1,0:T(8,128)(2,1)S(1)}, bf16[1040,512]{1,0:T(8,128)(2,1)S(1)}, u32[]{:S(2)}, u32[]{:S(2)}) collective-permute-start(bf16[1040,512]{1,0:T(8,128)(2,1)S(1)} %collective-permute-done.1.refs_1_), channel_id=1, source_target_pairs={{0,4},{1,5},{2,6},{3,7},{4,0},{5,1},{6,2},{7,3},{8,12},{9,13},{10,... | collective-permute-start | bytes 3194888 | tf_op jit(solution)/shard_map/ppermute | solution.py:35
  41.2 27.4 %copy-start.6 = (bf16[1040,512]{1,0:T(8,128)(2,1)}, bf16[1040,512]{1,0:T(8,128)(2,1)S(1)}, u32[]{:S(2)}) copy-start(bf16[1040,512]{1,0:T(8,128)(2,1)S(1)} %collective-permute-done.5.refs_3_) | copy-start | bytes 3194884
  41.2 27.0 %collective-permute-start.7 = (bf16[1040,512]{1,0:T(8,128)(2,1)S(1)}, bf16[1040,512]{1,0:T(8,128)(2,1)S(1)}, u32[]{:S(2)}, u32[]{:S(2)}) collective-permute-start(bf16[1040,512]{1,0:T(8,128)(2,1)S(1)} %collective-permute-done.5.refs_3_), channel_id=1, source_target_pairs={{0,1},{1,2},{2,3},{3,0},{4,5},{5,6},{6,7},{7,4},{8,9},{9,10},{10,1... | collective-permute-start | bytes 3194888 | tf_op jit(solution)/shard_map/ppermute | solution.py:43
  42.5 5.2 %copy-start.7 = (bf16[1040,512]{1,0:T(8,128)(2,1)}, bf16[1040,512]{1,0:T(8,128)(2,1)S(1)}, u32[]{:S(2)}) copy-start(bf16[1040,512]{1,0:T(8,128)(2,1)S(1)} %collective-permute-done.2.refs_2_) | copy-start | bytes 3194884
  42.5 12.6 %collective-permute-start.11 = (bf16[512,384]{1,0:T(8,128)(2,1)S(1)}, bf16[512,384]{1,0:T(8,128)(2,1)S(1)}, u32[]{:S(2)}, u32[]{:S(2)}) collective-permute-start(bf16[512,384]{1,0:T(8,128)(2,1)S(1)} %collective-permute-done.9), channel_id=1, source_target_pairs={{0,224},{8,232},{16,240},{24,248},{32,0},{40,8},{48,16},{56,24},{6... | collective-permute-start | bytes 1179656 | tf_op jit(solution)/shard_map/ppermute | solution.py:47
  47.7 10.6 %collective-permute-start.12 = (bf16[512,384]{1,0:T(8,128)(2,1)S(1)}, bf16[512,384]{1,0:T(8,128)(2,1)S(1)}, u32[]{:S(2)}, u32[]{:S(2)}) collective-permute-start(bf16[512,384]{1,0:T(8,128)(2,1)S(1)} %collective-permute-done.10), channel_id=1, source_target_pairs={{0,32},{8,40},{16,48},{24,56},{32,64},{40,72},{48,80},{56,88},{64,... | collective-permute-start | bytes 1179656 | tf_op jit(solution)/shard_map/ppermute | solution.py:51
  58.3 8.4 %collective-permute-start.13 = (bf16[512,384]{1,0:T(8,128)(2,1)S(1)}, bf16[512,384]{1,0:T(8,128)(2,1)S(1)}, u32[]{:S(2)}, u32[]{:S(2)}) collective-permute-start(bf16[512,384]{1,0:T(8,128)(2,1)S(1)} %collective-permute-done.11), channel_id=1, source_target_pairs={{0,224},{8,232},{16,240},{24,248},{32,0},{40,8},{48,16},{56,24},{6... | collective-permute-start | bytes 1179656 | tf_op jit(solution)/shard_map/ppermute | solution.py:47
  58.6 9.7 %collective-permute-start.14 = (bf16[512,384]{1,0:T(8,128)(2,1)S(1)}, bf16[512,384]{1,0:T(8,128)(2,1)S(1)}, u32[]{:S(2)}, u32[]{:S(2)}) collective-permute-start(bf16[512,384]{1,0:T(8,128)(2,1)S(1)} %collective-permute-done.12), channel_id=1, source_target_pairs={{0,32},{8,40},{16,48},{24,56},{32,64},{40,72},{48,80},{56,88},{64,... | collective-permute-start | bytes 1179656 | tf_op jit(solution)/shard_map/ppermute | solution.py:51
  68.2 4.1 %copy-start.8 = (bf16[1040,512]{1,0:T(8,128)(2,1)}, bf16[1040,512]{1,0:T(8,128)(2,1)S(1)}, u32[]{:S(2)}) copy-start(bf16[1040,512]{1,0:T(8,128)(2,1)S(1)} %collective-permute-done.6.refs_6_) | copy-start | bytes 3194884
  68.2 4.1 %copy-start.4 = (bf16[1040,512]{1,0:T(8,128)(2,1)}, bf16[1040,512]{1,0:T(8,128)(2,1)S(1)}, u32[]{:S(2)}) copy-start(bf16[1040,512]{1,0:T(8,128)(2,1)S(1)} %collective-permute-done.8.refs_4_) | copy-start | bytes 3194884
  69.3 14.3 %copy-start.1 = (bf16[7,512,384]{2,1,0:T(8,128)(2,1)}, bf16[7,512,384]{2,1,0:T(8,128)(2,1)S(1)}, u32[]{:S(2)}) copy-start(bf16[7,512,384]{2,1,0:T(8,128)(2,1)S(1)} %bitcast_dynamic-update-slice_fusion.refs_7_.refs_10_.refs_9_) | copy-start | bytes 8257540
  69.3 21.3 %collective-permute-start.19 = (bf16[7,512,384]{2,1,0:T(8,128)(2,1)S(1)}, bf16[7,512,384]{2,1,0:T(8,128)(2,1)}, u32[]{:S(2)}, u32[]{:S(2)}) collective-permute-start(bf16[7,512,384]{2,1,0:T(8,128)(2,1)S(1)} %bitcast_dynamic-update-slice_fusion.refs_7_.refs_10_.refs_9_), channel_id=1, source_target_pairs={{0,8},{8,0},{16,24},{24,16},{32,40},{40,32},{48,56},{56,48},{64,72... | collective-permute-start | bytes 8257544 | tf_op jit(solution)/shard_map/ppermute | solution.py:417
  72.5 7.6 %collective-permute-start.17 = (bf16[256,384]{1,0:T(8,128)(2,1)S(1)}, bf16[256,384]{1,0:T(8,128)(2,1)S(1)}, u32[]{:S(2)}, u32[]{:S(2)}) collective-permute-start(bf16[256,384]{1,0:T(8,128)(2,1)S(1)} %slice.45), channel_id=1, source_target_pairs={{0,224},{8,232},{16,240},{24,248},{32,0},{40,8},{48,16},{56,24},{6... | collective-permute-start | bytes 589832 | tf_op jit(solution)/shard_map/ppermute | solution.py:47
  74.3 7.4 %collective-permute-start.18 = (bf16[256,384]{1,0:T(8,128)(2,1)S(1)}, bf16[256,384]{1,0:T(8,128)(2,1)S(1)}, u32[]{:S(2)}, u32[]{:S(2)}) collective-permute-start(bf16[256,384]{1,0:T(8,128)(2,1)S(1)} %slice.46), channel_id=1, source_target_pairs={{0,32},{8,40},{16,48},{24,56},{32,64},{40,72},{48,80},{56,88},{64,... | collective-permute-start | bytes 589832 | tf_op jit(solution)/shard_map/ppermute | solution.py:51
  76.1 14.4 %collective-permute-start.16 = (bf16[528,512]{1,0:T(8,128)(2,1)S(1)}, bf16[528,512]{1,0:T(8,128)(2,1)S(1)}, u32[]{:S(2)}, u32[]{:S(2)}) collective-permute-start(bf16[528,512]{1,0:T(8,128)(2,1)S(1)} %slice.44), channel_id=1, source_target_pairs={{0,1},{1,2},{2,3},{3,0},{4,5},{5,6},{6,7},{7,4},{8,9},{9,10},{10,1... | collective-permute-start | bytes 1622024 | tf_op jit(solution)/shard_map/ppermute | solution.py:43
  78.5 12.0 %collective-permute-start.15 = (bf16[512,512]{1,0:T(8,128)(2,1)S(1)}, bf16[512,512]{1,0:T(8,128)(2,1)S(1)}, u32[]{:S(2)}, u32[]{:S(2)}) collective-permute-start(bf16[512,512]{1,0:T(8,128)(2,1)S(1)} %slice.43), channel_id=1, source_target_pairs={{0,3},{1,0},{2,1},{3,2},{4,7},{5,4},{6,5},{7,6},{8,11},{9,8},{10,9... | collective-permute-start | bytes 1572872 | tf_op jit(solution)/shard_map/ppermute | solution.py:39
  81.8 8.7 %collective-permute-start.20 = (bf16[512,384]{1,0:T(8,128)(2,1)S(1)}, bf16[512,384]{1,0:T(8,128)(2,1)S(1)}, u32[]{:S(2)}, u32[]{:S(2)}) collective-permute-start(bf16[512,384]{1,0:T(8,128)(2,1)S(1)} %constant_dynamic-update-slice_fusion.2.refs_8_.refs_11_.refs_10_), channel_id=1, source_target_pairs={{0,8},{8,0},{16,24},{24,16},{32,40},{40,32},{48,56},{56,48},{64,72... | collective-permute-start | bytes 1179656 | tf_op jit(solution)/shard_map/ppermute | solution.py:417
  99.5 10.4 %copy-start.15 = (f32[8]{0:T(128)S(1)}, f32[8]{0:T(128)}, u32[]{:S(2)}) copy-start(f32[8]{0:T(128)} %param.13) | copy-start | bytes 100
  99.5 24.9 %all-to-all-start = ((bf16[32,8,1024]{2,1,0:T(8,128)(2,1)}), bf16[32,8,1024]{2,1,0:T(8,128)(2,1)S(1)}, u32[]{:S(2)}, u32[]{:S(2)}) async-start(bf16[32,8,1024]{2,1,0:T(8,128)(2,1)} %shard_map.92), calls=%async_computation | async-start | bytes 1048576 | tf_op jit(solution)/shard_map/all_to_all | solution.py:424
  130.4 22.6 %all-to-all-start.1 = ((bf16[32,8,1024]{2,1,0:T(8,128)(2,1)}), bf16[32,8,1024]{2,1,0:T(8,128)(2,1)S(1)}, u32[]{:S(2)}, u32[]{:S(2)}) async-start(bf16[32,8,1024]{2,1,0:T(8,128)(2,1)} %shard_map.94), calls=%async_computation.1 | async-start | bytes 1048576 | tf_op jit(solution)/shard_map/all_to_all | solution.py:426
  (7 other events, 7.5 us)

commit v4 on v3

--- a/solution.py
+++ b/solution.py
@@ -143,22 +143,25 @@
 
 
 def partial_kernel(sizes, places, *refs):
-    units, (near, far, out_ref, a_buf, b_buf, w_buf, sems) = grouped(refs, sizes)
-    sum_units(places, 7, units, [((near, far), KV)], lambda w: w[0], out_ref, a_buf, b_buf, [w_buf], sems)
-
-
-def partial_products(places, units, w):
+    units, refs = grouped(refs, sizes)
+    own0, own1, sib0, sib1, out_ref, a_buf, b_buf, own_buf, sib_buf, sems = refs
+    weights = [((own0, own1), KV), ((sib0, sib1), KV)]
+    joined = lambda w: jnp.concatenate(w, 1)
+    sum_units(places, 7, units, weights, joined, out_ref, a_buf, b_buf, [own_buf, sib_buf], sems)
+
+
+def partial_products(places, units, own, sib):
     return pl.pallas_call(
         functools.partial(partial_kernel, [len(unit) for unit in units]),
-        out_shape=jax.ShapeDtypeStruct((HALO + ROWS, 256), F32),
-        in_specs=[SMEM] + [ANY] * (len(flat(units)) + 2),
+        out_shape=jax.ShapeDtypeStruct((HALO + ROWS, 512), F32),
+        in_specs=[SMEM] + [ANY] * (len(flat(units)) + 4),
         out_specs=pl.BlockSpec(memory_space=pltpu.VMEM),
-        scratch_shapes=unit_scratch(7, [256]),
+        scratch_shapes=unit_scratch(7, [256, 256]),
         compiler_params=pltpu.CompilerParams(vmem_limit_bytes=VMEM),
         cost_estimate=pl.CostEstimate(
-            flops=2 * 7 * 1024 * 512 * 256, bytes_accessed=11 * MIB, transcendentals=0
+            flops=2 * 7 * 1024 * 512 * 512, bytes_accessed=13 * MIB, transcendentals=0
         ),
-    )(places, *flat(units), *w)
+    )(places, *flat(units), *own, *sib)
 
 
 def filtered(branch, taps, start, size):
@@ -172,44 +175,48 @@
     branch[...] = branch[...].astype(BF16).astype(F32)
 
 
-def gated_kernel(sizes, places, *refs):
-    units, refs = grouped(refs, sizes)
-    acc_ref, own0, own1, sib0, sib1, taps_ref, out_ref, a_buf, b_buf, w_buf, sems = refs[:11]
-    own_buf, own_sems, mine, theirs = refs[11:]
+def gated_kernel(places, a_ref, b_ref, acc_ref, own0, own1, sib0, sib1, taps_ref, out_ref, *scratch):
+    a_buf, b_buf, own_buf, sib_buf, total, sems = scratch
     copies = [
-        pltpu.make_async_copy(acc_ref, mine, own_sems.at[0]),
-        WeightCopy(places[7], (own0, own1), KV, own_buf, own_sems.at[1]),
+        WeightCopy(places[7], (own0, own1), KV, own_buf, sems.at[0]),
+        WeightCopy(places[7], (sib0, sib1), KV, sib_buf, sems.at[1]),
+        pltpu.make_async_copy(a_ref, a_buf, sems.at[2]),
+        pltpu.make_async_copy(b_ref, b_buf, sems.at[3]),
+        pltpu.make_async_copy(acc_ref, total, sems.at[4]),
     ]
-    sum_units(places, 8, units, [((sib0, sib1), KV)], lambda w: w[0], theirs, a_buf, b_buf, [w_buf], sems, copies)
+    for copy in copies:
+        copy.start()
     for copy in copies:
         copy.wait()
-    add_products(mine, False, a_buf[7], b_buf[7], own_buf[...])
-    rounded(mine)
-    rounded(theirs)
+    w = jnp.concatenate([own_buf[...], sib_buf[...]], 1)
+    add_products(total, False, a_buf[...], b_buf[...], w)
+    rounded(total)
+    taps = jnp.concatenate([taps_ref[0], taps_ref[1]], 1)
     for r in range(ROWS // 256):
-        a = filtered(mine, taps_ref[0], r * 256, 256)
-        b = filtered(theirs, taps_ref[1], r * 256, 256)
-        out_ref[:, :, r * 256 : r * 256 + 256] = (a * b).T.reshape(32, 8, 256).astype(BF16)
-
-
-def gated_input(places, units, acc, own, sib, taps):
-    return pl.pallas_call(
-        functools.partial(gated_kernel, [len(unit) for unit in units]),
+        mixed = filtered(total, taps, r * 256, 256)
+        product = mixed[:, :256] * mixed[:, 256:]
+        out_ref[:, :, r * 256 : r * 256 + 256] = product.T.reshape(32, 8, 256).astype(BF16)
+
+
+def gated_input(places, last, acc, own, sib, taps):
+    return pl.pallas_call(
+        gated_kernel,
         out_shape=jax.ShapeDtypeStruct((32, 8, ROWS), BF16),
-        in_specs=[SMEM] + [ANY] * (len(flat(units)) + 5) + vmem_specs(1),
+        in_specs=[SMEM] + [ANY] * 7 + vmem_specs(1),
         out_specs=pl.BlockSpec(memory_space=pltpu.VMEM),
-        scratch_shapes=unit_scratch(8, [256])
-        + [
+        scratch_shapes=[
+            pltpu.VMEM((HALF, 512), BF16),
+            pltpu.VMEM((HALF + HALO, 512), BF16),
             pltpu.VMEM((512, 256), BF16),
-            pltpu.SemaphoreType.DMA((2,)),
-            pltpu.VMEM((HALO + ROWS, 256), F32),
-            pltpu.VMEM((HALO + ROWS, 256), F32),
+            pltpu.VMEM((512, 256), BF16),
+            pltpu.VMEM((HALO + ROWS, 512), F32),
+            pltpu.SemaphoreType.DMA((5,)),
         ],
         compiler_params=pltpu.CompilerParams(vmem_limit_bytes=VMEM),
         cost_estimate=pl.CostEstimate(
-            flops=2 * 9 * 1024 * 512 * 256, bytes_accessed=13 * MIB, transcendentals=0
+            flops=2 * 1024 * 512 * 512, bytes_accessed=5 * MIB, transcendentals=0
         ),
-    )(places, *flat(units), acc, *own, *sib, taps)
+    )(places, *last, acc, *own, *sib, taps)
 
 
 def query_kernel(sizes, places, even, *refs):
@@ -416,10 +423,10 @@
     places = jnp.where(places == 4, 7, jnp.where(places > 4, places - 1, places))
     sib = tuple(lax.ppermute(w, "ctx", OTHER_CORE) for w in own)
     units = ((a0,), (ap,), (am,), (b0,), (bp,), (bm,), (a2,))
-    own_acc = partial_products(places, units, own)
+    acc = partial_products(places, units, own, sib)
     taps = short_taps.transpose(1, 0, 2)
     taps_kv = jnp.where(even, taps[1:3], taps[2:0:-1])
-    gated = gated_input(places, units + (b2,), own_acc, own, sib, taps_kv)
+    gated = gated_input(places, b2, acc, own, sib, taps_kv)
 
     owned = lax.all_to_all(gated, "ctx", 0, 0)
     convolved = convolve(owned, spectrum, skip_gain[:, None], packed, twiddle)

time: 157 us -> 164 us (1.045)
  waiting for transfers between devices: 58.5 us -> 64.2 us
    ppermute x4, waiting for transfers between devices: 14.2 us -> 17.2 us  [from_above(): return lax.ppermute(x, 'ctx', FROM_ABOVE)]
    pallas_call x1, Pallas kernels: 7.85 us -> 5 us  [gated_input(): pl.pallas_call(gated_kernel, out_shape=jax.ShapeDtypeStruct((32, 8, ROWS)...]
    pallas_call x1, Pallas kernels: 5.93 us -> 8.64 us  [partial_products(): pl.pallas_call(functools.partial(partial_kernel, [len(unit) for unit in u...]
  transfers between devices with their start and end apart: 23 -> 23, of which waited for: 12 -> 14; matrix products, arithmetic and copies ran while one was open for 6% -> 6% of each run, Pallas kernels for 12% -> 13%
where the time goes in v4:
time: 164 us; the launch traced here: 162 us
  waiting for transfers between devices  64.2 us (39%)
  starting transfers between devices  48.6 us (30%)
  Pallas kernels  32.6 us (20%)
  local copies, waits for them, and re-layouts  13.3 us (8%)
  other arithmetic  3.11 us (2%)
    ppermute x4, waiting for transfers between devices, from_above(): return lax.ppermute(x, 'ctx', FROM_ABOVE)  17.2 us
    ppermute x3, waiting for transfers between devices, from_up(): return lax.ppermute(x, 'tp', FROM_UP)  15.1 us
    ppermute x4, starting transfers between devices, from_above(): return lax.ppermute(x, 'ctx', FROM_ABOVE)  12.9 us
    all_to_all x1, waiting for transfers between devices, body(): returned = lax.all_to_all(convolved, 'ctx', 0, 0)  9.81 us
    all_to_all x1, waiting for transfers between devices, body(): owned = lax.all_to_all(gated, 'ctx', 0, 0)  9.59 us
    pallas_call x1, Pallas kernels, partial_products(): pl.pallas_call(functools.partial(partial_kernel, [len(unit) for unit in u...  8.64 us
    ppermute x3, starting transfers between devices, from_up(): return lax.ppermute(x, 'tp', FROM_UP)  8.45 us
    unnamed x41, local copies, waits for them, and re-layouts  8.34 us
  transfers between devices with their start and end apart: 23, of which 14 were waited for; matrix products, arithmetic and copies ran while one was open for 6% of the time, Pallas kernels for 13%

profile of v4, /device:TPU:1, one launch (start us, length us, event | category | flops | bytes accessed | tf_op | source)
XLA Modules:
  0.0 162.3 jit_solution(8194067596885675322)
XLA Ops:
  1.0 3.3 %collective-permute-start.3 = (bf16[128,384]{1,0:T(8,128)(2,1)S(1)}, bf16[128,384]{1,0:T(8,128)(2,1)S(1)}, u32[]{:S(2)}, u32[]{:S(2)}) collective-permute-start(bf16[128,384]{1,0:T(8,128)(2,1)S(1)} %pad_maximum_fusion.3), channel_id=1, source_target_pairs={{0,8},{8,0},{16,24},{24,16},{32,40},{40,32},{48,56},{56,48},{64,72... | collective-permute-start | bytes 294920 | tf_op jit(solution)/shard_map/ppermute | solution.py:384
  5.0 2.8 %collective-permute-start = (bf16[16,512]{1,0:T(8,128)(2,1)S(1)}, bf16[16,512]{1,0:T(8,128)(2,1)S(1)}, u32[]{:S(2)}, u32[]{:S(2)}) collective-permute-start(bf16[16,512]{1,0:T(8,128)(2,1)S(1)} %slice.37), channel_id=1, source_target_pairs={{0,8},{8,16},{16,24},{24,32},{32,40},{40,48},{48,56},{56,64},{64,7... | collective-permute-start | bytes 49160 | tf_op jit(solution)/shard_map/ppermute | solution.py:372
  7.9 1.7 %collective-permute-start.4 = (bf16[256,384]{1,0:T(8,128)(2,1)S(1)}, bf16[256,384]{1,0:T(8,128)(2,1)S(1)}, u32[]{:S(2)}, u32[]{:S(2)}) collective-permute-start(bf16[256,384]{1,0:T(8,128)(2,1)S(1)} %pad_maximum_fusion.1), channel_id=1, source_target_pairs={{0,16},{8,24},{16,0},{24,8},{32,48},{40,56},{48,32},{56,40},{64,80... | collective-permute-start | bytes 589832 | tf_op jit(solution)/shard_map/ppermute | solution.py:386
  9.6 1.3 constant_dynamic-update-slice_fusion.1
  10.9 2.8 %collective-permute-start.1 = (bf16[1040,512]{1,0:T(8,128)(2,1)S(1)}, bf16[1040,512]{1,0:T(8,128)(2,1)S(1)}, u32[]{:S(2)}, u32[]{:S(2)}) collective-permute-start(bf16[1040,512]{1,0:T(8,128)(2,1)S(1)} %constant_dynamic-update-slice_fusion.refs_0_), channel_id=1, source_target_pairs={{0,3},{1,0},{2,1},{3,2},{4,7},{5,4},{6,5},{7,6},{8,11},{9,8},{10,9... | collective-permute-start | bytes 3194888 | tf_op jit(solution)/shard_map/ppermute | solution.py:39
  13.8 2.6 %collective-permute-done.4 = bf16[256,384]{1,0:T(8,128)(2,1)S(1)} collective-permute-done((bf16[256,384]{1,0:T(8,128)(2,1)S(1)}, bf16[256,384]{1,0:T(8,128)(2,1)S(1)}, u32[]{:S(2)}, u32[]{:S(2)}) %collective-permute-start.4) | collective-permute-done | bytes 196640 | tf_op jit(solution)/shard_map/ppermute | solution.py:386
  17.2 5.6 %collective-permute-start.8 = (bf16[512,384]{1,0:T(8,128)(2,1)S(1)}, bf16[512,384]{1,0:T(8,128)(2,1)S(1)}, u32[]{:S(2)}, u32[]{:S(2)}) collective-permute-start(bf16[512,384]{1,0:T(8,128)(2,1)S(1)} %pad_maximum_fusion), channel_id=1, source_target_pairs={{0,224},{8,232},{16,240},{24,248},{32,0},{40,8},{48,16},{56,24},{6... | collective-permute-start | bytes 1179656 | tf_op jit(solution)/shard_map/ppermute | solution.py:47
  22.8 14.1 %collective-permute-done.1.refs_1_ = bf16[1040,512]{1,0:T(8,128)(2,1)S(1)} collective-permute-done((bf16[1040,512]{1,0:T(8,128)(2,1)S(1)}, bf16[1040,512]{1,0:T(8,128)(2,1)S(1)}, u32[]{:S(2)}, u32[]{:S(2)}) %collective-permute-start.1) | collective-permute-done | bytes 1064992 | tf_op jit(solution)/shard_map/ppermute | solution.py:39
  36.9 3.2 %collective-permute-start.2 = (bf16[1040,512]{1,0:T(8,128)(2,1)S(1)}, bf16[1040,512]{1,0:T(8,128)(2,1)S(1)}, u32[]{:S(2)}, u32[]{:S(2)}) collective-permute-start(bf16[1040,512]{1,0:T(8,128)(2,1)S(1)} %collective-permute-done.1.refs_1_), channel_id=1, source_target_pairs={{0,3},{1,0},{2,1},{3,2},{4,7},{5,4},{6,5},{7,6},{8,11},{9,8},{10,9... | collective-permute-start | bytes 3194888 | tf_op jit(solution)/shard_map/ppermute | solution.py:39
  42.5 5.2 %collective-permute-start.11 = (bf16[512,384]{1,0:T(8,128)(2,1)S(1)}, bf16[512,384]{1,0:T(8,128)(2,1)S(1)}, u32[]{:S(2)}, u32[]{:S(2)}) collective-permute-start(bf16[512,384]{1,0:T(8,128)(2,1)S(1)} %collective-permute-done.8), channel_id=1, source_target_pairs={{0,224},{8,232},{16,240},{24,248},{32,0},{40,8},{48,16},{56,24},{6... | collective-permute-start | bytes 1179656 | tf_op jit(solution)/shard_map/ppermute | solution.py:47
  47.7 7.4 %collective-permute-done.11 = bf16[512,384]{1,0:T(8,128)(2,1)S(1)} collective-permute-done((bf16[512,384]{1,0:T(8,128)(2,1)S(1)}, bf16[512,384]{1,0:T(8,128)(2,1)S(1)}, u32[]{:S(2)}, u32[]{:S(2)}) %collective-permute-start.11) | collective-permute-done | bytes 393248 | tf_op jit(solution)/shard_map/ppermute | solution.py:47
  55.1 3.1 %collective-permute-done.12 = bf16[512,384]{1,0:T(8,128)(2,1)S(1)} collective-permute-done((bf16[512,384]{1,0:T(8,128)(2,1)S(1)}, bf16[512,384]{1,0:T(8,128)(2,1)S(1)}, u32[]{:S(2)}, u32[]{:S(2)}) %collective-permute-start.12) | collective-permute-done | bytes 393248 | tf_op jit(solution)/shard_map/ppermute | solution.py:51
  59.9 6.8 %collective-permute-done.13 = bf16[512,384]{1,0:T(8,128)(2,1)S(1)} collective-permute-done((bf16[512,384]{1,0:T(8,128)(2,1)S(1)}, bf16[512,384]{1,0:T(8,128)(2,1)S(1)}, u32[]{:S(2)}, u32[]{:S(2)}) %collective-permute-start.13) | collective-permute-done | bytes 393248 | tf_op jit(solution)/shard_map/ppermute | solution.py:47
  66.7 1.5 collective-permute-done.14
  69.3 3.1 %collective-permute-start.19 = (bf16[7,512,384]{2,1,0:T(8,128)(2,1)S(1)}, bf16[7,512,384]{2,1,0:T(8,128)(2,1)}, u32[]{:S(2)}, u32[]{:S(2)}) collective-permute-start(bf16[7,512,384]{2,1,0:T(8,128)(2,1)S(1)} %bitcast_dynamic-update-slice_fusion.refs_7_.own0.refs_9_), channel_id=1, source_target_pairs={{0,8},{8,0},{16,24},{24,16},{32,40},{40,32},{48,56},{56,48},{64,72... | collective-permute-start | bytes 8257544 | tf_op jit(solution)/shard_map/ppermute | solution.py:424
  72.4 1.9 %collective-permute-start.17 = (bf16[256,384]{1,0:T(8,128)(2,1)S(1)}, bf16[256,384]{1,0:T(8,128)(2,1)S(1)}, u32[]{:S(2)}, u32[]{:S(2)}) collective-permute-start(bf16[256,384]{1,0:T(8,128)(2,1)S(1)} %slice.45), channel_id=1, source_target_pairs={{0,224},{8,232},{16,240},{24,248},{32,0},{40,8},{48,16},{56,24},{6... | collective-permute-start | bytes 589832 | tf_op jit(solution)/shard_map/ppermute | solution.py:47
  75.8 2.9 %collective-permute-done.17 = bf16[256,384]{1,0:T(8,128)(2,1)S(1)} collective-permute-done((bf16[256,384]{1,0:T(8,128)(2,1)S(1)}, bf16[256,384]{1,0:T(8,128)(2,1)S(1)}, u32[]{:S(2)}, u32[]{:S(2)}) %collective-permute-start.17) | collective-permute-done | bytes 196640 | tf_op jit(solution)/shard_map/ppermute | solution.py:47
  78.8 3.0 %collective-permute-done.18 = bf16[256,384]{1,0:T(8,128)(2,1)S(1)} collective-permute-done((bf16[256,384]{1,0:T(8,128)(2,1)S(1)}, bf16[256,384]{1,0:T(8,128)(2,1)S(1)}, u32[]{:S(2)}, u32[]{:S(2)}) %collective-permute-start.18) | collective-permute-done | bytes 196640 | tf_op jit(solution)/shard_map/ppermute | solution.py:51
  81.8 1.2 collective-permute-start.20
  83.0 1.4 reverse_select_fusion.taps_ref
  86.9 2.5 %collective-permute-start.15 = (bf16[512,512]{1,0:T(8,128)(2,1)S(1)}, bf16[512,512]{1,0:T(8,128)(2,1)S(1)}, u32[]{:S(2)}, u32[]{:S(2)}) collective-permute-start(bf16[512,512]{1,0:T(8,128)(2,1)S(1)} %slice.43), channel_id=1, source_target_pairs={{0,3},{1,0},{2,1},{3,2},{4,7},{5,4},{6,5},{7,6},{8,11},{9,8},{10,9... | collective-permute-start | bytes 1572872 | tf_op jit(solution)/shard_map/ppermute | solution.py:39
  90.7 8.6 %shard_map.91.acc_ref = f32[1040,512]{1,0:T(8,128)} custom-call(s32[8]{0:T(128)} %compare_select_fusion.3.places, bf16[1040,512]{1,0:T(8,128)(2,1)} %copy-done.2, bf16[1040,512]{1,0:T(8,128)(2,1)} %copy-done.6, bf16[1040,512]{1,0:T(8,128)(2,1)} %copy-done.8, bf16[1040,512]{1,0:T(8,128)(2,1)} %copy-done.7, bf16[1040,512]{1,0:T(8,128)(2,1)} %copy-done.4, ...), custom_call_target="tpu_custom_call" | custom-call | flops 3758096384 | bytes 13631488 | tf_op jit(solution)/shard_map/pallas_call | solution.py:154
  102.0 5.0 %shard_map.92 = bf16[32,8,1024]{2,1,0:T(8,128)(2,1)} custom-call(s32[8]{0:T(128)} %compare_select_fusion.3.places, bf16[512,512]{1,0:T(8,128)(2,1)} %copy-done.12, bf16[528,512]{1,0:T(8,128)(2,1)} %copy-done.11, f32[1040,512]{1,0:T(8,128)} %shard_map.91.acc_ref, bf16[7,512,384]{2,1,0:T(8,128)(2,1)} %copy-done.1, bf16[512,384]{1,0:T(8,128)(2,1)} %copy-done.5, ...), custom_call_target="tpu_custom_call" | custom-call | flops 536870912 | bytes 5242880 | tf_op jit(solution)/shard_map/pallas_call | solution.py:202
  107.0 6.8 %all-to-all-start = ((bf16[32,8,1024]{2,1,0:T(8,128)(2,1)}), bf16[32,8,1024]{2,1,0:T(8,128)(2,1)S(1)}, u32[]{:S(2)}, u32[]{:S(2)}) async-start(bf16[32,8,1024]{2,1,0:T(8,128)(2,1)} %shard_map.92), calls=%async_computation | async-start | bytes 1048576 | tf_op jit(solution)/shard_map/all_to_all | solution.py:431
  113.9 1.3 copy.15
  115.8 5.5 %shard_map.93.h_ref = f32[8,256,256]{2,1,0:T(8,128)} custom-call(f32[8,128,256]{2,1,0:T(8,128)} %bitcast.40, bf16[2,256,128]{2,1,0:T(8,128)(2,1)} %constant.109.clone.first_ref, bf16[2,256,512]{2,1,0:T(8,128)(2,1)} %constant.110.clone.turn_ref, f32[2,128,256]{2,1,0:T(8,128)} %constant.112.clone.twiddle_ref), custom_call_target="tpu_custom_call" | custom-call | flops 2013265920 | bytes 5242880 | tf_op jit(solution)/shard_map/pallas_call | solution.py:300
  121.3 9.6 %all-to-all-done.x_ref = bf16[32,8,1024]{2,1,0:T(8,128)(2,1)S(1)} async-done(((bf16[32,8,1024]{2,1,0:T(8,128)(2,1)}), bf16[32,8,1024]{2,1,0:T(8,128)(2,1)S(1)}, u32[]{:S(2)}, u32[]{:S(2)}) %all-to-all-start) | async-done | bytes 524320 | tf_op jit(solution)/shard_map/all_to_all | solution.py:431
  131.7 5.2 %shard_map.94 = bf16[32,8,1024]{2,1,0:T(8,128)(2,1)} custom-call(bf16[32,8,1024]{2,1,0:T(8,128)(2,1)} %copy-done.14, f32[8,256,256]{2,1,0:T(8,128)} %shard_map.93.h_ref, f32[8,1]{1,0:T(8,128)} %copy.11.gain_ref, bf16[256,896]{1,0:T(8,128)(2,1)} %constant.111.clone.table_ref, f32[2,128,256]{2,1,0:T(8,128)} %constant.112.clone.twiddle_ref), custom_call_target="tpu_custom_call" | custom-call | flops 1342177280 | bytes 5242880 | tf_op jit(solution)/shard_map/pallas_call | solution.py:337
  136.9 5.6 %all-to-all-start.1 = ((bf16[32,8,1024]{2,1,0:T(8,128)(2,1)}), bf16[32,8,1024]{2,1,0:T(8,128)(2,1)S(1)}, u32[]{:S(2)}, u32[]{:S(2)}) async-start(bf16[32,8,1024]{2,1,0:T(8,128)(2,1)} %shard_map.94), calls=%async_computation.1 | async-start | bytes 1048576 | tf_op jit(solution)/shard_map/all_to_all | solution.py:433
  143.2 6.6 %shard_map.95.gate_ref = bf16[1024,256]{1,0:T(8,128)(2,1)} custom-call(s32[8]{0:T(128)} %compare_select_fusion.3.places, s32[1]{0:T(128)} %bitcast.20.even, bf16[1040,512]{1,0:T(8,128)(2,1)} %copy-done.2, bf16[1040,512]{1,0:T(8,128)(2,1)} %copy-done.6, bf16[1040,512]{1,0:T(8,128)(2,1)} %copy-done.8, bf16[1040,512]{1,0:T(8,128)(2,1)} %copy-done.7, ...), custom_call_target="tpu_custom_call" | custom-call | flops 2147483648 | bytes 12582912 | tf_op jit(solution)/shard_map/pallas_call | solution.py:238
  149.8 9.8 %all-to-all-done.1.conv_ref = bf16[32,8,1024]{2,1,0:T(8,128)(2,1)S(1)} async-done(((bf16[32,8,1024]{2,1,0:T(8,128)(2,1)}), bf16[32,8,1024]{2,1,0:T(8,128)(2,1)S(1)}, u32[]{:S(2)}, u32[]{:S(2)}) %all-to-all-start.1) | async-done | bytes 524320 | tf_op jit(solution)/shard_map/all_to_all | solution.py:433
  160.6 1.7 %shard_map.96 = bf16[1024,256]{1,0:T(8,128)(2,1)} custom-call(bf16[32,8,1024]{2,1,0:T(8,128)(2,1)S(1)} %all-to-all-done.1.conv_ref, bf16[1024,256]{1,0:T(8,128)(2,1)S(1)} %copy-done), custom_call_target="tpu_custom_call" | custom-call | flops 262144 | bytes 2097152 | tf_op jit(solution)/shard_map/pallas_call | solution.py:357
  (83 shorter events, 18.8 us)
Async XLA Ops:
  1.0 6.9 %collective-permute-start.3 = (bf16[128,384]{1,0:T(8,128)(2,1)S(1)}, bf16[128,384]{1,0:T(8,128)(2,1)S(1)}, u32[]{:S(2)}, u32[]{:S(2)}) collective-permute-start(bf16[128,384]{1,0:T(8,128)(2,1)S(1)} %pad_maximum_fusion.3), channel_id=1, source_target_pairs={{0,8},{8,0},{16,24},{24,16},{32,40},{40,32},{48,56},{56,48},{64,72... | collective-permute-start | bytes 294920 | tf_op jit(solution)/shard_map/ppermute | solution.py:384
  5.0 5.9 %collective-permute-start = (bf16[16,512]{1,0:T(8,128)(2,1)S(1)}, bf16[16,512]{1,0:T(8,128)(2,1)S(1)}, u32[]{:S(2)}, u32[]{:S(2)}) collective-permute-start(bf16[16,512]{1,0:T(8,128)(2,1)S(1)} %slice.37), channel_id=1, source_target_pairs={{0,8},{8,16},{16,24},{24,32},{32,40},{40,48},{48,56},{56,64},{64,7... | collective-permute-start | bytes 49160 | tf_op jit(solution)/shard_map/ppermute | solution.py:372
  7.9 8.5 %collective-permute-start.4 = (bf16[256,384]{1,0:T(8,128)(2,1)S(1)}, bf16[256,384]{1,0:T(8,128)(2,1)S(1)}, u32[]{:S(2)}, u32[]{:S(2)}) collective-permute-start(bf16[256,384]{1,0:T(8,128)(2,1)S(1)} %pad_maximum_fusion.1), channel_id=1, source_target_pairs={{0,16},{8,24},{16,0},{24,8},{32,48},{40,56},{48,32},{56,40},{64,80... | collective-permute-start | bytes 589832 | tf_op jit(solution)/shard_map/ppermute | solution.py:386
  10.9 36.8 %copy-start.2 = (bf16[1040,512]{1,0:T(8,128)(2,1)}, bf16[1040,512]{1,0:T(8,128)(2,1)S(1)}, u32[]{:S(2)}) copy-start(bf16[1040,512]{1,0:T(8,128)(2,1)S(1)} %constant_dynamic-update-slice_fusion.refs_0_) | copy-start | bytes 3194884
  10.9 25.9 %collective-permute-start.1 = (bf16[1040,512]{1,0:T(8,128)(2,1)S(1)}, bf16[1040,512]{1,0:T(8,128)(2,1)S(1)}, u32[]{:S(2)}, u32[]{:S(2)}) collective-permute-start(bf16[1040,512]{1,0:T(8,128)(2,1)S(1)} %constant_dynamic-update-slice_fusion.refs_0_), channel_id=1, source_target_pairs={{0,3},{1,0},{2,1},{3,2},{4,7},{5,4},{6,5},{7,6},{8,11},{9,8},{10,9... | collective-permute-start | bytes 3194888 | tf_op jit(solution)/shard_map/ppermute | solution.py:39
  16.5 24.7 %collective-permute-start.5 = (bf16[1040,512]{1,0:T(8,128)(2,1)S(1)}, bf16[1040,512]{1,0:T(8,128)(2,1)S(1)}, u32[]{:S(2)}, u32[]{:S(2)}) collective-permute-start(bf16[1040,512]{1,0:T(8,128)(2,1)S(1)} %constant_dynamic-update-slice_fusion.refs_0_), channel_id=1, source_target_pairs={{0,4},{1,5},{2,6},{3,7},{4,0},{5,1},{6,2},{7,3},{8,12},{9,13},{10,... | collective-permute-start | bytes 3194888 | tf_op jit(solution)/shard_map/ppermute | solution.py:35
  16.6 25.9 %collective-permute-start.10 = (bf16[1040,512]{1,0:T(8,128)(2,1)S(1)}, bf16[1040,512]{1,0:T(8,128)(2,1)S(1)}, u32[]{:S(2)}, u32[]{:S(2)}) collective-permute-start(bf16[1040,512]{1,0:T(8,128)(2,1)S(1)} %constant_dynamic-update-slice_fusion.refs_0_), channel_id=1, source_target_pairs={{0,1},{1,2},{2,3},{3,0},{4,5},{5,6},{6,7},{7,4},{8,9},{9,10},{10,1... | collective-permute-start | bytes 3194888 | tf_op jit(solution)/shard_map/ppermute | solution.py:43
  17.2 22.9 %collective-permute-start.8 = (bf16[512,384]{1,0:T(8,128)(2,1)S(1)}, bf16[512,384]{1,0:T(8,128)(2,1)S(1)}, u32[]{:S(2)}, u32[]{:S(2)}) collective-permute-start(bf16[512,384]{1,0:T(8,128)(2,1)S(1)} %pad_maximum_fusion), channel_id=1, source_target_pairs={{0,224},{8,232},{16,240},{24,248},{32,0},{40,8},{48,16},{56,24},{6... | collective-permute-start | bytes 1179656 | tf_op jit(solution)/shard_map/ppermute | solution.py:47
  22.7 18.6 %collective-permute-start.9 = (bf16[512,384]{1,0:T(8,128)(2,1)S(1)}, bf16[512,384]{1,0:T(8,128)(2,1)S(1)}, u32[]{:S(2)}, u32[]{:S(2)}) collective-permute-start(bf16[512,384]{1,0:T(8,128)(2,1)S(1)} %pad_maximum_fusion), channel_id=1, source_target_pairs={{0,32},{8,40},{16,48},{24,56},{32,64},{40,72},{48,80},{56,88},{64,... | collective-permute-start | bytes 1179656 | tf_op jit(solution)/shard_map/ppermute | solution.py:51
  36.8 31.7 %copy-start.6 = (bf16[1040,512]{1,0:T(8,128)(2,1)}, bf16[1040,512]{1,0:T(8,128)(2,1)S(1)}, u32[]{:S(2)}) copy-start(bf16[1040,512]{1,0:T(8,128)(2,1)S(1)} %collective-permute-done.1.refs_1_) | copy-start | bytes 3194884
  36.9 31.4 %collective-permute-start.2 = (bf16[1040,512]{1,0:T(8,128)(2,1)S(1)}, bf16[1040,512]{1,0:T(8,128)(2,1)S(1)}, u32[]{:S(2)}, u32[]{:S(2)}) collective-permute-start(bf16[1040,512]{1,0:T(8,128)(2,1)S(1)} %collective-permute-done.1.refs_1_), channel_id=1, source_target_pairs={{0,3},{1,0},{2,1},{3,2},{4,7},{5,4},{6,5},{7,6},{8,11},{9,8},{10,9... | collective-permute-start | bytes 3194888 | tf_op jit(solution)/shard_map/ppermute | solution.py:39
  40.0 28.2 %collective-permute-start.7 = (bf16[1040,512]{1,0:T(8,128)(2,1)S(1)}, bf16[1040,512]{1,0:T(8,128)(2,1)S(1)}, u32[]{:S(2)}, u32[]{:S(2)}) collective-permute-start(bf16[1040,512]{1,0:T(8,128)(2,1)S(1)} %collective-permute-done.1.refs_1_), channel_id=1, source_target_pairs={{0,4},{1,5},{2,6},{3,7},{4,0},{5,1},{6,2},{7,3},{8,12},{9,13},{10,... | collective-permute-start | bytes 3194888 | tf_op jit(solution)/shard_map/ppermute | solution.py:35
  41.2 27.4 %copy-start.7 = (bf16[1040,512]{1,0:T(8,128)(2,1)}, bf16[1040,512]{1,0:T(8,128)(2,1)S(1)}, u32[]{:S(2)}) copy-start(bf16[1040,512]{1,0:T(8,128)(2,1)S(1)} %collective-permute-done.5.refs_3_) | copy-start | bytes 3194884
  41.2 27.0 %collective-permute-start.6 = (bf16[1040,512]{1,0:T(8,128)(2,1)S(1)}, bf16[1040,512]{1,0:T(8,128)(2,1)S(1)}, u32[]{:S(2)}, u32[]{:S(2)}) collective-permute-start(bf16[1040,512]{1,0:T(8,128)(2,1)S(1)} %collective-permute-done.5.refs_3_), channel_id=1, source_target_pairs={{0,1},{1,2},{2,3},{3,0},{4,5},{5,6},{6,7},{7,4},{8,9},{9,10},{10,1... | collective-permute-start | bytes 3194888 | tf_op jit(solution)/shard_map/ppermute | solution.py:43
  42.5 5.2 %copy-start.8 = (bf16[1040,512]{1,0:T(8,128)(2,1)}, bf16[1040,512]{1,0:T(8,128)(2,1)S(1)}, u32[]{:S(2)}) copy-start(bf16[1040,512]{1,0:T(8,128)(2,1)S(1)} %collective-permute-done.10.refs_2_) | copy-start | bytes 3194884
  42.5 12.6 %collective-permute-start.11 = (bf16[512,384]{1,0:T(8,128)(2,1)S(1)}, bf16[512,384]{1,0:T(8,128)(2,1)S(1)}, u32[]{:S(2)}, u32[]{:S(2)}) collective-permute-start(bf16[512,384]{1,0:T(8,128)(2,1)S(1)} %collective-permute-done.8), channel_id=1, source_target_pairs={{0,224},{8,232},{16,240},{24,248},{32,0},{40,8},{48,16},{56,24},{6... | collective-permute-start | bytes 1179656 | tf_op jit(solution)/shard_map/ppermute | solution.py:47
  47.7 10.6 %collective-permute-start.12 = (bf16[512,384]{1,0:T(8,128)(2,1)S(1)}, bf16[512,384]{1,0:T(8,128)(2,1)S(1)}, u32[]{:S(2)}, u32[]{:S(2)}) collective-permute-start(bf16[512,384]{1,0:T(8,128)(2,1)S(1)} %collective-permute-done.9), channel_id=1, source_target_pairs={{0,32},{8,40},{16,48},{24,56},{32,64},{40,72},{48,80},{56,88},{64,... | collective-permute-start | bytes 1179656 | tf_op jit(solution)/shard_map/ppermute | solution.py:51
  58.3 8.4 %collective-permute-start.13 = (bf16[512,384]{1,0:T(8,128)(2,1)S(1)}, bf16[512,384]{1,0:T(8,128)(2,1)S(1)}, u32[]{:S(2)}, u32[]{:S(2)}) collective-permute-start(bf16[512,384]{1,0:T(8,128)(2,1)S(1)} %collective-permute-done.11), channel_id=1, source_target_pairs={{0,224},{8,232},{16,240},{24,248},{32,0},{40,8},{48,16},{56,24},{6... | collective-permute-start | bytes 1179656 | tf_op jit(solution)/shard_map/ppermute | solution.py:47
  58.6 9.7 %collective-permute-start.14 = (bf16[512,384]{1,0:T(8,128)(2,1)S(1)}, bf16[512,384]{1,0:T(8,128)(2,1)S(1)}, u32[]{:S(2)}, u32[]{:S(2)}) collective-permute-start(bf16[512,384]{1,0:T(8,128)(2,1)S(1)} %collective-permute-done.12), channel_id=1, source_target_pairs={{0,32},{8,40},{16,48},{24,56},{32,64},{40,72},{48,80},{56,88},{64,... | collective-permute-start | bytes 1179656 | tf_op jit(solution)/shard_map/ppermute | solution.py:51
  68.2 4.2 %copy-start.9 = (bf16[1040,512]{1,0:T(8,128)(2,1)}, bf16[1040,512]{1,0:T(8,128)(2,1)S(1)}, u32[]{:S(2)}) copy-start(bf16[1040,512]{1,0:T(8,128)(2,1)S(1)} %collective-permute-done.2.refs_6_) | copy-start | bytes 3194884
  69.3 20.7 %copy-start.1 = (bf16[7,512,384]{2,1,0:T(8,128)(2,1)}, bf16[7,512,384]{2,1,0:T(8,128)(2,1)S(1)}, u32[]{:S(2)}) copy-start(bf16[7,512,384]{2,1,0:T(8,128)(2,1)S(1)} %bitcast_dynamic-update-slice_fusion.refs_7_.own0.refs_9_) | copy-start | bytes 8257540
  69.3 20.7 %collective-permute-start.19 = (bf16[7,512,384]{2,1,0:T(8,128)(2,1)S(1)}, bf16[7,512,384]{2,1,0:T(8,128)(2,1)}, u32[]{:S(2)}, u32[]{:S(2)}) collective-permute-start(bf16[7,512,384]{2,1,0:T(8,128)(2,1)S(1)} %bitcast_dynamic-update-slice_fusion.refs_7_.own0.refs_9_), channel_id=1, source_target_pairs={{0,8},{8,0},{16,24},{24,16},{32,40},{40,32},{48,56},{56,48},{64,72... | collective-permute-start | bytes 8257544 | tf_op jit(solution)/shard_map/ppermute | solution.py:424
  72.4 6.4 %collective-permute-start.17 = (bf16[256,384]{1,0:T(8,128)(2,1)S(1)}, bf16[256,384]{1,0:T(8,128)(2,1)S(1)}, u32[]{:S(2)}, u32[]{:S(2)}) collective-permute-start(bf16[256,384]{1,0:T(8,128)(2,1)S(1)} %slice.45), channel_id=1, source_target_pairs={{0,224},{8,232},{16,240},{24,248},{32,0},{40,8},{48,16},{56,24},{6... | collective-permute-start | bytes 589832 | tf_op jit(solution)/shard_map/ppermute | solution.py:47
  74.3 7.5 %collective-permute-start.18 = (bf16[256,384]{1,0:T(8,128)(2,1)S(1)}, bf16[256,384]{1,0:T(8,128)(2,1)S(1)}, u32[]{:S(2)}, u32[]{:S(2)}) collective-permute-start(bf16[256,384]{1,0:T(8,128)(2,1)S(1)} %slice.46), channel_id=1, source_target_pairs={{0,32},{8,40},{16,48},{24,56},{32,64},{40,72},{48,80},{56,88},{64,... | collective-permute-start | bytes 589832 | tf_op jit(solution)/shard_map/ppermute | solution.py:51
  81.8 8.2 %copy-start.5 = (bf16[512,384]{1,0:T(8,128)(2,1)}, bf16[512,384]{1,0:T(8,128)(2,1)S(1)}, u32[]{:S(2)}) copy-start(bf16[512,384]{1,0:T(8,128)(2,1)S(1)} %constant_dynamic-update-slice_fusion.2.refs_8_.own1.refs_10_) | copy-start | bytes 1179652
  81.8 8.1 %collective-permute-start.20 = (bf16[512,384]{1,0:T(8,128)(2,1)S(1)}, bf16[512,384]{1,0:T(8,128)(2,1)S(1)}, u32[]{:S(2)}, u32[]{:S(2)}) collective-permute-start(bf16[512,384]{1,0:T(8,128)(2,1)S(1)} %constant_dynamic-update-slice_fusion.2.refs_8_.own1.refs_10_), channel_id=1, source_target_pairs={{0,8},{8,0},{16,24},{24,16},{32,40},{40,32},{48,56},{56,48},{64,72... | collective-permute-start | bytes 1179656 | tf_op jit(solution)/shard_map/ppermute | solution.py:424
  85.5 15.2 %collective-permute-start.16 = (bf16[528,512]{1,0:T(8,128)(2,1)S(1)}, bf16[528,512]{1,0:T(8,128)(2,1)S(1)}, u32[]{:S(2)}, u32[]{:S(2)}) collective-permute-start(bf16[528,512]{1,0:T(8,128)(2,1)S(1)} %slice.44), channel_id=1, source_target_pairs={{0,1},{1,2},{2,3},{3,0},{4,5},{5,6},{6,7},{7,4},{8,9},{9,10},{10,1... | collective-permute-start | bytes 1622024 | tf_op jit(solution)/shard_map/ppermute | solution.py:43
  86.9 13.5 %collective-permute-start.15 = (bf16[512,512]{1,0:T(8,128)(2,1)S(1)}, bf16[512,512]{1,0:T(8,128)(2,1)S(1)}, u32[]{:S(2)}, u32[]{:S(2)}) collective-permute-start(bf16[512,512]{1,0:T(8,128)(2,1)S(1)} %slice.43), channel_id=1, source_target_pairs={{0,3},{1,0},{2,1},{3,2},{4,7},{5,4},{6,5},{7,6},{8,11},{9,8},{10,9... | collective-permute-start | bytes 1572872 | tf_op jit(solution)/shard_map/ppermute | solution.py:39
  99.4 14.5 %copy-start.13 = (f32[8,32768]{1,0:T(8,128)S(1)}, f32[8,32768]{1,0:T(8,128)}, u32[]{:S(2)}) copy-start(f32[8,32768]{1,0:T(8,128)} %param.12) | copy-start | bytes 3145732
  107.0 8.2 %copy-start.15 = (f32[8]{0:T(128)S(1)}, f32[8]{0:T(128)}, u32[]{:S(2)}) copy-start(f32[8]{0:T(128)} %param.13) | copy-start | bytes 100
  107.0 23.9 %all-to-all-start = ((bf16[32,8,1024]{2,1,0:T(8,128)(2,1)}), bf16[32,8,1024]{2,1,0:T(8,128)(2,1)S(1)}, u32[]{:S(2)}, u32[]{:S(2)}) async-start(bf16[32,8,1024]{2,1,0:T(8,128)(2,1)} %shard_map.92), calls=%async_computation | async-start | bytes 1048576 | tf_op jit(solution)/shard_map/all_to_all | solution.py:431
  136.9 22.6 %all-to-all-start.1 = ((bf16[32,8,1024]{2,1,0:T(8,128)(2,1)}), bf16[32,8,1024]{2,1,0:T(8,128)(2,1)S(1)}, u32[]{:S(2)}, u32[]{:S(2)}) async-start(bf16[32,8,1024]{2,1,0:T(8,128)(2,1)} %shard_map.94), calls=%async_computation.1 | async-start | bytes 1048576 | tf_op jit(solution)/shard_map/all_to_all | solution.py:433
  (7 other events, 9.3 us)
